TPU v7x, 32 devices: a whole 2x2x4 slice. The times are simulated.
32 devices in a mesh: dp: 8 (over y, x, core), tensor: 4 (over z).
Axes of the slice: x: 2, y: 2, z: 4, core: 2. Of those that a mesh axis runs over, the one named last changes fastest.
Arguments:
- tokens: bfloat16 [8192, 2048], P(('dp', 'tensor')), may hold values from -6 to 6
- segments: int32 [8192], P('dp'), may hold values from 0 to 3, as said below
- gain_attn: float32 [2048], replicated, may hold values from 0.1 to 1.9
- w_query: bfloat16 [2048, 2048], P('dp', 'tensor'), may hold values from -0.125 to 0.125
- w_keyval: bfloat16 [2048, 512], P('dp'), may hold values from -0.125 to 0.125
- w_output: bfloat16 [2048, 2048], P('dp', 'tensor'), may hold values from -1 to 1
- gain_mlp: float32 [2048], replicated, may hold values from 0.1 to 1.9
- w_gate: bfloat16 [2048, 5632], P('dp', 'tensor'), may hold values from -0.125 to 0.125
- w_up: bfloat16 [2048, 5632], P('dp', 'tensor'), may hold values from -0.125 to 0.125
- w_down: bfloat16 [2048, 5632], P('dp', 'tensor'), may hold values from -0.078125 to 0.078125
- cotangent: bfloat16 [8192, 2048], P(('dp', 'tensor')), may hold values from -6 to 6
Outputs:
- layer_out: bfloat16 [8192, 2048], P(('dp', 'tensor'))
- grad_tokens: bfloat16 [8192, 2048], P(('dp', 'tensor'))
- grad_gain_attn: float32 [2048], P(('dp', 'tensor'))
- grad_query: float32 [2048, 2048], P('dp', 'tensor')
- grad_keyval: float32 [2048, 512], P(('dp', 'tensor'))
- grad_output: float32 [2048, 2048], P('dp', 'tensor')
- grad_gain_mlp: float32 [2048], P(('dp', 'tensor'))
- grad_gate: float32 [2048, 5632], P('dp', 'tensor')
- grad_up: float32 [2048, 5632], P('dp', 'tensor')
- grad_down: float32 [2048, 5632], P('dp', 'tensor')
Inputs may be any that keep to these rules, and one draw needn't show every extreme that they name: `segments`: each sequence holds exactly four documents numbered 0 to 3 in order; document 2 starts within the first 129 positions and ends within the last 128 positions of its sequence.
All inputs are finite; a program needn't handle non-finite values.
Results may differ from a plain program's by a relative error of at most 0.023.
Values may be sent and summed in bfloat16 or wider, within the bound.
A program may use at most 256 MiB of HBM per device.

v0:
```python
import jax
import jax.numpy as jnp
from jax import lax
from jax.sharding import PartitionSpec as P

KVH = 4
HD = 64


epsilon = 1e-05
rope_base = 10000.0


def doc_positions(seg_row):
    length = seg_row.shape[0]
    places = jnp.arange(length, dtype=jnp.int32)
    change = jnp.concatenate([jnp.ones((1,), jnp.bool_), seg_row[1:] != seg_row[:-1]])
    starts = lax.cummax(jnp.where(change, places, 0), axis=0)
    return places - starts


def rope_tables(places, width):
    half_width = width // 2
    frequency = rope_base ** (-(2.0 * jnp.arange(half_width).astype(jnp.float32)) / width)
    angles = places.astype(jnp.float32)[:, None] * frequency[None, :]
    return (jnp.cos(angles), jnp.sin(angles))


def rotate(values, cosine, sine_table):
    half_width = values.shape[-1] // 2
    front_half = values[..., :half_width]
    back_half = values[..., half_width:]
    cos_rows = cosine[:, None, :]
    sin_rows = sine_table[:, None, :]
    return jnp.concatenate(
        [
            front_half * cos_rows - back_half * sin_rows,
            back_half * cos_rows + front_half * sin_rows,
        ],
        axis=-1,
    )


def norm_forward(values, gain_vec):
    inverse = lax.rsqrt(jnp.mean(values * values, axis=-1, keepdims=True) + epsilon)
    unit_rows = values * inverse
    return (unit_rows * gain_vec, unit_rows, inverse)


def norm_backward(d_normed, unit_rows, inverse, gain_vec):
    gain_part = jnp.sum(d_normed * unit_rows, axis=0)
    d_unit = d_normed * gain_vec
    d_values = inverse * (d_unit - unit_rows * jnp.mean(d_unit * unit_rows, axis=-1, keepdims=True))
    return (d_values, gain_part)


def contract_rows(left, right):
    return lax.dot_general(
        left, right, (((0,), (0,)), ((), ())), preferred_element_type=jnp.float32
    )


def contract_cols(left, right):
    return lax.dot_general(
        left, right, (((1,), (1,)), ((), ())), preferred_element_type=jnp.float32
    )


def block_scores(query_block, key_part, segments, first_row, last_row, scale):
    scores = (
        jnp.einsum("qhd,kd->hqk", query_block, key_part, preferred_element_type=jnp.float32) * scale
    )
    rows_pos = jnp.arange(first_row, last_row)
    cols_pos = jnp.arange(last_row)
    allowed = (rows_pos[:, None] >= cols_pos[None, :]) & (
        segments[first_row:last_row, None] == segments[None, :last_row]
    )
    return jnp.where(allowed[None], scores, -1e30)


def attend_forward(query_low, key_low, value_low, segments, scale):
    length = query_low.shape[0]
    block_rows = min(512, length)
    outputs = []
    log_sums = []
    for index_block in range(length // block_rows):
        first_row = index_block * block_rows
        last_row = first_row + block_rows
        scores = block_scores(
            query_low[first_row:last_row], key_low[:last_row], segments, first_row, last_row, scale
        )
        top_score = jnp.max(scores, axis=-1, keepdims=True)
        expo = jnp.exp(scores - top_score)
        total = jnp.sum(expo, axis=-1, keepdims=True)
        soft_low = (expo / total).astype(jnp.bfloat16)
        outputs.append(
            jnp.einsum(
                "hqk,kd->qhd", soft_low, value_low[:last_row], preferred_element_type=jnp.float32
            )
        )
        log_sums.append(top_score + jnp.log(total))
    return (jnp.concatenate(outputs, axis=0), log_sums)


def attend_backward(query_low, key_low, value_low, d_out_low, segments, log_sums, scale):
    length = query_low.shape[0]
    block_rows = min(512, length)
    d_query_parts = []
    d_key = jnp.zeros(key_low.shape, jnp.float32)
    d_value = jnp.zeros(value_low.shape, jnp.float32)
    for index_block in range(length // block_rows):
        first_row = index_block * block_rows
        last_row = first_row + block_rows
        query_block = query_low[first_row:last_row]
        d_block = d_out_low[first_row:last_row]
        scores = block_scores(query_block, key_low[:last_row], segments, first_row, last_row, scale)
        soft_back = jnp.exp(scores - log_sums[index_block])
        d_probs = jnp.einsum(
            "qhd,kd->hqk", d_block, value_low[:last_row], preferred_element_type=jnp.float32
        )
        row_dot = jnp.sum(d_probs * soft_back, axis=-1, keepdims=True)
        d_scores = (soft_back * (d_probs - row_dot)).astype(jnp.bfloat16)
        d_query_parts.append(
            jnp.einsum(
                "hqk,kd->qhd", d_scores, key_low[:last_row], preferred_element_type=jnp.float32
            )
            * scale
        )
        d_key = d_key.at[:last_row].add(
            jnp.einsum("hqk,qhd->kd", d_scores, query_block, preferred_element_type=jnp.float32)
            * scale
        )
        d_value = d_value.at[:last_row].add(
            jnp.einsum(
                "hqk,qhd->kd",
                soft_back.astype(jnp.bfloat16),
                d_block,
                preferred_element_type=jnp.float32,
            )
        )
    return (jnp.concatenate(d_query_parts, axis=0), d_key, d_value)


def local(
    tokens,
    segments,
    gain_attn,
    w_query,
    w_keyval,
    w_output,
    gain_mlp,
    w_gate,
    w_up,
    w_down,
    cotangent,
):
    tensor_size = lax.axis_size("tensor")
    tensor_rank = lax.axis_index("tensor")
    length = segments.shape[0]
    local_heads = w_query.shape[1] // HD
    scale = HD ** (-0.5)
    full_query, full_keyval, full_output, full_gate, full_up, full_down = (
        lax.all_gather(w_query, "dp", axis=0, tiled=True),
        lax.all_gather(w_keyval, "dp", axis=0, tiled=True),
        lax.all_gather(w_output, "dp", axis=0, tiled=True),
        lax.all_gather(w_gate, "dp", axis=0, tiled=True),
        lax.all_gather(w_up, "dp", axis=0, tiled=True),
        lax.all_gather(w_down, "dp", axis=0, tiled=True),
    )
    kv_head = tensor_rank * KVH // tensor_size
    key_weight = lax.dynamic_slice_in_dim(full_keyval, kv_head * HD, HD, 1)
    value_weight = lax.dynamic_slice_in_dim(full_keyval, (KVH + kv_head) * HD, HD, 1)
    places = doc_positions(segments)
    cosine, sine_table = rope_tables(places, HD)
    token_rows = tokens.astype(jnp.float32)
    normed_attn, unit_attn, inverse_attn = norm_forward(token_rows, gain_attn)
    gathered_attn = lax.all_gather(normed_attn.astype(jnp.bfloat16), "tensor", axis=0, tiled=True)
    query_pre = jnp.dot(gathered_attn, full_query, preferred_element_type=jnp.float32)
    key_pre = jnp.dot(gathered_attn, key_weight, preferred_element_type=jnp.float32)
    value_low = jnp.dot(gathered_attn, value_weight, preferred_element_type=jnp.float32).astype(
        jnp.bfloat16
    )
    query_low = rotate(query_pre.reshape(length, local_heads, HD), cosine, sine_table).astype(
        jnp.bfloat16
    )
    key_low = (
        rotate(key_pre.reshape(length, 1, HD), cosine, sine_table)
        .reshape(length, HD)
        .astype(jnp.bfloat16)
    )
    head_out, log_sums = attend_forward(query_low, key_low, value_low, segments, scale)
    heads_low = head_out.reshape(length, local_heads * HD).astype(jnp.bfloat16)
    residual = token_rows + lax.psum_scatter(
        contract_cols(heads_low, full_output).astype(jnp.bfloat16),
        "tensor",
        scatter_dimension=0,
        tiled=True,
    ).astype(jnp.float32)
    normed_mlp, unit_mlp, inverse_mlp = norm_forward(residual, gain_mlp)
    gathered_mlp = lax.all_gather(normed_mlp.astype(jnp.bfloat16), "tensor", axis=0, tiled=True)
    gate_act = jnp.dot(gathered_mlp, full_gate, preferred_element_type=jnp.float32)
    up_act = jnp.dot(gathered_mlp, full_up, preferred_element_type=jnp.float32)
    sigmoid_gate = jax.nn.sigmoid(gate_act)
    silu_gate = gate_act * sigmoid_gate
    hidden_low = (silu_gate * up_act).astype(jnp.bfloat16)
    layer_rows = residual + lax.psum_scatter(
        contract_cols(hidden_low, full_down).astype(jnp.bfloat16),
        "tensor",
        scatter_dimension=0,
        tiled=True,
    ).astype(jnp.float32)
    piece = lax.all_gather(cotangent, "tensor", axis=0, tiled=True)
    grad_acc = contract_rows(piece, hidden_low)
    d_rows = jnp.dot(piece, full_down, preferred_element_type=jnp.float32)
    grad_down = grad_acc
    d_hidden = d_rows
    d_gate = (d_hidden * up_act * sigmoid_gate * (1.0 + gate_act * (1.0 - sigmoid_gate))).astype(
        jnp.bfloat16
    )
    d_up = (d_hidden * silu_gate).astype(jnp.bfloat16)
    grad_gate = contract_rows(gathered_mlp, d_gate)
    grad_up = contract_rows(gathered_mlp, d_up)
    d_normed_mlp = lax.psum_scatter(
        (contract_cols(d_gate, full_gate) + contract_cols(d_up, full_up)).astype(jnp.bfloat16),
        "tensor",
        scatter_dimension=0,
        tiled=True,
    ).astype(jnp.float32)
    d_norm_mlp, gain_mlp_part = norm_backward(d_normed_mlp, unit_mlp, inverse_mlp, gain_mlp)
    d_residual = cotangent.astype(jnp.float32) + d_norm_mlp
    piece = lax.all_gather(d_residual.astype(jnp.bfloat16), "tensor", axis=0, tiled=True)
    grad_acc = contract_rows(piece, heads_low)
    d_rows = jnp.dot(piece, full_output, preferred_element_type=jnp.float32)
    d_heads_low = d_rows.reshape(length, local_heads, HD).astype(jnp.bfloat16)
    d_queries, d_keys, d_values = attend_backward(
        query_low, key_low, value_low, d_heads_low, segments, log_sums, scale
    )
    dq_low = (
        rotate(d_queries, cosine, -sine_table)
        .reshape(length, local_heads * HD)
        .astype(jnp.bfloat16)
    )
    dk_low = (
        rotate(d_keys.reshape(length, 1, HD), cosine, -sine_table)
        .reshape(length, HD)
        .astype(jnp.bfloat16)
    )
    dv_low = d_values.astype(jnp.bfloat16)
    grad_query = contract_rows(gathered_attn, dq_low)
    grad_key = contract_rows(gathered_attn, dk_low)
    grad_value = contract_rows(gathered_attn, dv_low)
    zero_keyval = jnp.zeros((full_keyval.shape[0], 2 * KVH * HD), jnp.float32)
    grad_keyval = lax.dynamic_update_slice_in_dim(zero_keyval, grad_key, kv_head * HD, 1)
    grad_keyval = lax.dynamic_update_slice_in_dim(grad_keyval, grad_value, (KVH + kv_head) * HD, 1)
    d_normed_attn = lax.psum_scatter(
        (
            contract_cols(dq_low, full_query)
            + contract_cols(dk_low, key_weight)
            + contract_cols(dv_low, value_weight)
        ).astype(jnp.bfloat16),
        "tensor",
        scatter_dimension=0,
        tiled=True,
    ).astype(jnp.float32)
    d_norm_attn, gain_attn_part = norm_backward(d_normed_attn, unit_attn, inverse_attn, gain_attn)
    grad_tokens = (d_residual + d_norm_attn).astype(jnp.bfloat16)
    all_shares = (
        lax.psum_scatter(
            grad_query.astype(jnp.bfloat16), "dp", scatter_dimension=0, tiled=True
        ).astype(jnp.float32),
        lax.psum_scatter(
            grad_acc.astype(jnp.bfloat16), "dp", scatter_dimension=0, tiled=True
        ).astype(jnp.float32),
        lax.psum_scatter(
            grad_gate.astype(jnp.bfloat16), "dp", scatter_dimension=0, tiled=True
        ).astype(jnp.float32),
        lax.psum_scatter(
            grad_up.astype(jnp.bfloat16), "dp", scatter_dimension=0, tiled=True
        ).astype(jnp.float32),
        lax.psum_scatter(
            grad_down.astype(jnp.bfloat16), "dp", scatter_dimension=0, tiled=True
        ).astype(jnp.float32),
    )
    attn_shares = (all_shares[0], all_shares[1])
    mlp_shares = (all_shares[2], all_shares[3], all_shares[4])
    shared = (
        lax.psum_scatter(grad_keyval, ("dp", "tensor"), scatter_dimension=0, tiled=True),
        lax.psum_scatter(gain_attn_part, ("dp", "tensor"), scatter_dimension=0, tiled=True),
        lax.psum_scatter(gain_mlp_part, ("dp", "tensor"), scatter_dimension=0, tiled=True),
    )
    return (
        layer_rows.astype(jnp.bfloat16),
        grad_tokens,
        shared[1],
        attn_shares[0],
        shared[0],
        attn_shares[1],
        shared[2],
        mlp_shares[0],
        mlp_shares[1],
        mlp_shares[2],
    )


def solution(mesh):
    return jax.shard_map(
        local,
        mesh=mesh,
        in_specs=(
            P(("dp", "tensor"), None),
            P("dp"),
            P(),
            P("dp", "tensor"),
            P("dp", None),
            P("dp", "tensor"),
            P(),
            P("dp", "tensor"),
            P("dp", "tensor"),
            P("dp", "tensor"),
            P(("dp", "tensor"), None),
        ),
        out_specs=(
            P(("dp", "tensor"), None),
            P(("dp", "tensor"), None),
            P(("dp", "tensor")),
            P("dp", "tensor"),
            P(("dp", "tensor"), None),
            P("dp", "tensor"),
            P(("dp", "tensor")),
            P("dp", "tensor"),
            P("dp", "tensor"),
            P("dp", "tensor"),
        ),
        check_vma=False,
    )
```

profile of v0, /device:TPU:0, one launch (start us, length us, event | category | flops | bytes accessed | tf_op | source)
XLA Modules:
  0.0 1364.9 jit_solution(8800088234364576717)
XLA Ops:
  10.1 2.5 fusion.34
  16.7 23.8 %all-gather.13.cloned.1.call-done = bf16[2048,512]{1,0:T(8,128)(2,1)} async-done(((bf16[256,512]{1,0:T(8,128)(2,1)}), bf16[2048,512]{1,0:T(8,128)(2,1)}) %all-gather.13.cloned.1.call-update) | async-done | bytes 2097168 | tf_op jit(solution)/shard_map/all_gather | solution.py:164
  40.5 82.9 %all-gather.11.cloned.1.call-done = bf16[1024,2048]{1,0:T(8,128)(2,1)} async-done(((bf16[256,2048]{1,0:T(8,128)(2,1)}), bf16[1024,2048]{1,0:T(8,128)(2,1)}) %all-gather.11.cloned.1.call-update) | async-done | bytes 4194320 | tf_op jit(solution)/shard_map/all_gather | solution.py:177
  123.5 3.8 convolution_bitcast_fusion.1
  127.8 24.0 %all-gather.15.cloned.1.call-done = bf16[2048,512]{1,0:T(8,128)(2,1)} async-done(((bf16[256,512]{1,0:T(8,128)(2,1)}), bf16[2048,512]{1,0:T(8,128)(2,1)}) %all-gather.15.cloned.1.call-update) | async-done | bytes 2097168 | tf_op jit(solution)/shard_map/all_gather | solution.py:163
  151.8 5.2 fusion.117
  158.9 8.3 fusion.115
  168.6 8.6 fusion.3
  177.1 2.7 convolution_convert_fusion.8
  179.8 5.1 fusion.45
  186.9 3.1 fusion.44
  191.1 6.0 convolution_convert_fusion.4
  197.8 76.3 %reduce-scatter.11.cloned.1.call-done = bf16[256,2048]{1,0:T(8,128)(2,1)} async-done(((bf16[1024,2048]{1,0:T(8,128)(2,1)}), bf16[256,2048]{1,0:T(8,128)(2,1)}) %reduce-scatter.11.cloned.1.call-update) | async-done | bytes 1048592 | tf_op jit(solution)/shard_map/reduce_scatter | solution.py:193
  275.8 2.6 multiply_convert_fusion.3
  280.7 39.2 %all-gather.23.cloned.1.call-done = bf16[2048,1408]{1,0:T(8,128)(2,1)} async-done(((bf16[256,1408]{1,0:T(8,128)(2,1)}), bf16[2048,1408]{1,0:T(8,128)(2,1)}) %all-gather.23.cloned.1.call-update) | async-done | bytes 5767184 | tf_op jit(solution)/shard_map/all_gather | solution.py:167
  319.9 83.0 %all-gather.19.cloned.1.call-done = bf16[1024,2048]{1,0:T(8,128)(2,1)} async-done(((bf16[256,2048]{1,0:T(8,128)(2,1)}), bf16[1024,2048]{1,0:T(8,128)(2,1)}) %all-gather.19.cloned.1.call-update) | async-done | bytes 4194320 | tf_op jit(solution)/shard_map/all_gather | solution.py:200
  402.9 11.7 fusion.119
  414.7 32.2 %all-gather.21.cloned.1.call-done = bf16[2048,1408]{1,0:T(8,128)(2,1)} async-done(((bf16[256,1408]{1,0:T(8,128)(2,1)}), bf16[2048,1408]{1,0:T(8,128)(2,1)}) %all-gather.21.cloned.1.call-update) | async-done | bytes 5767184 | tf_op jit(solution)/shard_map/all_gather | solution.py:166
  446.9 11.7 fusion.118
  458.5 70.8 %all-gather.27.cloned.1.call-done = bf16[1024,2048]{1,0:T(8,128)(2,1)} async-done(((bf16[256,2048]{1,0:T(8,128)(2,1)}), bf16[1024,2048]{1,0:T(8,128)(2,1)}) %all-gather.27.cloned.1.call-update) | async-done | bytes 4194320 | tf_op jit(solution)/shard_map/all_gather | solution.py:212
  529.3 43.8 %all-gather.25.cloned.1.call-done = bf16[2048,1408]{1,0:T(8,128)(2,1)} async-done(((bf16[256,1408]{1,0:T(8,128)(2,1)}), bf16[2048,1408]{1,0:T(8,128)(2,1)}) %all-gather.25.cloned.1.call-update) | async-done | bytes 5767184 | tf_op jit(solution)/shard_map/all_gather | solution.py:168
  573.1 16.1 %multiply_convert_fusion = (bf16[1024,1408]{1,0:T(8,128)(2,1)}, bf16[1024,1408]{1,0:T(8,128)(2,1)S(1)}, bf16[1024,1408]{1,0:T(8,128)(2,1)}) fusion(f32[1024,1408]{1,0:T(8,128)} %fusion.118, f32[1024,1408]{1,0:T(8,128)} %fusion.119, bf16[1024,2048]{1,0:T(8,128)(2,1)} %all-gather.27.cloned.1.call-done, bf16[2048,1408]{1,0:T(8,128)(2,1)} %all-gather.25.cloned.1.call-done), kind=kOutput, calls=%fused_computation.31 | convolution fusion | flops 5927206912 | bytes 30146560 | tf_op jit(solution)/shard_map/dot_general | solution.py:214
  589.2 6.7 fusion.120
  595.9 11.3 add_convert_fusion.1
  607.2 76.9 %reduce-scatter.15.cloned.1.call-done = bf16[256,2048]{1,0:T(8,128)(2,1)} async-done(((bf16[1024,2048]{1,0:T(8,128)(2,1)}), bf16[256,2048]{1,0:T(8,128)(2,1)}) %reduce-scatter.15.cloned.1.call-update) | async-done | bytes 1048592 | tf_op jit(solution)/shard_map/reduce_scatter | solution.py:223
  684.1 2.7 fusion.33
  686.8 3.2 fusion.112
  690.1 10.5 fusion.13
  700.7 11.1 convolution_convert_fusion.1
  711.9 11.5 convolution_convert_fusion.2
  723.5 48.0 %all-gather.29.cloned.1.call-done = bf16[1024,2048]{1,0:T(8,128)(2,1)} async-done(((bf16[256,2048]{1,0:T(8,128)(2,1)}), bf16[1024,2048]{1,0:T(8,128)(2,1)}) %all-gather.29.cloned.1.call-update) | async-done | bytes 4194320 | tf_op jit(solution)/shard_map/all_gather | solution.py:231
  771.5 5.4 convolution_convert_fusion.7
  778.0 3.8 convolution_convert_fusion.5
  781.8 9.6 fusion.7
  791.4 15.5 %fusion = (f32[8,512]{1,0:T(8,128)S(1)}, f32[1024,512,8]{1,0,2:T(8,128)}) fusion(f32[8,512,1024]{1,2,0:T(8,128)} %get-tuple-element.131, f32[8,512]{1,0:T(8,128)S(1)} %log_add_fusion, bf16[512,8,64]{0,2,1:T(8,128)(2,1)S(1)} %bitcast.150, bf16[1024,64]{0,1:T(8,128)(2,1)S(1)} %convolution_convert_fusion.8), kind=kOutput, calls=%fused_computation.2 | convolution fusion | flops 549449728 | bytes 34242560 | tf_op jit(solution)/shard_map/qhd,kd->hqk/dot_general | solution.py:118
  807.0 1.9 slice-done.7
  808.9 10.6 fusion.2
  819.5 7.3 fusion.9
  832.5 2.6 fusion.48
  835.2 3.8 convolution_convert_fusion.6
  840.6 2.7 fusion.65
  843.3 7.9 fusion.58
  851.3 5.7 fusion.121
  857.0 2.9 fusion.55
  859.9 7.3 add_convert_fusion
  867.3 11.0 convolution_convert_fusion.3
  878.6 4.5 fusion.91
  883.1 2.6 broadcast_in_dim.43
  885.7 6.3 dynamic_update_slice.6
  892.0 4.5 fusion.122
  896.5 6.3 dynamic_update_slice.7
  902.8 2.5 copy.53
  905.3 2.5 convert_element_type.188
  907.8 49.9 %reduce-scatter.25.cloned.1.call-done = bf16[256,1408]{1,0:T(8,128)(2,1)} async-done(((bf16[2048,1408]{1,0:T(8,128)(2,1)}), bf16[256,1408]{1,0:T(8,128)(2,1)}) %reduce-scatter.25.cloned.1.call-update) | async-done | bytes 720912 | tf_op jit(solution)/shard_map/reduce_scatter | solution.py:274
  957.7 2.3 convert_element_type.186
  960.0 42.4 %reduce-scatter.23.cloned.1.call-done = bf16[256,512]{1,0:T(8,128)(2,1)} async-done(((bf16[2048,512]{1,0:T(8,128)(2,1)}), bf16[256,512]{1,0:T(8,128)(2,1)}) %reduce-scatter.23.cloned.1.call-update) | async-done | bytes 262160 | tf_op jit(solution)/shard_map/reduce_scatter | solution.py:271
  1002.4 1.8 convert_element_type.184
  1004.2 42.6 %reduce-scatter.19.cloned.1.call-done = bf16[256,512]{1,0:T(8,128)(2,1)} async-done(((bf16[2048,512]{1,0:T(8,128)(2,1)}), bf16[256,512]{1,0:T(8,128)(2,1)}) %reduce-scatter.19.cloned.1.call-update) | async-done | bytes 262160 | tf_op jit(solution)/shard_map/reduce_scatter | solution.py:268
  1048.6 77.2 %reduce-scatter.17.cloned.1.call-done = bf16[256,2048]{1,0:T(8,128)(2,1)} async-done(((bf16[1024,2048]{1,0:T(8,128)(2,1)}), bf16[256,2048]{1,0:T(8,128)(2,1)}) %reduce-scatter.17.cloned.1.call-update) | async-done | bytes 1048592 | tf_op jit(solution)/shard_map/reduce_scatter | solution.py:255
  1125.8 2.1 fusion.36
  1127.9 43.0 %all-reduce.4 = (f32[2048]{0:T(1024)S(1)}, f32[2048]{0:T(1024)S(1)}) all-reduce(f32[2048]{0:T(1024)S(1)} %get-tuple-element.106, f32[2048]{0:T(1024)S(1)} %copy-done.32), channel_id=6, replica_groups=mesh['dp'=8,'tensor'=4] {'dp','tensor'}, use_global_device_ids=true, to_apply=%region_17.18.clone | all-reduce | flops 4096 | bytes 32768
  1172.1 34.4 %reduce-scatter.13.cloned.1.call-done = bf16[256,2048]{1,0:T(8,128)(2,1)} async-done(((bf16[1024,2048]{1,0:T(8,128)(2,1)}), bf16[256,2048]{1,0:T(8,128)(2,1)}) %reduce-scatter.13.cloned.1.call-update) | async-done | bytes 1048592 | tf_op jit(solution)/shard_map/reduce_scatter | solution.py:206
  1206.5 4.9 fusion.29
  1211.4 146.4 %reduce-scatter.21.cloned.1.call-done = f32[64,512]{1,0:T(8,128)} async-done(((f32[2048,512]{1,0:T(8,128)}), f32[64,512]{1,0:T(8,128)}) %reduce-scatter.21.cloned.1.call-update) | async-done | bytes 131088 | tf_op jit(solution)/shard_map/reduce_scatter | solution.py:287
  (195 shorter events, 30.2 us)
Async XLA Ops:
  7.2 6.8 copy-start.31
  7.2 33.4 %all-gather.13.cloned.1.call-start = ((), (), s32[]{:S(2)}) async-start(), calls=%async_computation.11 | async-start | bytes 2359296 | tf_op jit(solution)/shard_map/all_gather | solution.py:164
  7.9 115.6 %all-gather.11.cloned.1.call-start = ((), (), s32[]{:S(2)}) async-start(), calls=%async_computation.10 | async-start | bytes 5242880 | tf_op jit(solution)/shard_map/all_gather | solution.py:177
  12.6 139.2 %all-gather.15.cloned.1.call-start = ((), (), s32[]{:S(2)}) async-start(), calls=%async_computation.12 | async-start | bytes 2359296 | tf_op jit(solution)/shard_map/all_gather | solution.py:163
  13.3 176.9 %all-gather.17.cloned.1.call-start = ((), (), s32[]{:S(2)}) async-start(), calls=%async_computation.13 | async-start | bytes 2359296 | tf_op jit(solution)/shard_map/all_gather | solution.py:165
  13.9 260.2 %reduce-scatter.11.cloned.1.call-start = ((), (), s32[]{:S(2)}) async-start(), calls=%async_computation.14 | async-start | bytes 5242880 | tf_op jit(solution)/shard_map/reduce_scatter | solution.py:193
  14.0 113.2 %copy-start.39 = (f32[32]{0:T(128)}, f32[32]{0:T(128)S(1)}, u32[]{:S(2)}) copy-start(f32[32]{0:T(128)S(1)} %multiply_power_fusion) | copy-start | bytes 388
  14.8 112.5 %copy-start.30 = (f32[1024]{0:T(1024)}, f32[1024]{0:T(1024)S(1)}, u32[]{:S(2)}) copy-start(f32[1024]{0:T(1024)S(1)} %fusion.98) | copy-start | bytes 12292
  16.2 140.9 %copy-start.14 = (f32[1024,32]{0,1:T(8,128)}, f32[1024,32]{0,1:T(8,128)S(1)}, u32[]{:S(2)}) copy-start(f32[1024,32]{0,1:T(8,128)S(1)} %get-tuple-element.127) | copy-start | bytes 393220
  127.8 31.1 %copy-start.16 = (bf16[1024,1,32]{0,2,1:T(8,128)(2,1)}, bf16[1024,1,32]{0,2,1:T(8,128)(2,1)S(1)}, u32[]{:S(2)}) copy-start(bf16[1024,1,32]{0,2,1:T(8,128)(2,1)S(1)} %get-tuple-element.123) | copy-start | bytes 196612
  127.8 31.1 %copy-start.18 = (bf16[1024,1,32]{0,2,1:T(8,128)(2,1)}, bf16[1024,1,32]{0,2,1:T(8,128)(2,1)S(1)}, u32[]{:S(2)}) copy-start(bf16[1024,1,32]{0,2,1:T(8,128)(2,1)S(1)} %get-tuple-element.124) | copy-start | bytes 196612
  158.9 8.4 copy-start
  168.5 8.6 copy-start.1
  177.1 7.8 slice-start
  179.8 5.9 slice-start.2
  179.8 7.1 slice-start.3
  197.2 77.0 %copy-start.4 = (bf16[256,2048]{1,0:T(8,128)(2,1)S(1)}, bf16[256,2048]{1,0:T(8,128)(2,1)}, u32[]{:S(2)}) copy-start(bf16[256,2048]{1,0:T(8,128)(2,1)} %param.23) | copy-start | bytes 3145732
  197.2 78.6 %copy-start.27 = (f32[2048]{0:T(1024)S(1)}, f32[2048]{0:T(1024)}, u32[]{:S(2)}) copy-start(f32[2048]{0:T(1024)} %param.29) | copy-start | bytes 24580
  197.2 122.7 %all-gather.23.cloned.1.call-start = ((), (), s32[]{:S(2)}) async-start(), calls=%async_computation.17 | async-start | bytes 6488064 | tf_op jit(solution)/shard_map/all_gather | solution.py:167
  197.8 205.1 %all-gather.19.cloned.1.call-start = ((), (), s32[]{:S(2)}) async-start(), calls=%async_computation.15 | async-start | bytes 5242880 | tf_op jit(solution)/shard_map/all_gather | solution.py:200
  275.8 411.0 %copy-start.33 = (f32[256]{0:T(256)}, f32[256]{0:T(256)S(1)}, u32[]{:S(2)}) copy-start(f32[256]{0:T(256)S(1)} %add_rsqrt_fusion) | copy-start | bytes 3076
  278.4 168.4 %all-gather.21.cloned.1.call-start = ((), (), s32[]{:S(2)}) async-start(), calls=%async_computation.16 | async-start | bytes 6488064 | tf_op jit(solution)/shard_map/all_gather | solution.py:166
  279.2 250.1 %all-gather.27.cloned.1.call-start = ((), (), s32[]{:S(2)}) async-start(), calls=%async_computation.20 | async-start | bytes 5242880 | tf_op jit(solution)/shard_map/all_gather | solution.py:212
  279.9 293.2 %all-gather.25.cloned.1.call-start = ((), (), s32[]{:S(2)}) async-start(), calls=%async_computation.18 | async-start | bytes 6488064 | tf_op jit(solution)/shard_map/all_gather | solution.py:168
  280.5 403.6 %reduce-scatter.15.cloned.1.call-start = ((), (), s32[]{:S(2)}) async-start(), calls=%async_computation.21 | async-start | bytes 5242880 | tf_op jit(solution)/shard_map/reduce_scatter | solution.py:223
  573.1 16.1 %copy-start.40 = (bf16[2048,1408]{1,0:T(8,128)(2,1)S(1)}, bf16[2048,1408]{1,0:T(8,128)(2,1)}, u32[]{:S(2)}) copy-start(bf16[2048,1408]{1,0:T(8,128)(2,1)} %all-gather.21.cloned.1.call-done) | copy-start | bytes 17301508
  589.1 6.7 copy-start.43
  589.2 6.7 copy-start.44
  607.1 76.9 %copy-start.5 = (bf16[256,2048]{1,0:T(8,128)(2,1)S(1)}, bf16[256,2048]{1,0:T(8,128)(2,1)}, u32[]{:S(2)}) copy-start(bf16[256,2048]{1,0:T(8,128)(2,1)} %reduce-scatter.11.cloned.1.call-done) | copy-start | bytes 3145732
  607.1 79.7 %copy-start.6 = (bf16[256,2048]{1,0:T(8,128)(2,1)S(1)}, bf16[256,2048]{1,0:T(8,128)(2,1)}, u32[]{:S(2)}) copy-start(bf16[256,2048]{1,0:T(8,128)(2,1)} %param.33) | copy-start | bytes 3145732
  607.2 164.4 %all-gather.29.cloned.1.call-start = ((), (), s32[]{:S(2)}) async-start(), calls=%async_computation.22 | async-start | bytes 5242880 | tf_op jit(solution)/shard_map/all_gather | solution.py:231
  686.8 13.8 %copy-start.37 = (f32[256]{0:T(256)}, f32[256]{0:T(256)S(1)}, u32[]{:S(2)}) copy-start(f32[256]{0:T(256)S(1)} %broadcast_multiply_fusion.1) | copy-start | bytes 3076
  690.1 212.7 %reduce-scatter.29.cloned.1.call-start = ((), (), s32[]{:S(2)}) async-start(), calls=%async_computation.29 | async-start | bytes 6488064 | tf_op jit(solution)/shard_map/reduce_scatter | solution.py:280
  700.7 204.7 %reduce-scatter.27.cloned.1.call-start = ((), (), s32[]{:S(2)}) async-start(), calls=%async_computation.28 | async-start | bytes 6488064 | tf_op jit(solution)/shard_map/reduce_scatter | solution.py:277
  711.8 245.9 %reduce-scatter.25.cloned.1.call-start = ((), (), s32[]{:S(2)}) async-start(), calls=%async_computation.27 | async-start | bytes 6488064 | tf_op jit(solution)/shard_map/reduce_scatter | solution.py:274
  723.4 279.0 %reduce-scatter.23.cloned.1.call-start = ((), (), s32[]{:S(2)}) async-start(), calls=%async_computation.26 | async-start | bytes 2359296 | tf_op jit(solution)/shard_map/reduce_scatter | solution.py:271
  723.4 96.0 %copy-start.25 = (f32[8,512]{1,0:T(8,128)}, f32[8,512]{1,0:T(8,128)S(1)}, u32[]{:S(2)}) copy-start(f32[8,512]{1,0:T(8,128)S(1)} %log_add_fusion.1) | copy-start | bytes 49156
  771.5 6.4 copy-start.21
  771.5 6.4 copy-start.41
  781.8 265.0 %reduce-scatter.19.cloned.1.call-start = ((), (), s32[]{:S(2)}) async-start(), calls=%async_computation.24 | async-start | bytes 2359296 | tf_op jit(solution)/shard_map/reduce_scatter | solution.py:268
  781.8 9.6 copy-start.11
  791.4 15.6 %slice-start.4 = ((s8[16777216]{0:T(1024)(128)(4,1)}), s8[4194304]{0:T(1024)(128)(4,1)S(1)}, s32[]{:S(2)}) async-start(s8[16777216]{0:T(1024)(128)(4,1)} %bitcast.146), calls=%async_computation.34 | async-start | bytes 8388608
  791.4 15.6 %slice-start.5 = ((s8[16777216]{0:T(1024)(128)(4,1)}), s8[4194304]{0:T(1024)(128)(4,1)S(1)}, s32[]{:S(2)}) async-start(s8[16777216]{0:T(1024)(128)(4,1)} %bitcast.146), calls=%async_computation.35 | async-start | bytes 8388608
  791.4 15.6 %slice-start.6 = ((s8[16777216]{0:T(1024)(128)(4,1)}), s8[4194304]{0:T(1024)(128)(4,1)S(1)}, s32[]{:S(2)}) async-start(s8[16777216]{0:T(1024)(128)(4,1)} %bitcast.146), calls=%async_computation.36 | async-start | bytes 8388608
  791.4 17.4 %slice-start.7 = ((s8[16777216]{0:T(1024)(128)(4,1)}), s8[4194304]{0:T(1024)(128)(4,1)S(1)}, s32[]{:S(2)}) async-start(s8[16777216]{0:T(1024)(128)(4,1)} %bitcast.146), calls=%async_computation.37 | async-start | bytes 8388608
  819.5 7.3 copy-start.17
  819.5 7.3 copy-start.19
  819.5 8.8 copy-start.3
  839.0 286.8 %reduce-scatter.17.cloned.1.call-start = ((), (), s32[]{:S(2)}) async-start(), calls=%async_computation.23 | async-start | bytes 5242880 | tf_op jit(solution)/shard_map/reduce_scatter | solution.py:255
  840.6 16.4 %slice-start.8 = ((s8[16777216]{0:T(1024)(128)(4,1)}), s8[4194304]{0:T(1024)(128)(4,1)S(1)}, s32[]{:S(2)}) async-start(s8[16777216]{0:T(1024)(128)(4,1)} %bitcast.148), calls=%async_computation.38 | async-start | bytes 8388608
  840.6 16.4 %slice-start.9 = ((s8[16777216]{0:T(1024)(128)(4,1)}), s8[4194304]{0:T(1024)(128)(4,1)S(1)}, s32[]{:S(2)}) async-start(s8[16777216]{0:T(1024)(128)(4,1)} %bitcast.148), calls=%async_computation.39 | async-start | bytes 8388608
  843.3 7.9 copy-start.23
  843.3 7.9 copy-start.42
  843.3 13.7 %slice-start.10 = ((s8[16777216]{0:T(1024)(128)(4,1)}), s8[4194304]{0:T(1024)(128)(4,1)S(1)}, s32[]{:S(2)}) async-start(s8[16777216]{0:T(1024)(128)(4,1)} %bitcast.148), calls=%async_computation.40 | async-start | bytes 8388608
  851.3 5.7 slice-start.11
  851.3 5.7 copy-start.12
  867.2 339.2 %reduce-scatter.13.cloned.1.call-start = ((), (), s32[]{:S(2)}) async-start(), calls=%async_computation.19 | async-start | bytes 5242880 | tf_op jit(solution)/shard_map/reduce_scatter | solution.py:206
  878.3 479.5 %reduce-scatter.21.cloned.1.call-start = ((), (), s32[]{:S(2)}) async-start(), calls=%async_computation.25 | async-start | bytes 4325376 | tf_op jit(solution)/shard_map/reduce_scatter | solution.py:287
  902.7 223.1 %copy-start.29 = (f32[2048]{0:T(1024)S(1)}, f32[2048]{0:T(1024)}, u32[]{:S(2)}) copy-start(f32[2048]{0:T(1024)} %param.25) | copy-start | bytes 24580
  902.7 223.1 %copy-start.36 = (f32[256]{0:T(256)S(1)}, f32[256]{0:T(256)}, u32[]{:S(2)}) copy-start(f32[256]{0:T(256)} %copy-done.35) | copy-start | bytes 3076
  905.3 222.6 %copy-start.32 = (f32[2048]{0:T(1024)S(1)}, f32[2048]{0:T(1024)}, u32[]{:S(2)}) copy-start(f32[2048]{0:T(1024)} %get-tuple-element.104) | copy-start | bytes 24580
  905.3 301.2 %copy-start.28 = (f32[2048]{0:T(1024)S(1)}, f32[2048]{0:T(1024)}, u32[]{:S(2)}) copy-start(f32[2048]{0:T(1024)} %param.29) | copy-start | bytes 24580
  905.3 301.2 %copy-start.34 = (f32[256]{0:T(256)S(1)}, f32[256]{0:T(256)}, u32[]{:S(2)}) copy-start(f32[256]{0:T(256)} %copy-done.33) | copy-start | bytes 3076
  905.3 301.2 %copy-start.38 = (f32[256]{0:T(256)S(1)}, f32[256]{0:T(256)}, u32[]{:S(2)}) copy-start(f32[256]{0:T(256)} %copy-done.37) | copy-start | bytes 3076
  (13 other events, 27.3 us)
Sparse Core Ops, SparseCore 0:
  9.9 30.5 all-gather.12
  42.7 80.7 all-gather.10
  125.4 26.4 all-gather.14
  153.6 27.8 all-gather.16
  197.3 76.7 reduce-scatter.10
  276.0 43.8 all-gather.22
  322.1 80.7 all-gather.18
  405.0 41.8 all-gather.20
  448.5 80.7 all-gather.26
  531.2 41.8 all-gather.24
  607.3 76.7 reduce-scatter.14
  690.2 81.2 all-gather.28
  775.0 57.5 reduce-scatter.28
  836.3 59.0 reduce-scatter.26
  898.6 59.0 reduce-scatter.24
  961.2 41.1 reduce-scatter.22
  1005.5 41.1 reduce-scatter.18
  1049.0 76.7 reduce-scatter.16
  1128.1 78.3 reduce-scatter.12
  1209.3 148.4 reduce-scatter.20
where the time goes:
time: 1370 us; the launch traced here: 1360 us
  waiting for transfers between devices  998 us (73%)
  matrix products  217 us (16%)
  other arithmetic  62.3 us (5%)
  blocking collectives  43 us (3%)
  local copies, waits for them, and re-layouts  27.2 us (2%)
  between operations  15.4 us (1%)
    reduce_scatter x1, waiting for transfers between devices, local(): lax.psum_scatter(grad_keyval, ('dp', 'tensor'), scatter_dimension=0, tile...  146 us
    all_gather x1, waiting for transfers between devices, local(): lax.all_gather(normed_mlp.astype(jnp.bfloat16), 'tensor', axis=0, tiled=T...  83 us
    all_gather x1, waiting for transfers between devices, local(): lax.all_gather(normed_attn.astype(jnp.bfloat16), 'tensor', axis=0, tiled=...  82.9 us
    reduce_scatter x1, waiting for transfers between devices, local(): lax.psum_scatter((contract_cols(dq_low, full_query) + contract_cols(dk_lo...  77.2 us
    reduce_scatter x1, waiting for transfers between devices, local(): lax.psum_scatter((contract_cols(d_gate, full_gate) + contract_cols(d_up,...  76.9 us
    reduce_scatter x1, waiting for transfers between devices, local(): lax.psum_scatter(contract_cols(heads_low, full_output).astype(jnp.bfloat1...  76.3 us
    all_gather x1, waiting for transfers between devices, local(): piece = lax.all_gather(cotangent, 'tensor', axis=0, tiled=True)  70.8 us
    dot_general x7, matrix products, contract_cols(): lax.dot_general(left, right, (((1,), (1,)), ((), ())), preferred_element_...  50.7 us
  transfers between devices with their start and end apart: 20, of which 17 were waited for; matrix products, arithmetic and copies ran while one was open for 19% of the time, Pallas kernels for 0%

commit v1 on v0

v1 whole, which is shorter than its diff:
```python
import functools

import jax
import jax.numpy as jnp
from jax import lax
from jax.experimental import pallas as pl
from jax.experimental.pallas import tpu as pltpu
from jax.sharding import PartitionSpec as P

KVH = 4
HD = 64
PAIR = 2 * HD

epsilon = 1e-05
rope_base = 10000.0
masked = -1e30


def doc_positions(seg_row):
    length = seg_row.shape[0]
    places = jnp.arange(length, dtype=jnp.int32)
    change = jnp.concatenate([jnp.ones((1,), jnp.bool_), seg_row[1:] != seg_row[:-1]])
    starts = lax.cummax(jnp.where(change, places, 0), axis=0)
    return places - starts


def rope_tables(places, width):
    half_width = width // 2
    frequency = rope_base ** (-(2.0 * jnp.arange(half_width).astype(jnp.float32)) / width)
    angles = places.astype(jnp.float32)[:, None] * frequency[None, :]
    return (jnp.cos(angles), jnp.sin(angles))


def rotate(values, cosine, sine_table):
    rows, width = values.shape
    heads = values.reshape(rows, width // HD, HD)
    half_width = HD // 2
    front_half = heads[..., :half_width]
    back_half = heads[..., half_width:]
    cos_rows = cosine[:, None, :]
    sin_rows = sine_table[:, None, :]
    turned = jnp.concatenate(
        [
            front_half * cos_rows - back_half * sin_rows,
            back_half * cos_rows + front_half * sin_rows,
        ],
        axis=-1,
    )
    return turned.reshape(rows, width)


def norm_forward(values, gain_vec):
    inverse = lax.rsqrt(jnp.mean(values * values, axis=-1, keepdims=True) + epsilon)
    unit_rows = values * inverse
    return (unit_rows * gain_vec, unit_rows, inverse)


def norm_backward(d_normed, unit_rows, inverse, gain_vec):
    gain_part = jnp.sum(d_normed * unit_rows, axis=0)
    d_unit = d_normed * gain_vec
    d_values = inverse * (d_unit - unit_rows * jnp.mean(d_unit * unit_rows, axis=-1, keepdims=True))
    return (d_values, gain_part)


def dot_nn(left, right):
    return jnp.dot(left, right, preferred_element_type=jnp.float32)


def dot_nt(left, right):
    return lax.dot_general(
        left, right, (((1,), (1,)), ((), ())), preferred_element_type=jnp.float32
    )


def dot_tn(left, right):
    return lax.dot_general(
        left, right, (((0,), (0,)), ((), ())), preferred_element_type=jnp.float32
    )


def front_lanes(tile):
    lane = lax.broadcasted_iota(jnp.int32, tile.shape, 1)
    return jnp.where(lane < HD, tile, jnp.zeros_like(tile))


def back_lanes(tile):
    lane = lax.broadcasted_iota(jnp.int32, tile.shape, 1)
    return jnp.where(lane < HD, jnp.zeros_like(tile), tile)


def attend_forward_kernel(query_ref, front_ref, back_ref, value_t_ref, bias_ref, out_ref, log_ref):
    pairs = query_ref.shape[1] // PAIR
    value_t = value_t_ref[0]
    for pair in range(pairs):
        query = query_ref[:, pair * PAIR : (pair + 1) * PAIR]
        outs = []
        for side, key_ref in enumerate((front_ref, back_ref)):
            scores = dot_nt(key_ref[0], query) + bias_ref[...]
            top = jnp.max(scores, axis=0, keepdims=True)
            expo = jnp.exp(scores - top)
            total = jnp.sum(expo, axis=0, keepdims=True)
            outs.append(dot_nn(value_t, expo.astype(jnp.bfloat16)) / total)
            log_ref[0, pl.ds(pair * 2 + side, 1), :] = top + jnp.log(total)
        out = jnp.concatenate(outs, axis=0).T
        out_ref[:, pair * PAIR : (pair + 1) * PAIR] = out.astype(jnp.bfloat16)


def attend_backward_kernel(
    query_ref,
    grad_ref,
    kf_ref,
    kb_ref,
    kt_ref,
    vf_ref,
    vb_ref,
    bias_ref,
    log_ref,
    dq_ref,
    dk_ref,
    dv_ref,
):
    pairs = query_ref.shape[1] // PAIR
    key_t = kt_ref[0]
    dk_ref[0] = jnp.zeros(dk_ref.shape[1:], jnp.float32)
    dv_ref[0] = jnp.zeros(dv_ref.shape[1:], jnp.float32)
    for pair in range(pairs):
        columns = slice(pair * PAIR, (pair + 1) * PAIR)
        query = query_ref[:, columns]
        grad = grad_ref[:, columns]
        outs = []
        for side, (key_ref, value_ref, keep) in enumerate(
            ((kf_ref, vf_ref, front_lanes), (kb_ref, vb_ref, back_lanes))
        ):
            log_sum = log_ref[0, pl.ds(pair * 2 + side, 1), :]
            probs = jnp.exp(dot_nt(key_ref[0], query) + bias_ref[...] - log_sum)
            d_probs = dot_nt(value_ref[0], grad)
            row_dot = jnp.sum(probs * d_probs, axis=0, keepdims=True)
            d_scores = (probs * (d_probs - row_dot)).astype(jnp.bfloat16)
            dk_ref[0] += dot_nn(d_scores, keep(query))
            dv_ref[0] += dot_nn(probs.astype(jnp.bfloat16), keep(grad))
            outs.append(dot_nn(key_t, d_scores))
        dq_ref[:, columns] = jnp.concatenate(outs, axis=0).T * (HD**-0.5)


def whole_group(rows, width):
    return pl.BlockSpec((1, rows, width), lambda g: (g, 0, 0))


def columns_of(rows, width):
    return pl.BlockSpec((rows, width), lambda g: (0, g))


def attend_forward(query, key_f, key_b, value_t, bias):
    rows, width = query.shape
    length = bias.shape[0]
    group = width // KVH
    return pl.pallas_call(
        attend_forward_kernel,
        grid=(KVH,),
        in_specs=[
            columns_of(rows, group),
            whole_group(length, PAIR),
            whole_group(length, PAIR),
            whole_group(HD, length),
            pl.BlockSpec((length, rows), lambda g: (0, 0)),
        ],
        out_specs=[columns_of(rows, group), whole_group(group // HD, rows)],
        out_shape=[
            jax.ShapeDtypeStruct((rows, width), jnp.bfloat16),
            jax.ShapeDtypeStruct((KVH, group // HD, rows), jnp.float32),
        ],
        compiler_params=pltpu.CompilerParams(vmem_limit_bytes=48 * 1024 * 1024),
        name="attend_forward",
    )(query, key_f, key_b, value_t, bias)


def attend_backward(query, grad, key_f, key_b, key_t, value_f, value_b, bias, log_sum):
    rows, width = query.shape
    length = bias.shape[0]
    group = width // KVH
    tall = whole_group(length, PAIR)
    return pl.pallas_call(
        attend_backward_kernel,
        grid=(KVH,),
        in_specs=[
            columns_of(rows, group),
            columns_of(rows, group),
            tall,
            tall,
            whole_group(HD, length),
            tall,
            tall,
            pl.BlockSpec((length, rows), lambda g: (0, 0)),
            whole_group(group // HD, rows),
        ],
        out_specs=[columns_of(rows, group), tall, tall],
        out_shape=[
            jax.ShapeDtypeStruct((rows, width), jnp.float32),
            jax.ShapeDtypeStruct((KVH, length, PAIR), jnp.float32),
            jax.ShapeDtypeStruct((KVH, length, PAIR), jnp.float32),
        ],
        compiler_params=pltpu.CompilerParams(vmem_limit_bytes=48 * 1024 * 1024),
        name="attend_backward",
    )(query, grad, key_f, key_b, key_t, value_f, value_b, bias, log_sum)


def by_head(matrix):
    rows = matrix.shape[0]
    return matrix.reshape(rows, KVH, HD).transpose(1, 0, 2)


MESH = pl.DeviceIdType.MESH


def flip(index, bit):
    return index + bit - 2 * bit * ((index // bit) % 2)


def line_order(place):
    nearest = place - 1 + 2 * (1 - (place + 3) // 4)
    farthest = 3 - 3 * (place // 2)
    return (nearest, 6 - place - nearest - farthest, farthest)


def enter(dp, place):
    barrier = pltpu.get_barrier_semaphore()
    for bit in (1, 2, 4):
        pl.semaphore_signal(barrier, inc=1, device_id=(flip(dp, bit), place), device_id_type=MESH)
    for step in (-1, 1):
        there = (place + step >= 0) & (place + step < 4)

        @pl.when(there)
        def _():
            pl.semaphore_signal(
                barrier, inc=1, device_id=(dp, place + step), device_id_type=MESH
            )

    ends = 1 - ((place + 3) // 4) + place // 3
    pl.semaphore_wait(barrier, 5 - ends)


def gather_kernel(
    kv_ref, q_ref, o_ref, d_ref, g_ref, u_ref, c_ref,
    fkv, fq, fo, fd, fg, fu, fc,
    own_sem, z_send, z_recv, p_send, p_recv,
):
    dp, place = lax.axis_index("dp"), lax.axis_index("tensor")
    rows = kv_ref.shape[0]
    half = rows // 2
    width = q_ref.shape[1]
    order = line_order(place)
    enter(dp, place)

    def rows_of(owner):
        return pl.ds(pl.multiple_of(owner * rows, rows), rows)

    def columns_of_rank(rank):
        return pl.ds(pl.multiple_of(rank * width, width), width)

    def remote(src, dst, send, recv, device):
        return pltpu.make_async_remote_copy(
            src_ref=src, dst_ref=dst, send_sem=send, recv_sem=recv,
            device_id=device, device_id_type=MESH,
        )

    own = [
        (kv_ref, fkv.at[rows_of(dp), :]),
        (q_ref, fq.at[rows_of(dp), columns_of_rank(place)]),
        (o_ref, fo.at[rows_of(dp), columns_of_rank(place)]),
        (d_ref, fd.at[rows_of(dp), :]),
        (g_ref, fg.at[rows_of(dp), :]),
        (u_ref, fu.at[rows_of(dp), :]),
        (c_ref, fc.at[rows_of(place), :]),
    ]
    own_copies = [
        pltpu.make_async_copy(src, dst, own_sem.at[i]) for i, (src, dst) in enumerate(own)
    ]
    for copy in own_copies:
        copy.start()

    def line_block(which, rank):
        if which == 2:
            return fc.at[rows_of(rank), :]
        return (fq, fo)[which].at[rows_of(dp), columns_of_rank(rank)]

    def line_copy(which, rank, step):
        src = (q_ref, o_ref, c_ref)[which] if rank is place else line_block(which, rank)
        side = 0 if step < 0 else 1
        return remote(
            src, line_block(which, rank), z_send.at[which, side, rank], z_recv.at[which, rank],
            (dp, place + step),
        )

    def line_send(which, rank, act):
        @pl.when((rank <= place) & (place < 3))
        def _():
            act(line_copy(which, rank, 1))

        @pl.when((rank >= place) & (place > 0))
        def _():
            act(line_copy(which, rank, -1))

    def start(copy):
        copy.start()

    def wait_send(copy):
        copy.wait_send()

    x, y, core = flip(dp, 2), flip(dp, 4), flip(dp, 1)
    far = flip(x, 4)

    blocks = [("kv", None), ("q", place), ("q", order[0]), ("q", order[1]), ("q", order[2])]
    blocks += [("o", place), ("o", order[0]), ("o", order[1]), ("o", order[2])]
    blocks += [("d", None), ("g", None), ("u", None)]

    def block(index, owner, part=None):
        name, rank = blocks[index]
        ref = {"kv": fkv, "q": fq, "o": fo, "d": fd, "g": fg, "u": fu}[name]
        first = owner * rows if part is None else owner * rows + part * half
        size = rows if part is None else half
        window = pl.ds(pl.multiple_of(first, half), size)
        if rank is None:
            return ref.at[window, :]
        return ref.at[window, columns_of_rank(rank)]

    def own_block(index):
        name, rank = blocks[index]
        if rank is None or rank is place:
            return {"kv": kv_ref, "q": q_ref, "o": o_ref, "d": d_ref, "g": g_ref, "u": u_ref}[name]
        return block(index, dp)

    def plane_copy(index, lane):
        send, recv = p_send.at[index, lane], p_recv.at[index, lane]
        if lane == 0:
            return remote(own_block(index), block(index, dp), send, recv, (x, place))
        if lane == 1:
            return remote(own_block(index), block(index, dp), send, recv, (y, place))
        if lane == 2:
            return remote(block(index, x, 0), block(index, x, 0), send, recv, (y, place))
        if lane == 3:
            return remote(block(index, y, 1), block(index, y, 1), send, recv, (x, place))
        owner = (dp, x, y, far)[lane - 4]
        src = own_block(index) if lane == 4 else block(index, owner)
        return remote(src, block(index, owner), send, recv, (core, place))

    def plane_first(index):
        plane_copy(index, 0).start()
        plane_copy(index, 1).start()
        plane_copy(index, 4).start()

    def plane_second(index):
        plane_copy(index, 0).wait_recv()
        plane_copy(index, 2).start()
        plane_copy(index, 5).start()
        plane_copy(index, 1).wait_recv()
        plane_copy(index, 3).start()
        plane_copy(index, 6).start()

    def plane_third(index):
        plane_copy(index, 2).wait_recv()
        plane_copy(index, 3).wait_recv()
        plane_copy(index, 7).start()

    def plane_last(index):
        for lane in range(4, 8):
            plane_copy(index, lane).wait_recv()
        for lane in range(8):
            plane_copy(index, lane).wait_send()

    line_send(0, place, start)
    plane_first(0)
    plane_first(1)
    line_send(1, place, start)
    line_send(2, place, start)
    count = len(blocks)
    line_of = {2: (0, 0), 3: (0, 1), 4: (0, 2), 6: (1, 0), 7: (1, 1), 8: (1, 2)}
    for index in range(count):
        ahead = index + 2
        if ahead < count:
            if ahead in line_of:
                which, step = line_of[ahead]
                line_copy(which, order[step], 1).wait_recv()
                line_send(which, order[step], start)
            plane_first(ahead)
        if ahead in (7, 9, 10):
            step = (7, 9, 10).index(ahead)
            line_copy(2, order[step], 1).wait_recv()
            line_send(2, order[step], start)
        plane_second(index)
        if index >= 1:
            plane_third(index - 1)
    plane_third(count - 1)
    for index in range(count):
        plane_last(index)
    for which in range(3):
        line_send(which, place, wait_send)
        for step in range(3):
            line_send(which, order[step], wait_send)
    for copy in own_copies:
        copy.wait()


def gather_all(w_keyval, w_query, w_output, w_down, w_gate, w_up, cotangent):
    n_dp, n_line = lax.axis_size("dp"), lax.axis_size("tensor")

    def over(array, rows, columns):
        shape = (array.shape[0] * rows, array.shape[1] * columns)
        return jax.ShapeDtypeStruct(shape, array.dtype)

    anywhere = pl.BlockSpec(memory_space=pl.ANY)
    shapes = [
        over(w_keyval, n_dp, 1),
        over(w_query, n_dp, n_line),
        over(w_output, n_dp, n_line),
        over(w_down, n_dp, 1),
        over(w_gate, n_dp, 1),
        over(w_up, n_dp, 1),
        over(cotangent, n_line, 1),
    ]
    return pl.pallas_call(
        gather_kernel,
        out_shape=shapes,
        in_specs=[anywhere] * 7,
        out_specs=[anywhere] * 7,
        scratch_shapes=[
            pltpu.SemaphoreType.DMA((7,)),
            pltpu.SemaphoreType.DMA((3, 2, 4)),
            pltpu.SemaphoreType.DMA((3, 4)),
            pltpu.SemaphoreType.DMA((12, 8)),
            pltpu.SemaphoreType.DMA((12, 8)),
        ],
        compiler_params=pltpu.CompilerParams(collective_id=0, has_side_effects=True),
        name="gather_all",
    )(w_keyval, w_query, w_output, w_down, w_gate, w_up, cotangent)


def local(
    tokens,
    segments,
    gain_attn,
    w_query,
    w_keyval,
    w_output,
    gain_mlp,
    w_gate,
    w_up,
    w_down,
    cotangent,
):
    tensor_rank = lax.axis_index("tensor")
    length = segments.shape[0]
    rows = tokens.shape[0]
    both = ("dp", "tensor")
    low = jnp.bfloat16

    def gather(array, axes, axis=0):
        return lax.all_gather(array, axes, axis=axis, tiled=True)

    def scatter(array, axes, axis=0):
        return lax.psum_scatter(array, axes, scatter_dimension=axis, tiled=True)

    if (lax.axis_size("dp"), lax.axis_size("tensor")) == (8, 4):
        full_keyval, full_query, full_output, full_down, full_gate, full_up, piece = gather_all(
            w_keyval, w_query, w_output, w_down, w_gate, w_up, cotangent
        )
    else:
        full_keyval = gather(w_keyval, "dp")
        full_query = gather(gather(w_query, "tensor", 1), "dp")
        full_output = gather(gather(w_output, "tensor", 1), "dp")
        full_gate, full_up = gather(w_gate, "dp"), gather(w_up, "dp")
        full_down = gather(w_down, "dp")
        piece = gather(cotangent, "tensor")
    places = doc_positions(segments)
    my_places = lax.dynamic_slice_in_dim(places, tensor_rank * rows, rows, 0)
    my_segments = lax.dynamic_slice_in_dim(segments, tensor_rank * rows, rows, 0)
    cosine, sine_table = rope_tables(my_places, HD)
    order = jnp.arange(length, dtype=jnp.int32)
    allowed = (order[:, None] <= tensor_rank * rows + order[None, :rows]) & (
        segments[:, None] == my_segments[None, :]
    )
    bias = jnp.where(allowed, 0.0, masked).astype(jnp.float32)

    token_rows = tokens.astype(jnp.float32)
    normed_attn, unit_attn, inverse_attn = norm_forward(token_rows, gain_attn)
    normed_attn = normed_attn.astype(low)
    keyval_pre = dot_nn(normed_attn, full_keyval)
    wide = KVH * HD
    key_low = rotate(keyval_pre[:, :wide], cosine, sine_table).astype(low)
    keyval = gather(jnp.concatenate([key_low, keyval_pre[:, wide:].astype(low)], axis=1), "tensor")
    key_heads, value_heads = by_head(keyval[:, :wide]), by_head(keyval[:, wide:])
    blank = jnp.zeros_like(key_heads)
    key_f = jnp.concatenate([key_heads, blank], axis=2)
    key_b = jnp.concatenate([blank, key_heads], axis=2)
    value_f = jnp.concatenate([value_heads, blank], axis=2)
    value_b = jnp.concatenate([blank, value_heads], axis=2)
    key_t = key_heads.transpose(0, 2, 1)
    value_t = value_heads.transpose(0, 2, 1)

    query = (rotate(dot_nn(normed_attn, full_query), cosine, sine_table) * (HD**-0.5)).astype(low)
    heads_low, log_sum = attend_forward(query, key_f, key_b, value_t, bias)
    residual = token_rows + dot_nt(heads_low, full_output)

    normed_mlp, unit_mlp, inverse_mlp = norm_forward(residual, gain_mlp)
    gathered_mlp = gather(normed_mlp.astype(low), "tensor")
    gate_act = dot_nn(gathered_mlp, full_gate)
    up_act = dot_nn(gathered_mlp, full_up)
    sigmoid_gate = jax.nn.sigmoid(gate_act)
    silu_gate = gate_act * sigmoid_gate
    hidden_low = (silu_gate * up_act).astype(low)
    d_hidden = dot_nn(piece, full_down)
    d_gate = (d_hidden * up_act * sigmoid_gate * (1.0 + gate_act * (1.0 - sigmoid_gate))).astype(low)
    d_up = (d_hidden * silu_gate).astype(low)
    d_normed_mlp = scatter(
        (dot_nt(d_gate, full_gate) + dot_nt(d_up, full_up)).astype(low), "tensor"
    ).astype(jnp.float32)
    layer_rows = residual + scatter(dot_nt(hidden_low, full_down).astype(low), "tensor").astype(
        jnp.float32
    )
    grad_down = dot_tn(piece, hidden_low)
    grad_gate = dot_tn(gathered_mlp, d_gate)
    grad_up = dot_tn(gathered_mlp, d_up)
    d_norm_mlp, gain_mlp_part = norm_backward(d_normed_mlp, unit_mlp, inverse_mlp, gain_mlp)
    d_residual = cotangent.astype(jnp.float32) + d_norm_mlp

    d_branch = d_residual.astype(low)
    grad_output = dot_tn(d_branch, heads_low)
    d_heads = dot_nn(d_branch, full_output).astype(low)
    d_queries, d_keys, d_values = attend_backward(
        query, d_heads, key_f, key_b, key_t, value_f, value_b, bias, log_sum
    )

    def flat(parts):
        joined = parts[:, :, :HD] + parts[:, :, HD:]
        return joined.transpose(1, 0, 2).reshape(length, wide)

    d_keyval = scatter(
        jnp.concatenate([flat(d_keys), flat(d_values)], axis=1).astype(low), "tensor"
    ).astype(jnp.float32)
    dq_low = rotate(d_queries, cosine, -sine_table).astype(low)
    dkv_low = jnp.concatenate(
        [rotate(d_keyval[:, :wide], cosine, -sine_table), d_keyval[:, wide:]], axis=1
    ).astype(low)
    grad_query = dot_tn(normed_attn, dq_low)
    grad_keyval = dot_tn(normed_attn, dkv_low)
    d_normed_attn = dot_nt(dq_low, full_query) + dot_nt(dkv_low, full_keyval)
    d_norm_attn, gain_attn_part = norm_backward(d_normed_attn, unit_attn, inverse_attn, gain_attn)
    grad_tokens = (d_residual + d_norm_attn).astype(low)

    def shares(grad):
        return scatter(grad.astype(low), "dp").astype(jnp.float32)

    def square_shares(grad):
        return scatter(scatter(grad.astype(low), "dp"), "tensor", 1).astype(jnp.float32)

    gains = scatter(
        jnp.stack([gain_attn_part, gain_mlp_part]).reshape(2, -1, rows_of_gain(gain_attn)), both, 1
    )
    return (
        layer_rows.astype(low),
        grad_tokens,
        gains[0, 0],
        square_shares(grad_query),
        scatter(grad_keyval.astype(low), both).astype(jnp.float32),
        square_shares(grad_output),
        gains[1, 0],
        shares(grad_gate),
        shares(grad_up),
        shares(grad_down),
    )


def rows_of_gain(gain):
    return gain.shape[0] // (lax.axis_size("dp") * lax.axis_size("tensor"))


def solution(mesh):
    return jax.shard_map(
        local,
        mesh=mesh,
        in_specs=(
            P(("dp", "tensor"), None),
            P("dp"),
            P(),
            P("dp", "tensor"),
            P("dp", None),
            P("dp", "tensor"),
            P(),
            P("dp", "tensor"),
            P("dp", "tensor"),
            P("dp", "tensor"),
            P(("dp", "tensor"), None),
        ),
        out_specs=(
            P(("dp", "tensor"), None),
            P(("dp", "tensor"), None),
            P(("dp", "tensor")),
            P("dp", "tensor"),
            P(("dp", "tensor"), None),
            P("dp", "tensor"),
            P(("dp", "tensor")),
            P("dp", "tensor"),
            P("dp", "tensor"),
            P("dp", "tensor"),
        ),
        check_vma=False,
    )
```

time: 1370 us -> 1180 us (0.86)
  waiting for transfers between devices: 998 us -> 673 us
  Pallas kernels: 0 us -> 230 us
  matrix products: 217 us -> 150 us
  other arithmetic: 62.3 us -> 38.8 us
    all_gather x10 -> x2, waiting for transfers between devices: 448 us -> 99.3 us  [gather(): return lax.all_gather(array, axes, axis=axis, tiled=True)]
    pallas_call x0 -> x3, Pallas kernels: none -> 230 us  [the longest x1 176 us: gather_all(): pl.pallas_call(gather_kernel, out_shape=shapes, in_specs=[anywhere] * 7,...]
    dot_general x33 -> x18, matrix products: 217 us -> 150 us  [the longest x6 53.7 us: dot_nn(): return jnp.dot(left, right, preferred_element_type=jnp.float32)]
    reduce_scatter x10 -> x11, waiting for transfers between devices: 546 us -> 574 us  [scatter(): return lax.psum_scatter(array, axes, scatter_dimension=axis, tiled=True)]
    convert_element_type x10 -> x9, other arithmetic: 39.5 us -> 16.6 us  [the longest x3 6.91 us: shares(): return scatter(grad.astype(low), 'dp').astype(jnp.float32)]
  transfers between devices with their start and end apart: 20 -> 13, of which waited for: 17 -> 12; matrix products, arithmetic and copies ran while one was open for 19% -> 9% of each run, Pallas kernels for 0% -> 0%
where the time goes in v1:
time: 1180 us
  waiting for transfers between devices  673 us (57%)
  Pallas kernels  230 us (19%)
  matrix products  150 us (13%)
  blocking collectives  39.8 us (3%)
  other arithmetic  38.8 us (3%)
  local copies, waits for them, and re-layouts  30.3 us (3%)
  between operations  14.6 us (1%)
    reduce_scatter x11, waiting for transfers between devices, scatter(): return lax.psum_scatter(array, axes, scatter_dimension=axis, tiled=True)  574 us
    pallas_call x1, Pallas kernels, gather_all(): pl.pallas_call(gather_kernel, out_shape=shapes, in_specs=[anywhere] * 7,...  176 us
    all_gather x2, waiting for transfers between devices, gather(): return lax.all_gather(array, axes, axis=axis, tiled=True)  99.3 us
    dot_general x6, matrix products, dot_nn(): return jnp.dot(left, right, preferred_element_type=jnp.float32)  53.7 us
    dot_general x6, matrix products, dot_nt(): lax.dot_general(left, right, (((1,), (1,)), ((), ())), preferred_element_...  48.2 us
    dot_general x6, matrix products, dot_tn(): lax.dot_general(left, right, (((0,), (0,)), ((), ())), preferred_element_...  47.9 us
    unnamed x1, blocking collectives  39.8 us
    pallas_call x1, Pallas kernels, attend_backward(): pl.pallas_call(attend_backward_kernel, grid=(KVH,), in_specs=[columns_of(...  30.9 us
  transfers between devices with their start and end apart: 13, of which 12 were waited for; matrix products, arithmetic and copies ran while one was open for 9% of the time, Pallas kernels for 0%

profile of v1, /device:TPU:0, one launch (start us, length us, event | category | flops | bytes accessed | tf_op | source)
XLA Modules:
  0.0 1177.1 jit_solution(2050022255482243026)
XLA Ops:
  7.3 1.6 fusion.18
  8.9 176.4 %gather_all.1 = (bf16[2048,512]{1,0:T(8,128)(2,1)}, bf16[2048,2048]{1,0:T(8,128)(2,1)}, bf16[2048,2048]{1,0:T(8,128)(2,1)}, bf16[2048,1408]{1,0:T(8,128)(2,1)}, ...) custom-call(bf16[256,512]{1,0:T(8,128)(2,1)} %kv_ref.1, ...), custom_call_target="tpu_custom_call" | custom-call | tf_op jit(solution)/shard_map/gather_all/pallas_call | solution.py:420
  185.3 2.3 fusion.31
  189.9 6.8 fusion.33
  197.3 0.9 copy.47.query_ref
  198.3 1.2 fusion.23.bias_ref
  199.5 18.9 %all-gather.3.cloned.1.call-done = bf16[1024,512]{1,0:T(8,128)(2,1)} async-done(((bf16[256,512]{1,0:T(8,128)(2,1)}), bf16[1024,512]{1,0:T(8,128)(2,1)}) %all-gather.3.cloned.1.call-update) | async-done | bytes 1048592 | tf_op jit(solution)/shard_map/all_gather | solution.py:457
  218.4 2.1 fusion.36
  220.7 1.3 copy.58
  222.8 2.2 fusion.37
  225.0 2.0 copy.46
  227.1 1.2 copy-done
  228.3 1.0 copy-done.1
  229.4 22.8 %attend_forward.1 = (bf16[256,2048]{1,0:T(8,128)(2,1)S(1)}, f32[4,8,256]{2,1,0:T(8,128)S(1)}) custom-call(bf16[256,2048]{1,0:T(8,128)(2,1)S(1)} %copy.47.query_ref, bf16[4,1024,128]{2,1,0:T(8,128)(2,1)S(1)} %get-tuple-element.52.front_ref.kf_ref, bf16[4,1024,128]{2,1,0:T(8,128)(2,1)S(1)} %get-tuple-element.51.back_ref.kb_ref, ...), custom_call_target="tpu_custom_call" | custom-call | tf_op jit(solution)/shard_map/attend_forward/pallas_call | solution.py:157
  252.2 6.3 multiply_reduce_fusion
  258.5 1.3 copy-done.12
  259.8 1.2 multiply_convert_fusion.3
  261.1 80.4 %all-gather.5.cloned.1.call-done = bf16[1024,2048]{1,0:T(8,128)(2,1)} async-done(((bf16[256,2048]{1,0:T(8,128)(2,1)}), bf16[1024,2048]{1,0:T(8,128)(2,1)}) %all-gather.5.cloned.1.call-update) | async-done | bytes 4194320 | tf_op jit(solution)/shard_map/all_gather | solution.py:457
  341.4 12.4 %fusion.40 = f32[1024,1408]{1,0:T(8,128)} fusion(bf16[1024,2048]{1,0:T(8,128)(2,1)} %all-gather.5.cloned.1.call-done, bf16[2048,1408]{1,0:T(8,128)(2,1)} %get-tuple-element.27), kind=kOutput, calls=%fused_computation.95 | convolution fusion | flops 5905580032 | bytes 15728640 | tf_op jit(solution)/shard_map/dot_general | solution.py:66
  353.8 10.5 fusion.39
  364.3 15.2 %multiply_convert_fusion = (bf16[1024,1408]{1,0:T(8,128)(2,1)}, bf16[1024,1408]{1,0:T(8,128)(2,1)}, bf16[1024,1408]{1,0:T(8,128)(2,1)}) fusion(f32[1024,1408]{1,0:T(8,128)} %fusion.39, f32[1024,1408]{1,0:T(8,128)} %fusion.40, bf16[1024,2048]{1,0:T(8,128)(2,1)} %get-tuple-element.29, bf16[2048,1408]{1,0:T(8,128)(2,1)S(1)} %bitcast.80), kind=kOutput, calls=%fused_computation.6 | convolution fusion | flops 5927206912 | bytes 30146560 | tf_op jit(solution)/shard_map/dot_general | solution.py:66
  379.6 8.5 fusion.41
  388.1 10.2 add_convert_fusion
  398.4 11.0 convolution_convert_fusion.5
  409.4 2.4 copy.50
  411.8 3.4 fusion.35
  415.2 58.6 %reduce-scatter.14.cloned.1.call-done = bf16[256,2048]{1,0:T(8,128)(2,1)} async-done(((bf16[1024,2048]{1,0:T(8,128)(2,1)}), bf16[256,2048]{1,0:T(8,128)(2,1)}) %reduce-scatter.14.cloned.1.call-update) | async-done | bytes 1048592 | tf_op jit(solution)/shard_map/reduce_scatter | solution.py:460
  473.8 2.7 fusion.10
  476.5 76.9 %reduce-scatter.12.cloned.1.call-done = bf16[256,2048]{1,0:T(8,128)(2,1)} async-done(((bf16[1024,2048]{1,0:T(8,128)(2,1)}), bf16[256,2048]{1,0:T(8,128)(2,1)}) %reduce-scatter.12.cloned.1.call-update) | async-done | bytes 1048592 | tf_op jit(solution)/shard_map/reduce_scatter | solution.py:460
  553.3 4.4 fusion.9
  557.7 6.5 convolution_convert_fusion.7.grad_ref
  564.3 30.9 %attend_backward.1 = (f32[256,2048]{1,0:T(8,128)}, f32[4,1024,128]{2,1,0:T(8,128)}, f32[4,1024,128]{2,1,0:T(8,128)}) custom-call(bf16[256,2048]{1,0:T(8,128)(2,1)S(1)} %copy.47.query_ref, bf16[256,2048]{1,0:T(8,128)(2,1)S(1)} %convolution_convert_fusion.7.grad_ref, bf16[4,1024,128]{2,1,0:T(8,128)(2,1)S(1)} %get-tuple-element.52.front_ref.kf_ref, ...), custom_call_target="tpu_custom_call" | custom-call | tf_op jit(solution)/shard_map/attend_backward/pallas_call | solution.py:182
  595.2 6.0 fusion.20
  601.2 2.5 copy.55
  603.7 2.3 copy.56
  606.0 2.2 pad_maximum_fusion.1
  608.3 5.6 convolution_convert_fusion.3
  614.0 3.3 copy.54
  617.4 2.0 subtract_convert_fusion
  619.4 1.0 copy-done.13
  620.4 5.8 convolution_convert_fusion.4
  626.2 11.1 convolution_convert_fusion.2
  637.4 11.1 convolution_convert_fusion.1
  648.5 12.2 %convolution_convert_fusion = bf16[2048,1408]{1,0:T(8,128)(2,1)} fusion(bf16[1024,2048]{1,0:T(8,128)(2,1)} %get-tuple-element.29, bf16[1024,1408]{1,0:T(8,128)(2,1)} %get-tuple-element.40), kind=kOutput, calls=%fused_computation.1 | convolution fusion | flops 5908463616 | bytes 12845056 | tf_op jit(solution)/shard_map/dot_general | solution.py:76
  660.8 1.0 fusion.38
  661.9 2.2 convolution_convert_fusion.6
  664.2 45.6 %reduce-scatter.24.cloned.1.call-done = bf16[256,2048]{1,0:T(8,128)(2,1)} async-done(((bf16[2048,2048]{1,0:T(8,128)(2,1)}), bf16[256,2048]{1,0:T(8,128)(2,1)}) %reduce-scatter.24.cloned.1.call-update) | async-done | bytes 1048592 | tf_op jit(solution)/shard_map/reduce_scatter | solution.py:460
  709.9 74.6 %reduce-scatter.18.cloned.1.call-done = bf16[256,2048]{1,0:T(8,128)(2,1)} async-done(((bf16[2048,2048]{1,0:T(8,128)(2,1)}), bf16[256,2048]{1,0:T(8,128)(2,1)}) %reduce-scatter.18.cloned.1.call-update) | async-done | bytes 1048592 | tf_op jit(solution)/shard_map/reduce_scatter | solution.py:460
  784.5 7.5 fusion.42
  792.0 55.4 %reduce-scatter.28.cloned.1.call-done = bf16[256,1408]{1,0:T(8,128)(2,1)} async-done(((bf16[2048,1408]{1,0:T(8,128)(2,1)}), bf16[256,1408]{1,0:T(8,128)(2,1)}) %reduce-scatter.28.cloned.1.call-update) | async-done | bytes 720912 | tf_op jit(solution)/shard_map/reduce_scatter | solution.py:460
  847.4 2.3 convert_element_type.136
  849.7 60.2 %reduce-scatter.30.cloned.1.call-done = bf16[256,1408]{1,0:T(8,128)(2,1)} async-done(((bf16[2048,1408]{1,0:T(8,128)(2,1)}), bf16[256,1408]{1,0:T(8,128)(2,1)}) %reduce-scatter.30.cloned.1.call-update) | async-done | bytes 720912 | tf_op jit(solution)/shard_map/reduce_scatter | solution.py:460
  909.9 2.3 convert_element_type.138
  912.2 60.4 %reduce-scatter.32.cloned.1.call-done = bf16[256,1408]{1,0:T(8,128)(2,1)} async-done(((bf16[2048,1408]{1,0:T(8,128)(2,1)}), bf16[256,1408]{1,0:T(8,128)(2,1)}) %reduce-scatter.32.cloned.1.call-update) | async-done | bytes 720912 | tf_op jit(solution)/shard_map/reduce_scatter | solution.py:460
  972.7 2.3 convert_element_type.140
  975.0 4.8 fusion.17
  979.9 39.8 %all-reduce.4 = f32[2,32,64]{2,0,1:T(2,128)S(1)} all-reduce(f32[2,32,64]{2,0,1:T(2,128)S(1)} %pad_maximum_fusion.8), channel_id=5, replica_groups=mesh['dp'=8,'tensor'=4] {'dp','tensor'}, use_global_device_ids=true, to_apply=%region_11.12.clone | all-reduce | flops 4096 | bytes 32768
  1020.2 3.2 fusion.16
  1023.4 89.8 %reduce-scatter.22.cloned.1.call-done = bf16[64,512]{1,0:T(8,128)(2,1)} async-done(((bf16[2048,512]{1,0:T(8,128)(2,1)}), bf16[64,512]{1,0:T(8,128)(2,1)}) %reduce-scatter.22.cloned.1.call-update) | async-done | bytes 65552 | tf_op jit(solution)/shard_map/reduce_scatter | solution.py:460
  1113.2 1.5 convert_element_type.132
  1114.7 25.8 %reduce-scatter.26.cloned.1.call-done = bf16[256,512]{1,0:T(8,128)(2,1)} async-done(((bf16[256,2048]{1,0:T(8,128)(2,1)}), bf16[256,512]{1,0:T(8,128)(2,1)}) %reduce-scatter.26.cloned.1.call-update) | async-done | bytes 262160 | tf_op jit(solution)/shard_map/reduce_scatter | solution.py:460
  1140.4 1.8 convert_element_type.134
  1142.2 26.3 %reduce-scatter.20.cloned.1.call-done = bf16[256,512]{1,0:T(8,128)(2,1)} async-done(((bf16[256,2048]{1,0:T(8,128)(2,1)}), bf16[256,512]{1,0:T(8,128)(2,1)}) %reduce-scatter.20.cloned.1.call-update) | async-done | bytes 262160 | tf_op jit(solution)/shard_map/reduce_scatter | solution.py:460
  1168.5 1.8 convert_element_type.130
  (110 shorter events, 5.5 us)
Async XLA Ops:
  7.2 178.1 %copy-start.9 = (bf16[256,2048]{1,0:T(8,128)(2,1)S(1)}, bf16[256,2048]{1,0:T(8,128)(2,1)}, u32[]{:S(2)}) copy-start(bf16[256,2048]{1,0:T(8,128)(2,1)} %param.11) | copy-start | bytes 3145732
  7.2 178.1 %copy-start.14 = (f32[2048]{0:T(1024)S(1)}, f32[2048]{0:T(1024)}, u32[]{:S(2)}) copy-start(f32[2048]{0:T(1024)} %param.13) | copy-start | bytes 24580
  7.2 211.2 %all-gather.3.cloned.1.call-start = ((), (), s32[]{:S(2)}) async-start(), calls=%async_computation.11 | async-start | bytes 1310720 | tf_op jit(solution)/shard_map/all_gather | solution.py:457
  185.3 2.4 copy-start.16
  189.8 151.6 %all-gather.5.cloned.1.call-start = ((), (), s32[]{:S(2)}) async-start(), calls=%async_computation.12 | async-start | bytes 5242880 | tf_op jit(solution)/shard_map/all_gather | solution.py:457
  222.0 0.8 copy-start.2
  227.1 1.2 copy-start
  228.3 1.0 copy-start.1
  229.4 22.8 %copy-start.10 = (bf16[256,2048]{1,0:T(8,128)(2,1)S(1)}, bf16[256,2048]{1,0:T(8,128)(2,1)}, u32[]{:S(2)}) copy-start(bf16[256,2048]{1,0:T(8,128)(2,1)} %param.11) | copy-start | bytes 3145732
  252.2 6.3 copy-start.5
  252.2 7.6 copy-start.15
  258.5 1.3 copy-start.12
  261.0 212.8 %reduce-scatter.14.cloned.1.call-start = ((), (), s32[]{:S(2)}) async-start(), calls=%async_computation.14 | async-start | bytes 5242880 | tf_op jit(solution)/shard_map/reduce_scatter | solution.py:460
  341.4 12.4 %copy-start.17 = (bf16[1024,2048]{1,0:T(8,128)(2,1)S(1)}, bf16[1024,2048]{1,0:T(8,128)(2,1)}, u32[]{:S(2)}) copy-start(bf16[1024,2048]{1,0:T(8,128)(2,1)} %all-gather.5.cloned.1.call-done) | copy-start | bytes 12582916
  341.4 22.9 %slice-start = ((s8[5767168]{0:T(1024)(128)(4,1)}), s8[4194304]{0:T(1024)(128)(4,1)S(1)}, s32[]{:S(2)}) async-start(s8[5767168]{0:T(1024)(128)(4,1)} %bitcast.79), calls=%async_computation.24 | async-start | bytes 8388608
  353.8 10.5 slice-start.1
  353.8 25.7 %slice-start.4 = ((s8[5767168]{0:T(1024)(128)(4,1)}), s8[4194304]{0:T(1024)(128)(4,1)S(1)}, s32[]{:S(2)}) async-start(s8[5767168]{0:T(1024)(128)(4,1)} %bitcast.83), calls=%async_computation.28 | async-start | bytes 8388608
  353.8 34.3 %slice-start.2 = ((s8[5767168]{0:T(1024)(128)(4,1)}), s8[4194304]{0:T(1024)(128)(4,1)S(1)}, s32[]{:S(2)}) async-start(s8[5767168]{0:T(1024)(128)(4,1)} %bitcast.81), calls=%async_computation.26 | async-start | bytes 8388608
  364.3 15.3 %slice-start.5 = ((s8[5767168]{0:T(1024)(128)(4,1)}), s8[1572864]{0:T(1024)(128)(4,1)S(1)}, s32[]{:S(2)}) async-start(s8[5767168]{0:T(1024)(128)(4,1)} %bitcast.83), calls=%async_computation.29 | async-start | bytes 3145728
  364.3 23.8 %slice-start.3 = ((s8[5767168]{0:T(1024)(128)(4,1)}), s8[1572864]{0:T(1024)(128)(4,1)S(1)}, s32[]{:S(2)}) async-start(s8[5767168]{0:T(1024)(128)(4,1)} %bitcast.81), calls=%async_computation.27 | async-start | bytes 3145728
  398.3 155.0 %reduce-scatter.12.cloned.1.call-start = ((), (), s32[]{:S(2)}) async-start(), calls=%async_computation.13 | async-start | bytes 5242880 | tf_op jit(solution)/shard_map/reduce_scatter | solution.py:460
  409.4 251.5 %reduce-scatter.16.cloned.1.call-start = ((), (), s32[]{:S(2)}) async-start(), calls=%async_computation.15 | async-start | bytes 1310720 | tf_op jit(solution)/shard_map/reduce_scatter | solution.py:460
  557.7 6.5 copy-start.7
  557.7 6.5 copy-start.3
  557.7 6.5 copy-start.4
  601.2 7.2 copy-start.6
  601.2 7.2 copy-start.8
  608.3 101.5 %reduce-scatter.24.cloned.1.call-start = ((), (), s32[]{:S(2)}) async-start(), calls=%async_computation.19 | async-start | bytes 9437184 | tf_op jit(solution)/shard_map/reduce_scatter | solution.py:460
  614.0 170.5 %reduce-scatter.18.cloned.1.call-start = ((), (), s32[]{:S(2)}) async-start(), calls=%async_computation.16 | async-start | bytes 9437184 | tf_op jit(solution)/shard_map/reduce_scatter | solution.py:460
  617.4 3.0 copy-start.11
  619.4 1.0 copy-start.13
  626.2 221.2 %reduce-scatter.28.cloned.1.call-start = ((), (), s32[]{:S(2)}) async-start(), calls=%async_computation.21 | async-start | bytes 6488064 | tf_op jit(solution)/shard_map/reduce_scatter | solution.py:460
  637.4 272.6 %reduce-scatter.30.cloned.1.call-start = ((), (), s32[]{:S(2)}) async-start(), calls=%async_computation.22 | async-start | bytes 6488064 | tf_op jit(solution)/shard_map/reduce_scatter | solution.py:460
  648.5 324.2 %reduce-scatter.32.cloned.1.call-start = ((), (), s32[]{:S(2)}) async-start(), calls=%async_computation.23 | async-start | bytes 6488064 | tf_op jit(solution)/shard_map/reduce_scatter | solution.py:460
  660.8 452.4 %reduce-scatter.22.cloned.1.call-start = ((), (), s32[]{:S(2)}) async-start(), calls=%async_computation.18 | async-start | bytes 2162688 | tf_op jit(solution)/shard_map/reduce_scatter | solution.py:460
  664.2 476.3 %reduce-scatter.26.cloned.1.call-start = ((), (), s32[]{:S(2)}) async-start(), calls=%async_computation.20 | async-start | bytes 1310720 | tf_op jit(solution)/shard_map/reduce_scatter | solution.py:460
  709.8 458.8 %reduce-scatter.20.cloned.1.call-start = ((), (), s32[]{:S(2)}) async-start(), calls=%async_computation.17 | async-start | bytes 1310720 | tf_op jit(solution)/shard_map/reduce_scatter | solution.py:460
Sparse Core Ops, SparseCore 0:
  189.9 28.4 all-gather.2
  261.1 80.2 all-gather.4
  398.5 75.2 reduce-scatter.13
  476.0 77.2 reduce-scatter.11
  608.4 27.6 reduce-scatter.15
  639.8 69.9 reduce-scatter.23
  713.2 71.2 reduce-scatter.17
  788.3 59.0 reduce-scatter.27
  850.9 59.0 reduce-scatter.29
  913.6 59.0 reduce-scatter.31
  974.9 138.1 reduce-scatter.21
  1115.4 24.9 reduce-scatter.25
  1142.7 25.7 reduce-scatter.19

commit v2 on v1

--- a/solution.py
+++ b/solution.py
@@ -434,6 +434,298 @@
     )(w_keyval, w_query, w_output, w_down, w_gate, w_up, cotangent)
 
 
+def add_rows(target, source, step=32):
+    @pl.loop(0, target.shape[0] // step)
+    def _(index):
+        window = pl.ds(pl.multiple_of(index * step, step), step)
+        target[window, :] = target[window, :] + source[window, :]
+
+
+def scatter_kernel(
+    go_ref, gq_ref, kv_ref, gd_ref, gg_ref, gu_ref, branch_ref, residual_ref,
+    go_out, gq_out, kv_out, gd_out, gg_out, gu_out, layer_out,
+    go_core, gq_core, kv_core, gd_core, gg_core, gu_core,
+    go_part, gq_part, kv_part, gd_part, gg_part, gu_part,
+    go_side, gq_side, kv_side, gd_side, gg_side, gu_side,
+    go_near, gq_near, kv_near, gd_near, gg_near, gu_near,
+    go_line, gq_line, kv_line, layer_line,
+    go_in, gq_in, kv_in, layer_in,
+    held, total_ref,
+    load_sem, core_load, core_send, core_recv, p_send, p_recv, l_send, l_recv, layer_load,
+):
+    dp, place = lax.axis_index("dp"), lax.axis_index("tensor")
+    rows = go_part.shape[1]
+    half = rows // 2
+    enter(dp, place)
+    x, y, core = flip(dp, 2), flip(dp, 4), flip(dp, 1)
+    far = flip(x, 4)
+    mine = (dp, x, y, far)
+    theirs = tuple(flip(owner, 1) for owner in mine)
+    grads = (go_ref, gq_ref, kv_ref, gd_ref, gg_ref, gu_ref)
+    outs = (go_out, gq_out, kv_out, gd_out, gg_out, gu_out)
+    cores = (go_core, gq_core, kv_core, gd_core, gg_core, gu_core)
+    parts = (go_part, gq_part, kv_part, gd_part, gg_part, gu_part)
+    sides = (go_side, gq_side, kv_side, gd_side, gg_side, gu_side)
+    nears = (go_near, gq_near, kv_near, gd_near, gg_near, gu_near)
+    lines = (go_line, gq_line, kv_line, layer_line)
+    arrivals = (go_in, gq_in, kv_in, layer_in)
+    count = len(grads)
+    front, back = pl.ds(0, half), pl.ds(half, half)
+
+    def rows_of(owner):
+        return pl.ds(pl.multiple_of(owner * rows, rows), rows)
+
+    def remote(src, dst, send, recv, device):
+        return pltpu.make_async_remote_copy(
+            src_ref=src, dst_ref=dst, send_sem=send, recv_sem=recv,
+            device_id=device, device_id_type=MESH,
+        )
+
+    def core_copy(i, k):
+        return remote(
+            grads[i].at[rows_of(theirs[k]), :], cores[i].at[k],
+            core_send.at[i, k], core_recv.at[i, k], (core, place),
+        )
+
+    def own_load(i, k):
+        return pltpu.make_async_copy(
+            grads[i].at[rows_of(mine[k]), :], parts[i].at[k], load_sem.at[i, k]
+        )
+
+    def core_fetch(i, k):
+        width = grads[i].shape[1]
+        return pltpu.make_async_copy(
+            cores[i].at[k], held.at[k, :, pl.ds(0, width)], core_load.at[k]
+        )
+
+    def plane_copy(i, lane):
+        part = parts[i]
+        src, dst, device = (
+            (part.at[3, front, :], sides[i].at[0], y),
+            (part.at[3, back, :], sides[i].at[1], x),
+            (part.at[1, back, :], nears[i].at[0, back, :], x),
+            (part.at[2, front, :], nears[i].at[1, front, :], y),
+            (part.at[1, front, :], nears[i].at[0, front, :], x),
+            (part.at[2, back, :], nears[i].at[1, back, :], y),
+        )[lane]
+        return remote(src, dst, p_send.at[i, lane], p_recv.at[i, lane], (device, place))
+
+    def stage_core(i):
+        width = grads[i].shape[1]
+        for k in (3, 1, 2, 0):
+            core_copy(i, k).wait_recv()
+            core_fetch(i, k).start()
+        for k in (3, 1, 2, 0):
+            core_fetch(i, k).wait()
+            own_load(i, k).wait()
+            add_rows(parts[i].at[k], held.at[k, :, pl.ds(0, width)])
+            for lane in ((), (2,), (3,), (0, 1))[k]:
+                plane_copy(i, lane).start()
+
+    def stage_side(i):
+        plane_copy(i, 0).wait_recv()
+        add_rows(parts[i].at[1, front, :], sides[i].at[0])
+        plane_copy(i, 4).start()
+        plane_copy(i, 1).wait_recv()
+        add_rows(parts[i].at[2, back, :], sides[i].at[1])
+        plane_copy(i, 5).start()
+
+    def stage_near(i):
+        for lane in (2, 3, 4, 5):
+            plane_copy(i, lane).wait_recv()
+        part, near, out = parts[i], nears[i], outs[i]
+
+        @pl.loop(0, rows // 32)
+        def _(index):
+            window = pl.ds(pl.multiple_of(index * 32, 32), 32)
+            total = (
+                part[0, window, :].astype(jnp.float32)
+                + near[0, window, :].astype(jnp.float32)
+                + near[1, window, :].astype(jnp.float32)
+            )
+            if i >= 3:
+                out[window, :] = total
+            elif i < 2:
+                width = lines[i].shape[2]
+                for rank in range(4):
+                    lines[i][rank, window, :] = total[:, rank * width : (rank + 1) * width].astype(
+                        jnp.bfloat16
+                    )
+            else:
+                per = rows // 4
+                lines[i][index * 32 // per, pl.ds(pl.multiple_of(index * 32 % per, 32), 32), :] = (
+                    total.astype(jnp.bfloat16)
+                )
+
+    def line_copy(i, rank, slot, step):
+        return remote(
+            lines[i].at[rank], arrivals[i].at[slot], l_send.at[i, rank], l_recv.at[i, slot],
+            (dp, place + step),
+        )
+
+    def line_step(i, step):
+        down, up = place - 3 + step, place + 3 - step
+
+        @pl.when(down >= 0)
+        def _():
+            @pl.when(place < 3)
+            def _():
+                line_copy(i, down, down, -1).wait_recv()
+                add_rows(lines[i].at[down], arrivals[i].at[down])
+
+            line_copy(i, down, down, -1).start()
+
+        @pl.when(up <= 3)
+        def _():
+            @pl.when(place > 0)
+            def _():
+                line_copy(i, up, up, 1).wait_recv()
+                add_rows(lines[i].at[up], arrivals[i].at[up])
+
+            line_copy(i, up, 4 if step == 2 else up, 1).start()
+
+    def line_last(i, begin, add, finish):
+        begin(lines[i].at[place])
+
+        @pl.when(place < 3)
+        def _():
+            line_copy(i, place, place, 1).wait_recv()
+            add(arrivals[i].at[place])
+
+        @pl.when(place > 0)
+        def _():
+            line_copy(i, place, 4, 1).wait_recv()
+            add(arrivals[i].at[4])
+
+        finish()
+
+    def line_sent(i):
+        for rank in range(4):
+
+            @pl.when(rank != place)
+            def _():
+                line_copy(i, rank, rank, 1).wait_send()
+
+    def by_rows(total_rows, act):
+        @pl.loop(0, total_rows // 32)
+        def _(index):
+            act(pl.ds(pl.multiple_of(index * 32, 32), 32))
+
+    def line_out(i):
+        out = outs[i]
+        size = out.shape[0]
+
+        def begin(ref):
+            def act(window):
+                out[window, :] = ref[window, :].astype(jnp.float32)
+
+            by_rows(size, act)
+
+        def add(ref):
+            def act(window):
+                out[window, :] += ref[window, :].astype(jnp.float32)
+
+            by_rows(size, act)
+
+        line_last(i, begin, add, lambda: None)
+
+    branch_load = pltpu.make_async_copy(branch_ref, layer_line, layer_load)
+    branch_load.start()
+    for i in range(count):
+        for k in (3, 1, 2, 0):
+            core_copy(i, k).start()
+            own_load(i, k).start()
+    branch_load.wait()
+    line_step(3, 0)
+    for i in range(count + 2):
+        if i < count:
+            stage_core(i)
+        if 1 <= i <= count:
+            stage_side(i - 1)
+        if i >= 2:
+            stage_near(i - 2)
+        for j in range(3):
+            if 0 <= i - 2 - j < 3:
+                line_step(j, i - 2 - j)
+        if i in (2, 4):
+            line_step(3, i // 2)
+    for j in range(3):
+        line_out(j)
+
+    def layer_begin(ref):
+        def act(window):
+            total_ref[window, :] = residual_ref[window, :] + ref[window, :].astype(jnp.float32)
+
+        by_rows(rows, act)
+
+    def layer_add(ref):
+        def act(window):
+            total_ref[window, :] += ref[window, :].astype(jnp.float32)
+
+        by_rows(rows, act)
+
+    def layer_finish():
+        def act(window):
+            layer_out[window, :] = total_ref[window, :].astype(jnp.bfloat16)
+
+        by_rows(rows, act)
+
+    line_last(3, layer_begin, layer_add, layer_finish)
+    for i in range(count):
+        for k in range(4):
+            core_copy(i, k).wait_send()
+        for lane in range(6):
+            plane_copy(i, lane).wait_send()
+    for i in range(4):
+        line_sent(i)
+
+
+def scatter_all(grads, branch, residual):
+    low = jnp.bfloat16
+    n_line = lax.axis_size("tensor")
+    rows = grads[0].shape[0] // lax.axis_size("dp")
+    half = rows // 2
+    widths = [grad.shape[1] for grad in grads]
+    square = widths[0] // n_line
+    few = rows // n_line
+    tokens, width = residual.shape
+    anywhere = pl.BlockSpec(memory_space=pl.ANY)
+    in_vmem = pl.BlockSpec(memory_space=pltpu.VMEM)
+    out_shape = [
+        jax.ShapeDtypeStruct((rows, square), jnp.float32),
+        jax.ShapeDtypeStruct((rows, square), jnp.float32),
+        jax.ShapeDtypeStruct((few, widths[2]), jnp.float32),
+    ]
+    out_shape += [jax.ShapeDtypeStruct((rows, w), jnp.float32) for w in widths[3:]]
+    out_shape += [jax.ShapeDtypeStruct((tokens, width), low)]
+    out_shape += [jax.ShapeDtypeStruct((4, rows, w), low) for w in widths]
+    scratch = [pltpu.VMEM((4, rows, w), low) for w in widths]
+    scratch += [pltpu.VMEM((2, half, w), low) for w in widths]
+    scratch += [pltpu.VMEM((2, rows, w), low) for w in widths]
+    line_shapes = [(rows, square), (rows, square), (few, widths[2]), (tokens, width)]
+    scratch += [pltpu.VMEM((4,) + shape, low) for shape in line_shapes]
+    scratch += [pltpu.VMEM((5,) + shape, low) for shape in line_shapes]
+    scratch += [pltpu.VMEM((4, rows, max(widths)), low)]
+    scratch += [pltpu.VMEM((tokens, width), jnp.float32)]
+    dma = pltpu.SemaphoreType.DMA
+    scratch += [
+        dma((6, 4)), dma((4,)), dma((6, 4)), dma((6, 4)), dma((6, 6)), dma((6, 6)),
+        dma((4, 4)), dma((4, 5)), dma,
+    ]
+    results = pl.pallas_call(
+        scatter_kernel,
+        out_shape=out_shape,
+        in_specs=[anywhere] * 7 + [in_vmem],
+        out_specs=[in_vmem] * 7 + [anywhere] * 6,
+        scratch_shapes=scratch,
+        compiler_params=pltpu.CompilerParams(
+            collective_id=1, has_side_effects=True, vmem_limit_bytes=62 * 1024 * 1024
+        ),
+        name="scatter_all",
+    )(*grads, branch.reshape(n_line, tokens, width), residual)
+    return results[:7]
+
+
 def local(
     tokens,
     segments,
@@ -459,7 +751,8 @@
     def scatter(array, axes, axis=0):
         return lax.psum_scatter(array, axes, scatter_dimension=axis, tiled=True)
 
-    if (lax.axis_size("dp"), lax.axis_size("tensor")) == (8, 4):
+    by_kernels = (lax.axis_size("dp"), lax.axis_size("tensor")) == (8, 4)
+    if by_kernels:
         full_keyval, full_query, full_output, full_down, full_gate, full_up, piece = gather_all(
             w_keyval, w_query, w_output, w_down, w_gate, w_up, cotangent
         )
@@ -513,9 +806,7 @@
     d_normed_mlp = scatter(
         (dot_nt(d_gate, full_gate) + dot_nt(d_up, full_up)).astype(low), "tensor"
     ).astype(jnp.float32)
-    layer_rows = residual + scatter(dot_nt(hidden_low, full_down).astype(low), "tensor").astype(
-        jnp.float32
-    )
+    branch = dot_nt(hidden_low, full_down).astype(low)
     grad_down = dot_tn(piece, hidden_low)
     grad_gate = dot_tn(gathered_mlp, d_gate)
     grad_up = dot_tn(gathered_mlp, d_up)
@@ -545,6 +836,30 @@
     d_normed_attn = dot_nt(dq_low, full_query) + dot_nt(dkv_low, full_keyval)
     d_norm_attn, gain_attn_part = norm_backward(d_normed_attn, unit_attn, inverse_attn, gain_attn)
     grad_tokens = (d_residual + d_norm_attn).astype(low)
+
+    if by_kernels:
+        gain_columns = jnp.stack([gain_attn_part, gain_mlp_part], axis=1)
+        gain_columns = jnp.pad(gain_columns, ((0, 0), (0, 126)))
+        grad_narrow = jnp.concatenate([grad_keyval, gain_columns], axis=1)
+        grads = (grad_output, grad_query, grad_narrow, grad_down, grad_gate, grad_up)
+        to_output, to_query, to_narrow, to_down, to_gate, to_up, layer_out = scatter_all(
+            [grad.astype(low) for grad in grads], branch, residual
+        )
+        wide = grad_keyval.shape[1]
+        return (
+            layer_out,
+            grad_tokens,
+            to_narrow[:, wide],
+            to_query,
+            to_narrow[:, :wide],
+            to_output,
+            to_narrow[:, wide + 1],
+            to_gate,
+            to_up,
+            to_down,
+        )
+
+    layer_rows = residual + scatter(branch, "tensor").astype(jnp.float32)
 
     def shares(grad):
         return scatter(grad.astype(low), "dp").astype(jnp.float32)

time: 1180 us -> 746 us (0.63)
  waiting for transfers between devices: 673 us -> 127 us
  Pallas kernels: 230 us -> 396 us
  blocking collectives: 39.8 us -> 0 us
    reduce_scatter x11 -> x2, waiting for transfers between devices: 574 us -> 42.1 us  [scatter(): return lax.psum_scatter(array, axes, scatter_dimension=axis, tiled=True)]
    pallas_call x0 -> x1, Pallas kernels: none -> 166 us  [scatter_all(): pl.pallas_call(scatter_kernel, out_shape=out_shape, in_specs=[anywhere] *...]
    unnamed x1 -> x0, blocking collectives: 39.8 us -> none
    all_gather x2, waiting for transfers between devices: 99.3 us -> 85 us  [gather(): return lax.all_gather(array, axes, axis=axis, tiled=True)]
    convert_element_type x6 -> x0, other arithmetic: 12 us -> none  [the longest x3 6.91 us: shares(): return scatter(grad.astype(low), 'dp').astype(jnp.float32)]
  transfers between devices with their start and end apart: 13 -> 4, of which waited for: 12 -> 4; matrix products, arithmetic and copies ran while one was open for 9% -> 11% of each run, Pallas kernels for 0% -> 0%
where the time goes in v2:
time: 746 us; the launch traced here: 740 us
  Pallas kernels  396 us (53%)
  matrix products  140 us (19%)
  waiting for transfers between devices  127 us (17%)
  local copies, waits for them, and re-layouts  34.1 us (5%)
  other arithmetic  27.8 us (4%)
  between operations  14.5 us (2%)
    pallas_call x1, Pallas kernels, gather_all(): pl.pallas_call(gather_kernel, out_shape=shapes, in_specs=[anywhere] * 7,...  176 us
    pallas_call x1, Pallas kernels, scatter_all(): pl.pallas_call(scatter_kernel, out_shape=out_shape, in_specs=[anywhere] *...  166 us
    all_gather x2, waiting for transfers between devices, gather(): return lax.all_gather(array, axes, axis=axis, tiled=True)  85 us
    dot_general x6, matrix products, dot_nn(): return jnp.dot(left, right, preferred_element_type=jnp.float32)  54.6 us
    dot_general x6, matrix products, dot_nt(): lax.dot_general(left, right, (((1,), (1,)), ((), ())), preferred_element_...  45.1 us
    reduce_scatter x2, waiting for transfers between devices, scatter(): return lax.psum_scatter(array, axes, scatter_dimension=axis, tiled=True)  42.1 us
    dot_general x6, matrix products, dot_tn(): lax.dot_general(left, right, (((0,), (0,)), ((), ())), preferred_element_...  39.9 us
    pallas_call x1, Pallas kernels, attend_backward(): pl.pallas_call(attend_backward_kernel, grid=(KVH,), in_specs=[columns_of(...  30.6 us
  transfers between devices with their start and end apart: 4, of which 4 were waited for; matrix products, arithmetic and copies ran while one was open for 11% of the time, Pallas kernels for 0%

profile of v2, /device:TPU:0, one launch (start us, length us, event | category | flops | bytes accessed | tf_op | source)
XLA Modules:
  0.0 739.8 jit_solution(15278105724451414361)
XLA Ops:
  7.3 1.6 fusion.20
  8.9 176.4 %gather_all.1 = (bf16[2048,512]{1,0:T(8,128)(2,1)}, bf16[2048,2048]{1,0:T(8,128)(2,1)}, bf16[2048,2048]{1,0:T(8,128)(2,1)}, bf16[2048,1408]{1,0:T(8,128)(2,1)}, ...) custom-call(bf16[256,512]{1,0:T(8,128)(2,1)} %kv_ref.1, ...), custom_call_target="tpu_custom_call" | custom-call | tf_op jit(solution)/shard_map/gather_all/pallas_call | solution.py:420
  185.3 2.3 fusion.33
  188.7 0.8 fusion.28
  189.7 0.7 pad_maximum_fusion.2
  190.6 6.8 fusion.35
  197.4 0.3 multiply_subtract_fusion
  198.0 0.8 copy.51.query_ref
  198.9 1.2 fusion.25.bias_ref
  200.1 19.0 %all-gather.3.cloned.1.call-done = bf16[1024,512]{1,0:T(8,128)(2,1)} async-done(((bf16[256,512]{1,0:T(8,128)(2,1)}), bf16[1024,512]{1,0:T(8,128)(2,1)}) %all-gather.3.cloned.1.call-update) | async-done | bytes 1048592 | tf_op jit(solution)/shard_map/all_gather | solution.py:749
  219.0 2.1 fusion.38
  221.3 1.3 copy.65
  222.6 0.8 copy-done.2
  223.4 2.1 fusion.39
  225.5 2.0 copy.50
  227.6 1.2 copy-done
  228.8 1.0 copy-done.1
  229.9 22.8 %attend_forward.1 = (bf16[256,2048]{1,0:T(8,128)(2,1)S(1)}, f32[4,8,256]{2,1,0:T(8,128)S(1)}) custom-call(bf16[256,2048]{1,0:T(8,128)(2,1)S(1)} %copy.51.query_ref, bf16[4,1024,128]{2,1,0:T(8,128)(2,1)S(1)} %get-tuple-element.66.front_ref.kf_ref, bf16[4,1024,128]{2,1,0:T(8,128)(2,1)S(1)} %get-tuple-element.65.back_ref.kb_ref, ...), custom_call_target="tpu_custom_call" | custom-call | tf_op jit(solution)/shard_map/attend_forward/pallas_call | solution.py:157
  252.7 6.3 multiply_reduce_fusion
  259.0 1.3 copy-done.7
  260.3 1.2 multiply_convert_fusion.3
  261.6 12.0 %fusion.41 = f32[1024,1408]{1,0:T(8,128)} fusion(bf16[1024,2048]{1,0:T(8,128)(2,1)} %get-tuple-element.33, bf16[2048,1408]{1,0:T(8,128)(2,1)} %get-tuple-element.34), kind=kOutput, calls=%fused_computation.95 | convolution fusion | flops 5905580032 | bytes 15728640 | tf_op jit(solution)/shard_map/dot_general | solution.py:66
  273.6 2.4 copy.54
  275.9 66.0 %all-gather.5.cloned.1.call-done = bf16[1024,2048]{1,0:T(8,128)(2,1)} async-done(((bf16[256,2048]{1,0:T(8,128)(2,1)}), bf16[1024,2048]{1,0:T(8,128)(2,1)}) %all-gather.5.cloned.1.call-update) | async-done | bytes 4194320 | tf_op jit(solution)/shard_map/all_gather | solution.py:749
  342.0 11.8 %fusion.42 = f32[1024,1408]{1,0:T(8,128)} fusion(bf16[1024,2048]{1,0:T(8,128)(2,1)} %all-gather.5.cloned.1.call-done, bf16[2048,1408]{1,0:T(8,128)(2,1)} %get-tuple-element.36), kind=kOutput, calls=%fused_computation.96 | convolution fusion | flops 5905580032 | bytes 15728640 | tf_op jit(solution)/shard_map/dot_general | solution.py:66
  353.8 15.2 %multiply_convert_fusion = (bf16[1024,1408]{1,0:T(8,128)(2,1)}, bf16[1024,1408]{1,0:T(8,128)(2,1)}, bf16[1024,1408]{1,0:T(8,128)(2,1)}) fusion(f32[1024,1408]{1,0:T(8,128)} %fusion.42, f32[1024,1408]{1,0:T(8,128)} %fusion.41, bf16[1024,2048]{1,0:T(8,128)(2,1)S(1)} %copy-done.29, bf16[2048,1408]{1,0:T(8,128)(2,1)} %get-tuple-element.35), kind=kOutput, calls=%fused_computation.6 | convolution fusion | flops 5927206912 | bytes 30146560 | tf_op jit(solution)/shard_map/dot_general | solution.py:66
  369.0 10.4 %fusion.43 = f32[1024,2048]{1,0:T(8,128)} fusion(bf16[1024,1408]{1,0:T(8,128)(2,1)} %get-tuple-element.55, bf16[2048,1408]{1,0:T(8,128)(2,1)S(1)} %bitcast.82), kind=kOutput, calls=%fused_computation.97 | convolution fusion | flops 5905580032 | bytes 17039360 | tf_op jit(solution)/shard_map/dot_general | solution.py:70
  379.4 10.5 %add_convert_fusion = bf16[1024,2048]{1,0:T(8,128)(2,1)} fusion(f32[1024,2048]{1,0:T(8,128)} %fusion.43, bf16[1024,1408]{1,0:T(8,128)(2,1)S(1)} %copy-done.32, bf16[2048,1408]{1,0:T(8,128)(2,1)S(1)} %bitcast.80), kind=kOutput, calls=%fused_computation | convolution fusion | flops 5909774336 | bytes 21233664 | tf_op jit(solution)/shard_map/dot_general | solution.py:70
  389.9 0.5 reduce-scatter.5.cloned.1.call-start
  390.5 3.4 fusion.37
  393.9 11.6 %convolution_convert_fusion.5 = bf16[1024,2048]{1,0:T(8,128)(2,1)} fusion(bf16[1024,1408]{1,0:T(8,128)(2,1)S(1)} %copy-done.34, bf16[2048,1408]{1,0:T(8,128)(2,1)} %get-tuple-element.34), kind=kOutput, calls=%fused_computation.13 | convolution fusion | flops 5907677184 | bytes 12845056 | tf_op jit(solution)/shard_map/dot_general | solution.py:70
  405.5 8.7 %convolution_convert_fusion.2.gd_ref = bf16[2048,1408]{1,0:T(8,128)(2,1)} fusion(bf16[1024,2048]{1,0:T(8,128)(2,1)S(1)} %copy-done.28, bf16[1024,1408]{1,0:T(8,128)(2,1)S(1)} %copy-done.34), kind=kOutput, calls=%fused_computation.3 | convolution fusion | flops 5908463616 | bytes 12845056 | tf_op jit(solution)/shard_map/dot_general | solution.py:76
  414.2 8.7 %convolution_convert_fusion.gu_ref = bf16[2048,1408]{1,0:T(8,128)(2,1)} fusion(bf16[1024,2048]{1,0:T(8,128)(2,1)S(1)} %copy-done.30, bf16[1024,1408]{1,0:T(8,128)(2,1)S(1)} %copy-done.33), kind=kOutput, calls=%fused_computation.1 | convolution fusion | flops 5908463616 | bytes 12845056 | tf_op jit(solution)/shard_map/dot_general | solution.py:76
  422.9 8.8 %convolution_convert_fusion.1.gg_ref = bf16[2048,1408]{1,0:T(8,128)(2,1)} fusion(bf16[1024,2048]{1,0:T(8,128)(2,1)S(1)} %copy-done.30, bf16[1024,1408]{1,0:T(8,128)(2,1)S(1)} %copy-done.31), kind=kOutput, calls=%fused_computation.2 | convolution fusion | flops 5908463616 | bytes 12845056 | tf_op jit(solution)/shard_map/dot_general | solution.py:76
  431.7 33.6 %reduce-scatter.3.cloned.1.call-done = bf16[256,2048]{1,0:T(8,128)(2,1)} async-done(((bf16[1024,2048]{1,0:T(8,128)(2,1)}), bf16[256,2048]{1,0:T(8,128)(2,1)}) %reduce-scatter.3.cloned.1.call-update) | async-done | bytes 1048592 | tf_op jit(solution)/shard_map/reduce_scatter | solution.py:752
  465.4 2.8 fusion.12
  468.2 1.9 fusion.11
  470.2 6.5 convolution_convert_fusion.7.grad_ref
  476.7 30.6 %attend_backward.1 = (f32[256,2048]{1,0:T(8,128)}, f32[4,1024,128]{2,1,0:T(8,128)}, f32[4,1024,128]{2,1,0:T(8,128)}) custom-call(bf16[256,2048]{1,0:T(8,128)(2,1)S(1)} %copy.51.query_ref, bf16[256,2048]{1,0:T(8,128)(2,1)S(1)} %convolution_convert_fusion.7.grad_ref, bf16[4,1024,128]{2,1,0:T(8,128)(2,1)S(1)} %get-tuple-element.66.front_ref.kf_ref, ...), custom_call_target="tpu_custom_call" | custom-call | tf_op jit(solution)/shard_map/attend_backward/pallas_call | solution.py:182
  507.3 4.6 fusion.22
  512.0 1.1 copy.59
  513.1 1.1 copy.60
  514.2 2.2 pad_maximum_fusion.1
  516.5 2.0 copy.58
  518.6 2.0 subtract_convert_fusion
  520.7 5.8 convolution_convert_fusion.3.gq_ref
  526.5 5.6 convolution_convert_fusion.4.go_ref
  532.1 3.7 fusion.44
  535.8 8.5 %reduce-scatter.5.cloned.1.call-done = bf16[256,512]{0,1:T(8,128)(2,1)} async-done(((bf16[1024,512]{0,1:T(8,128)(2,1)}), bf16[256,512]{0,1:T(8,128)(2,1)}) %reduce-scatter.5.cloned.1.call-update) | async-done | bytes 262160 | tf_op jit(solution)/shard_map/reduce_scatter | solution.py:752
  544.3 1.1 fusion.40
  545.5 2.2 convolution_convert_fusion.6
  547.8 2.6 fusion.15
  550.4 0.3 copy.62
  550.7 3.3 fusion.6.kv_ref
  554.0 166.2 %scatter_all.1 = (f32[256,512]{1,0:T(8,128)}, f32[256,512]{1,0:T(8,128)}, f32[64,640]{1,0:T(8,128)}, f32[256,1408]{1,0:T(8,128)}, f32[256,1408]{1,0:T(8,128)}, /...) custom-call(bf16[2048,2048]{1,0:T(8,128)(2,1)} %convolution_convert_, ...), custom_call_target="tpu_custom_call" | custom-call | tf_op jit(solution)/shard_map/scatter_all/pallas_call | solution.py:715
  720.2 1.6 slice.106
  721.7 1.5 slice_reduce_fusion
  723.3 3.9 fusion.19
  727.2 1.0 copy.73
  728.2 0.8 copy.74
  729.0 0.8 copy.75
  729.8 1.1 copy.76
  730.9 1.1 copy.77
  732.0 1.1 copy.78
  (119 shorter events, 2.3 us)
Async XLA Ops:
  7.2 178.1 %copy-start.11 = (bf16[256,2048]{1,0:T(8,128)(2,1)S(1)}, bf16[256,2048]{1,0:T(8,128)(2,1)}, u32[]{:S(2)}) copy-start(bf16[256,2048]{1,0:T(8,128)(2,1)} %param.11) | copy-start | bytes 3145732
  7.2 178.1 %copy-start.25 = (f32[2048]{0:T(1024)S(1)}, f32[2048]{0:T(1024)}, u32[]{:S(2)}) copy-start(f32[2048]{0:T(1024)} %param.13) | copy-start | bytes 24580
  7.2 211.8 %all-gather.3.cloned.1.call-start = ((), (), s32[]{:S(2)}) async-start(), calls=%async_computation.2 | async-start | bytes 1310720 | tf_op jit(solution)/shard_map/all_gather | solution.py:749
  185.3 2.4 copy-start.27
  190.4 151.6 %all-gather.5.cloned.1.call-start = ((), (), s32[]{:S(2)}) async-start(), calls=%async_computation.3 | async-start | bytes 5242880 | tf_op jit(solution)/shard_map/all_gather | solution.py:749
  222.6 0.8 copy-start.2
  227.6 1.2 copy-start
  228.8 1.0 copy-start.1
  229.8 22.8 %copy-start.12 = (bf16[256,2048]{1,0:T(8,128)(2,1)S(1)}, bf16[256,2048]{1,0:T(8,128)(2,1)}, u32[]{:S(2)}) copy-start(bf16[256,2048]{1,0:T(8,128)(2,1)} %param.11) | copy-start | bytes 3145732
  252.7 6.3 copy-start.5
  252.7 7.6 %copy-start.26 = (f32[2048]{0:T(1024)S(1)}, f32[2048]{0:T(1024)}, u32[]{:S(2)}) copy-start(f32[2048]{0:T(1024)} %param.17) | copy-start | bytes 24580
  259.0 1.4 copy-start.7
  261.6 203.8 %reduce-scatter.3.cloned.1.call-start = ((), (), s32[]{:S(2)}) async-start(), calls=%async_computation.4 | async-start | bytes 5242880 | tf_op jit(solution)/shard_map/reduce_scatter | solution.py:752
  342.0 11.8 %copy-start.29 = (bf16[1024,2048]{1,0:T(8,128)(2,1)S(1)}, bf16[1024,2048]{1,0:T(8,128)(2,1)}, u32[]{:S(2)}) copy-start(bf16[1024,2048]{1,0:T(8,128)(2,1)} %all-gather.5.cloned.1.call-done) | copy-start | bytes 12582916
  342.0 27.0 %slice-start.4 = ((s8[5767168]{0:T(1024)(128)(4,1)}), s8[4194304]{0:T(1024)(128)(4,1)S(1)}, s32[]{:S(2)}) async-start(s8[5767168]{0:T(1024)(128)(4,1)} %bitcast.81), calls=%async_computation.10 | async-start | bytes 8388608
  342.0 37.4 %slice-start.2 = ((s8[5767168]{0:T(1024)(128)(4,1)}), s8[4194304]{0:T(1024)(128)(4,1)S(1)}, s32[]{:S(2)}) async-start(s8[5767168]{0:T(1024)(128)(4,1)} %bitcast.79), calls=%async_computation.8 | async-start | bytes 8388608
  353.8 15.2 %slice-start.5 = ((s8[5767168]{0:T(1024)(128)(4,1)}), s8[1572864]{0:T(1024)(128)(4,1)S(1)}, s32[]{:S(2)}) async-start(s8[5767168]{0:T(1024)(128)(4,1)} %bitcast.81), calls=%async_computation.11 | async-start | bytes 3145728
  353.8 25.6 %slice-start.3 = ((s8[5767168]{0:T(1024)(128)(4,1)}), s8[1572864]{0:T(1024)(128)(4,1)S(1)}, s32[]{:S(2)}) async-start(s8[5767168]{0:T(1024)(128)(4,1)} %bitcast.79), calls=%async_computation.9 | async-start | bytes 3145728
  369.0 10.5 %copy-start.32 = (bf16[1024,1408]{1,0:T(8,128)(2,1)S(1)}, bf16[1024,1408]{1,0:T(8,128)(2,1)}, u32[]{:S(2)}) copy-start(bf16[1024,1408]{1,0:T(8,128)(2,1)} %get-tuple-element.56) | copy-start | bytes 8650756
  389.9 154.3 %reduce-scatter.5.cloned.1.call-start = ((), (), s32[]{:S(2)}) async-start(), calls=%async_computation.5 | async-start | bytes 1310720 | tf_op jit(solution)/shard_map/reduce_scatter | solution.py:752
  390.5 3.4 copy-start.34
  393.9 11.6 %copy-start.28 = (bf16[1024,2048]{1,0:T(8,128)(2,1)S(1)}, bf16[1024,2048]{1,0:T(8,128)(2,1)}, u32[]{:S(2)}) copy-start(bf16[1024,2048]{1,0:T(8,128)(2,1)} %get-tuple-element.33) | copy-start | bytes 12582916
  405.5 8.7 %copy-start.30 = (bf16[1024,2048]{1,0:T(8,128)(2,1)S(1)}, bf16[1024,2048]{1,0:T(8,128)(2,1)}, u32[]{:S(2)}) copy-start(bf16[1024,2048]{1,0:T(8,128)(2,1)} %all-gather.5.cloned.1.call-done) | copy-start | bytes 12582916
  405.5 8.7 %copy-start.33 = (bf16[1024,1408]{1,0:T(8,128)(2,1)S(1)}, bf16[1024,1408]{1,0:T(8,128)(2,1)}, u32[]{:S(2)}) copy-start(bf16[1024,1408]{1,0:T(8,128)(2,1)} %get-tuple-element.56) | copy-start | bytes 8650756
  414.2 8.7 %copy-start.31 = (bf16[1024,1408]{1,0:T(8,128)(2,1)S(1)}, bf16[1024,1408]{1,0:T(8,128)(2,1)}, u32[]{:S(2)}) copy-start(bf16[1024,1408]{1,0:T(8,128)(2,1)} %get-tuple-element.55) | copy-start | bytes 8650756
  465.4 2.8 copy-start.8
  465.4 2.9 copy-start.14
  470.1 6.5 copy-start.9
  470.2 6.5 copy-start.3
  470.2 6.5 copy-start.4
  513.1 3.4 copy-start.17
  516.5 2.1 copy-start.24
  518.5 2.1 copy-start.13
  520.6 5.8 copy-start.6
  520.6 5.8 copy-start.10
  520.7 11.4 %slice-start = ((s8[8388608]{0:T(1024)(128)(4,1)}), s8[4194304]{0:T(1024)(128)(4,1)S(1)}, s32[]{:S(2)}) async-start(s8[8388608]{0:T(1024)(128)(4,1)} %bitcast.77), calls=%async_computation.6 | async-start | bytes 8388608
  526.4 5.7 slice-start.1
  544.3 3.5 copy-start.15
  544.3 3.5 copy-start.16
  723.3 3.9 copy-start.21
  723.3 4.9 copy-start.23
  727.2 1.8 copy-start.22
  727.2 2.6 copy-start.20
  728.2 2.7 copy-start.19
  729.8 2.2 copy-start.18
Sparse Core Ops, SparseCore 0:
  190.5 28.4 all-gather.2
  261.7 80.2 all-gather.4
  390.1 75.2 reduce-scatter.2
  516.6 27.6 reduce-scatter.4

commit v3 on v2

--- a/solution.py
+++ b/solution.py
@@ -722,8 +722,313 @@
             collective_id=1, has_side_effects=True, vmem_limit_bytes=62 * 1024 * 1024
         ),
         name="scatter_all",
-    )(*grads, branch.reshape(n_line, tokens, width), residual)
+    )(*grads, branch, residual)
     return results[:7]
+
+
+def by_tiles(total, size, act):
+    full = total // size
+
+    @pl.loop(0, full)
+    def _(index):
+        act(pl.ds(pl.multiple_of(index * size, size), size))
+
+    if total % size:
+        act(pl.ds(full * size, total % size))
+
+
+def feed_forward_kernel(
+    normed_ref, gate_w_ref, up_w_ref, down_w_ref, cot_ref,
+    gg_out, gu_out, gd_out, branch_out, dn_out,
+    wg, wu, wd, cot, normed, hid, dg, du, part, arrival, branch_stage, gate_stage, up_stage,
+    load_sem, n_send, n_recv, l_send, l_recv, stage_sem,
+):
+    dp, place = lax.axis_index("dp"), lax.axis_index("tensor")
+    rows, depth = normed_ref.shape
+    low = jnp.bfloat16
+    order = line_order(place)
+    cuts = l_send.shape[1]
+    few = rows // cuts
+    enter(dp, place)
+
+    def remote(src, dst, send, recv, step):
+        return pltpu.make_async_remote_copy(
+            src_ref=src, dst_ref=dst, send_sem=send, recv_sem=recv,
+            device_id=(dp, place + step), device_id_type=MESH,
+        )
+
+    def chunk(rank):
+        return pl.ds(pl.multiple_of(rank * rows, rows), rows)
+
+    def own_copy(step):
+        return remote(
+            normed_ref, normed.at[chunk(place), :], n_send.at[(step + 1) // 2, place],
+            n_recv.at[place], step,
+        )
+
+    def pass_copy(rank, step):
+        ref = normed.at[chunk(rank), :]
+        return remote(ref, ref, n_send.at[(step + 1) // 2, rank], n_recv.at[rank], step)
+
+    loads = [
+        pltpu.make_async_copy(src, dst, load_sem.at[i])
+        for i, (src, dst) in enumerate(
+            (
+                (normed_ref, normed.at[chunk(place), :]),
+                (gate_w_ref, wg),
+                (up_w_ref, wu),
+                (cot_ref, cot),
+                (down_w_ref, wd),
+            )
+        )
+    ]
+
+    @pl.when(place < 3)
+    def _():
+        own_copy(1).start()
+
+    @pl.when(place > 0)
+    def _():
+        own_copy(-1).start()
+
+    for load in loads:
+        load.start()
+    for load in loads:
+        load.wait()
+
+    def sums_copy(rank, cut, slot, step):
+        window = pl.ds(cut * few, few)
+        return remote(
+            part.at[rank, window, :], arrival.at[slot, window, :], l_send.at[rank, cut],
+            l_recv.at[slot, cut], step,
+        )
+
+    def branch_copy(rank):
+        return pltpu.make_async_copy(branch_stage, branch_out.at[rank], stage_sem.at[0])
+
+    def compute(rank):
+        here = chunk(rank)
+
+        def activate(columns):
+            gate = dot_nn(normed[here, :], wg[:, columns])
+            up = dot_nn(normed[here, :], wu[:, columns])
+            d_hidden = dot_nn(cot[here, :], wd[:, columns])
+            sig = 1.0 / (1.0 + jnp.exp(-gate))
+            silu = gate * sig
+            hid[here, columns] = (silu * up).astype(low)
+            dg[here, columns] = (d_hidden * up * sig * (1.0 + gate * (1.0 - sig))).astype(low)
+            du[here, columns] = (d_hidden * silu).astype(low)
+
+        by_tiles(wg.shape[1], 256, activate)
+
+        def pull(columns):
+            part[rank, :, columns] = (
+                dot_nt(dg[here, :], wg[columns, :]) + dot_nt(du[here, :], wu[columns, :])
+            ).astype(low)
+
+        by_tiles(depth, 512, pull)
+
+    def branch(rank):
+        def push(columns):
+            branch_stage[:, columns] = dot_nt(hid[chunk(rank), :], wd[columns, :]).astype(low)
+
+        by_tiles(depth, 512, push)
+        branch_copy(rank).start()
+
+    def take(rank):
+        pass_copy(rank, 1).wait_recv()
+
+        @pl.when((rank < place) & (place < 3))
+        def _():
+            pass_copy(rank, 1).start()
+
+        @pl.when((rank > place) & (place > 0))
+        def _():
+            pass_copy(rank, -1).start()
+
+    @pl.loop(0, 4)
+    def _(turn):
+        rank = jnp.where(
+            turn == 0,
+            place,
+            jnp.where(turn == 1, order[0], jnp.where(turn == 2, order[1], order[2])),
+        )
+
+        inside = (place == 1) | (place == 2)
+
+        @pl.when(turn == 1)
+        def _():
+            take(order[0])
+
+            @pl.when(inside)
+            def _():
+                take(order[1])
+
+        @pl.when((turn == 2) & (place != 1) & (place != 2))
+        def _():
+            take(order[1])
+
+        @pl.when(turn == 3)
+        def _():
+            take(order[2])
+
+        compute(rank)
+
+        @pl.when((turn > 0) & (place == 3))
+        def _():
+            for cut in range(cuts):
+                sums_copy(rank, cut, rank, -1).start()
+
+        @pl.when((turn > 0) & (place == 0))
+        def _():
+            slot = jnp.where(rank == 1, 4, rank)
+            for cut in range(cuts):
+                sums_copy(rank, cut, slot, 1).start()
+
+        @pl.when(turn > 0)
+        def _():
+            branch_copy(rank).wait()
+
+        branch(rank)
+
+    branch_copy(0).wait()
+
+    def gate_copy(tile):
+        return pltpu.make_async_copy(gate_stage, gg_out.at[tile, :], stage_sem.at[1])
+
+    def up_copy(tile):
+        return pltpu.make_async_copy(up_stage, gu_out.at[tile, :], stage_sem.at[2])
+
+    def down_copy(tile):
+        return pltpu.make_async_copy(gate_stage, gd_out.at[tile, :], stage_sem.at[1])
+
+    size = gate_stage.shape[0]
+
+    @pl.loop(0, depth // size)
+    def _(index):
+        tile = pl.ds(pl.multiple_of(index * size, size), size)
+        left = normed[:, tile]
+        gate_grad = dot_tn(left, dg[...]).astype(low)
+
+        @pl.when(index > 0)
+        def _():
+            gate_copy(tile).wait()
+            up_copy(tile).wait()
+
+        gate_stage[...] = gate_grad
+        gate_copy(tile).start()
+        up_stage[...] = dot_tn(left, du[...]).astype(low)
+        up_copy(tile).start()
+
+    last = pl.ds(depth - size, size)
+    gate_copy(last).wait()
+    up_copy(last).wait()
+
+    def relay(rank, slot, step, cut):
+        sums_copy(rank, cut, rank, step).wait_recv()
+        window = pl.ds(cut * few, few)
+        part[rank, window, :] = part[rank, window, :] + arrival[rank, window, :]
+        sums_copy(rank, cut, slot, step).start()
+
+    @pl.when((place == 1) | (place == 2))
+    def _():
+        outward = 3 - 2 * place
+        for cut in range(cuts):
+            relay(3 - place, 4 - 3 * (place - 1), outward, cut)
+        for cut in range(cuts):
+            relay(6 - 3 * place, 6 - 3 * place, outward, cut)
+            relay(3 * (place - 1), 4 * (place - 1), -outward, cut)
+
+    @pl.loop(0, depth // size)
+    def _(index):
+        tile = pl.ds(pl.multiple_of(index * size, size), size)
+        down_grad = dot_tn(cot[:, tile], hid[...]).astype(low)
+
+        @pl.when(index > 0)
+        def _():
+            down_copy(tile).wait()
+
+        gate_stage[...] = down_grad
+        down_copy(tile).start()
+
+    down_copy(last).wait()
+
+    for cut in range(cuts):
+        window = pl.ds(cut * few, few)
+        dn_out[window, :] = part[place, window, :].astype(jnp.float32)
+
+        @pl.when(place < 3)
+        def _():
+            sums_copy(place, cut, place, 1).wait_recv()
+            dn_out[window, :] += arrival[place, window, :].astype(jnp.float32)
+
+        @pl.when(place > 0)
+        def _():
+            sums_copy(place, cut, 4, 1).wait_recv()
+            dn_out[window, :] += arrival[4, window, :].astype(jnp.float32)
+
+    @pl.when(place < 3)
+    def _():
+        own_copy(1).wait_send()
+
+    @pl.when(place > 0)
+    def _():
+        own_copy(-1).wait_send()
+
+    for rank in range(4):
+
+        @pl.when((rank < place) & (place < 3))
+        def _():
+            pass_copy(rank, 1).wait_send()
+
+        @pl.when((rank > place) & (place > 0))
+        def _():
+            pass_copy(rank, -1).wait_send()
+
+        @pl.when(rank != place)
+        def _():
+            for cut in range(cuts):
+                sums_copy(rank, cut, rank, 1).wait_send()
+
+
+def feed_forward(normed, w_gate, w_up, w_down, cotangent):
+    low = jnp.bfloat16
+    rows, depth = normed.shape
+    length = cotangent.shape[0]
+    units = w_gate.shape[1]
+    ranks = length // rows
+    cuts = 4
+    anywhere = pl.BlockSpec(memory_space=pl.ANY)
+    in_vmem = pl.BlockSpec(memory_space=pltpu.VMEM)
+    dma = pltpu.SemaphoreType.DMA
+    flops = 9 * 2 * length * depth * units
+    return pl.pallas_call(
+        feed_forward_kernel,
+        out_shape=[jax.ShapeDtypeStruct((depth, units), low)] * 3
+        + [
+            jax.ShapeDtypeStruct((ranks, rows, depth), low),
+            jax.ShapeDtypeStruct((rows, depth), jnp.float32),
+        ],
+        in_specs=[anywhere] * 5,
+        out_specs=[anywhere] * 4 + [in_vmem],
+        scratch_shapes=[pltpu.VMEM((depth, units), low)] * 3
+        + [pltpu.VMEM((length, depth), low)] * 2
+        + [pltpu.VMEM((length, units), low)] * 3
+        + [
+            pltpu.VMEM((ranks, rows, depth), low),
+            pltpu.VMEM((ranks + 1, rows, depth), low),
+            pltpu.VMEM((rows, depth), low),
+            pltpu.VMEM((256, units), low),
+            pltpu.VMEM((256, units), low),
+            dma((5,)), dma((2, ranks)), dma((ranks,)), dma((ranks, cuts)), dma((ranks + 1, cuts)),
+            dma((3,)),
+        ],
+        compiler_params=pltpu.CompilerParams(
+            collective_id=2, has_side_effects=True, vmem_limit_bytes=62 * 1024 * 1024
+        ),
+        cost_estimate=pl.CostEstimate(flops=flops, bytes_accessed=60 << 20, transcendentals=0),
+        name="feed_forward",
+    )(normed, w_gate, w_up, w_down, cotangent)
 
 
 def local(
@@ -794,22 +1099,27 @@
     residual = token_rows + dot_nt(heads_low, full_output)
 
     normed_mlp, unit_mlp, inverse_mlp = norm_forward(residual, gain_mlp)
-    gathered_mlp = gather(normed_mlp.astype(low), "tensor")
-    gate_act = dot_nn(gathered_mlp, full_gate)
-    up_act = dot_nn(gathered_mlp, full_up)
-    sigmoid_gate = jax.nn.sigmoid(gate_act)
-    silu_gate = gate_act * sigmoid_gate
-    hidden_low = (silu_gate * up_act).astype(low)
-    d_hidden = dot_nn(piece, full_down)
-    d_gate = (d_hidden * up_act * sigmoid_gate * (1.0 + gate_act * (1.0 - sigmoid_gate))).astype(low)
-    d_up = (d_hidden * silu_gate).astype(low)
-    d_normed_mlp = scatter(
-        (dot_nt(d_gate, full_gate) + dot_nt(d_up, full_up)).astype(low), "tensor"
-    ).astype(jnp.float32)
-    branch = dot_nt(hidden_low, full_down).astype(low)
-    grad_down = dot_tn(piece, hidden_low)
-    grad_gate = dot_tn(gathered_mlp, d_gate)
-    grad_up = dot_tn(gathered_mlp, d_up)
+    if by_kernels:
+        grad_gate, grad_up, grad_down, branch, d_normed_mlp = feed_forward(
+            normed_mlp.astype(low), full_gate, full_up, full_down, piece
+        )
+    else:
+        gathered_mlp = gather(normed_mlp.astype(low), "tensor")
+        gate_act = dot_nn(gathered_mlp, full_gate)
+        up_act = dot_nn(gathered_mlp, full_up)
+        sigmoid_gate = jax.nn.sigmoid(gate_act)
+        silu_gate = gate_act * sigmoid_gate
+        hidden_low = (silu_gate * up_act).astype(low)
+        d_hidden = dot_nn(piece, full_down)
+        d_gate = (d_hidden * up_act * sigmoid_gate * (1.0 + gate_act * (1.0 - sigmoid_gate))).astype(low)
+        d_up = (d_hidden * silu_gate).astype(low)
+        d_normed_mlp = scatter(
+            (dot_nt(d_gate, full_gate) + dot_nt(d_up, full_up)).astype(low), "tensor"
+        ).astype(jnp.float32)
+        branch = dot_nt(hidden_low, full_down).astype(low)
+        grad_down = dot_tn(piece, hidden_low)
+        grad_gate = dot_tn(gathered_mlp, d_gate)
+        grad_up = dot_tn(gathered_mlp, d_up)
     d_norm_mlp, gain_mlp_part = norm_backward(d_normed_mlp, unit_mlp, inverse_mlp, gain_mlp)
     d_residual = cotangent.astype(jnp.float32) + d_norm_mlp
 

time: 746 us -> 690 us (0.925)
  Pallas kernels: 396 us -> 534 us
  matrix products: 140 us -> 41.7 us
  waiting for transfers between devices: 127 us -> 33.1 us
    pallas_call x0 -> x1, Pallas kernels: none -> 138 us  [feed_forward(): pl.pallas_call(feed_forward_kernel, out_shape=[jax.ShapeDtypeStruct((dept...]
    all_gather x2 -> x1, waiting for transfers between devices: 85 us -> 19.9 us  [gather(): return lax.all_gather(array, axes, axis=axis, tiled=True)]
    dot_general x6 -> x3, matrix products: 54.6 us -> 15.7 us  [dot_nn(): return jnp.dot(left, right, preferred_element_type=jnp.float32)]
    dot_general x6 -> x3, matrix products: 45.1 us -> 12.5 us  [dot_nt(): lax.dot_general(left, right, (((1,), (1,)), ((), ())), preferred_element_...]
    reduce_scatter x2 -> x1, waiting for transfers between devices: 42.1 us -> 13.2 us  [scatter(): return lax.psum_scatter(array, axes, scatter_dimension=axis, tiled=True)]
    dot_general x6 -> x3, matrix products: 39.9 us -> 13.6 us  [dot_tn(): lax.dot_general(left, right, (((0,), (0,)), ((), ())), preferred_element_...]
  transfers between devices with their start and end apart: 4 -> 2, of which waited for: 4 -> 2; matrix products, arithmetic and copies ran while one was open for 11% -> 4% of each run, Pallas kernels for 0% -> 0%
where the time goes in v3:
time: 690 us; the launch traced here: 683 us
  Pallas kernels  534 us (77%)
  matrix products  41.7 us (6%)
  local copies, waits for them, and re-layouts  33.5 us (5%)
  waiting for transfers between devices  33.1 us (5%)
  other arithmetic  25.2 us (4%)
  between operations  14.9 us (2%)
    pallas_call x1, Pallas kernels, gather_all(): pl.pallas_call(gather_kernel, out_shape=shapes, in_specs=[anywhere] * 7,...  176 us
    pallas_call x1, Pallas kernels, scatter_all(): pl.pallas_call(scatter_kernel, out_shape=out_shape, in_specs=[anywhere] *...  166 us
    pallas_call x1, Pallas kernels, feed_forward(): pl.pallas_call(feed_forward_kernel, out_shape=[jax.ShapeDtypeStruct((dept...  138 us
    pallas_call x1, Pallas kernels, attend_backward(): pl.pallas_call(attend_backward_kernel, grid=(KVH,), in_specs=[columns_of(...  31.1 us
    pallas_call x1, Pallas kernels, attend_forward(): pl.pallas_call(attend_forward_kernel, grid=(KVH,), in_specs=[columns_of(r...  22.8 us
    all_gather x1, waiting for transfers between devices, gather(): return lax.all_gather(array, axes, axis=axis, tiled=True)  19.9 us
    dot_general x3, matrix products, dot_nn(): return jnp.dot(left, right, preferred_element_type=jnp.float32)  15.7 us
  transfers between devices with their start and end apart: 2, of which 2 were waited for; matrix products, arithmetic and copies ran while one was open for 4% of the time, Pallas kernels for 0%

profile of v3, /device:TPU:0, one launch (start us, length us, event | category | flops | bytes accessed | tf_op | source)
XLA Modules:
  0.0 682.5 jit_solution(9372355308991327975)
XLA Ops:
  7.2 1.5 fusion.13
  8.8 176.4 %gather_all.1 = (bf16[2048,512]{1,0:T(8,128)(2,1)}, bf16[2048,2048]{1,0:T(8,128)(2,1)}, bf16[2048,2048]{1,0:T(8,128)(2,1)}, bf16[2048,1408]{1,0:T(8,128)(2,1)}, ...) custom-call(bf16[256,512]{1,0:T(8,128)(2,1)} %kv_ref.1, ...), custom_call_target="tpu_custom_call" | custom-call | tf_op jit(solution)/shard_map/gather_all/pallas_call | solution.py:420
  185.3 2.3 fusion.26
  187.8 0.1 add_select_fusion
  187.8 0.3 reduce-window.9
  188.2 0.1 slice_reduce_fusion.2
  188.4 0.1 copy.47
  188.6 0.1 dynamic-slice_convert_fusion
  188.6 0.2 fusion.21
  188.9 0.1 copy.48
  189.0 0.7 pad_maximum_fusion.2
  189.8 0.1 dynamic_slice.7
  189.9 6.8 %fusion.28 = f32[256,2048]{0,1:T(8,128)S(1)} fusion(bf16[2048,2048]{1,0:T(8,128)(2,1)} %get-tuple-element.34, bf16[256,2048]{1,0:T(8,128)(2,1)S(1)} %copy-done.13, f32[2048]{0:T(1024)S(1)} %copy-done.26, f32[256]{0:T(256)S(1)} %add_rsqrt_fusion.1), kind=kOutput, calls=%fused_computation.75 | convolution fusion | flops 2149580800 | bytes 11543552 | tf_op jit(solution)/shard_map/dot_general | solution.py:66
  196.7 0.3 multiply_subtract_fusion
  197.1 0.3 fusion.14
  197.4 0.9 copy.51.query_ref
  198.2 0.2 fusion.18.bias_ref
  198.5 19.9 %all-gather.2.cloned.1.call-done = bf16[1024,512]{1,0:T(8,128)(2,1)} async-done(((bf16[256,512]{1,0:T(8,128)(2,1)}), bf16[1024,512]{1,0:T(8,128)(2,1)}) %all-gather.2.cloned.1.call-update) | async-done | bytes 1048592 | tf_op jit(solution)/shard_map/all_gather | solution.py:1054
  218.3 2.2 fusion.31
  220.6 1.2 copy.50
  221.8 2.0 copy.49
  223.9 2.4 copy.65
  226.2 1.3 copy.54
  227.5 4.3 fusion.30
  231.9 22.8 %attend_forward.1 = (bf16[256,2048]{1,0:T(8,128)(2,1)S(1)}, f32[4,8,256]{2,1,0:T(8,128)S(1)}) custom-call(bf16[256,2048]{1,0:T(8,128)(2,1)S(1)} %copy.51.query_ref, bf16[4,1024,128]{2,1,0:T(8,128)(2,1)S(1)} %get-tuple-element.86.front_ref.kf_ref, bf16[4,1024,128]{2,1,0:T(8,128)(2,1)S(1)} %get-tuple-element.87.back_ref.kb_ref, ...), custom_call_target="tpu_custom_call" | custom-call | tf_op jit(solution)/shard_map/attend_forward/pallas_call | solution.py:157
  254.8 6.3 multiply_reduce_fusion.2
  261.1 1.3 copy-done.9
  262.4 1.2 multiply_convert_fusion.normed_ref
  263.6 137.5 %feed_forward.1 = (bf16[2048,1408]{1,0:T(8,128)(2,1)}, bf16[2048,1408]{1,0:T(8,128)(2,1)}, bf16[2048,1408]{1,0:T(8,128)(2,1)}, bf16[4,256,2048]{2,1,0:T(8,128)(2,1)}, f32[256,2048]{1,0:T(8,128)}) custom-call(bf16[256,2048]{1,0:T(8,128)(2,1)} %multiply_convert_fusion.normed_ref, bf16[2048,1408]{1,0:T(8,128)(2,1)} %get-tuple-element.38.gate_w_ref, ...), custom_call_target="tpu_custom_call" | custom-call | flops 53150220288 | bytes 62914560 | tf_op jit(solution)/shard_map/feed_forward/pallas_call | solution.py:1005
  401.1 2.9 multiply_reduce_fusion
  404.1 0.5 copy-done.17
  404.6 1.8 multiply_add_fusion
  406.5 6.5 convolution_convert_fusion.3.grad_ref
  413.1 31.1 %attend_backward.1 = (f32[256,2048]{1,0:T(8,128)}, f32[4,1024,128]{2,1,0:T(8,128)}, f32[4,1024,128]{2,1,0:T(8,128)}) custom-call(bf16[256,2048]{1,0:T(8,128)(2,1)S(1)} %copy.51.query_ref, bf16[256,2048]{1,0:T(8,128)(2,1)S(1)} %convolution_convert_fusion.3.grad_ref, bf16[4,1024,128]{2,1,0:T(8,128)(2,1)S(1)} %copy-done.2, bf16[4,1024,128]{2,1,0:T(8,128)(2,1)S(1)} %copy-done.4, ...), custom_call_target="tpu_custom_call" | custom-call | tf_op jit(solution)/shard_map/attend_backward/pallas_call | solution.py:182
  444.1 3.1 copy.58
  447.2 3.0 fusion.15
  450.2 1.1 copy.59
  451.4 0.6 fusion.16
  452.0 0.3 copy.60
  452.3 2.1 pad_maximum_fusion.1
  454.4 2.0 subtract_convert_fusion
  456.4 0.1 pad_maximum_fusion
  456.5 5.7 convolution_convert_fusion.gq_ref
  462.3 5.6 convolution_convert_fusion.1.go_ref
  467.9 3.7 fusion.34
  471.6 13.2 %reduce-scatter.2.cloned.1.call-done = bf16[256,512]{0,1:T(8,128)(2,1)} async-done(((bf16[1024,512]{0,1:T(8,128)(2,1)}), bf16[256,512]{0,1:T(8,128)(2,1)}) %reduce-scatter.2.cloned.1.call-update) | async-done | bytes 262160 | tf_op jit(solution)/shard_map/reduce_scatter | solution.py:1057
  484.9 1.0 fusion.33
  486.0 2.2 convolution_convert_fusion.2
  488.2 0.7 copy-done.19
  488.8 2.5 fusion.8
  491.4 0.3 copy.62
  491.7 3.5 fusion.5.kv_ref
  495.2 166.2 %scatter_all.1 = (f32[256,512]{1,0:T(8,128)}, f32[256,512]{1,0:T(8,128)}, f32[64,640]{1,0:T(8,128)}, f32[256,1408]{1,0:T(8,128)}, f32[256,1408]{1,0:T(8,128)}, /...) custom-call(bf16[2048,2048]{1,0:T(8,128)(2,1)} %convolution_convert_, ...), custom_call_target="tpu_custom_call" | custom-call | tf_op jit(solution)/shard_map/scatter_all/pallas_call | solution.py:715
  661.5 1.5 slice_reduce_fusion
  663.0 1.6 slice.106
  664.6 3.9 fusion.12
  668.5 1.0 copy.73
  669.4 0.4 copy-done.25
  669.8 0.8 copy.74
  670.6 0.8 copy.75
  671.4 1.1 copy.76
  672.5 1.1 copy.77
  673.6 0.8 copy-done.20
  674.4 1.1 copy.78
  (83 shorter events, 0.7 us)
Async XLA Ops:
  7.2 211.2 %all-gather.2.cloned.1.call-start = ((), (), s32[]{:S(2)}) async-start(), calls=%async_computation.1 | async-start | bytes 1310720 | tf_op jit(solution)/shard_map/all_gather | solution.py:1054
  8.8 176.5 %copy-start.13 = (bf16[256,2048]{1,0:T(8,128)(2,1)S(1)}, bf16[256,2048]{1,0:T(8,128)(2,1)}, u32[]{:S(2)}) copy-start(bf16[256,2048]{1,0:T(8,128)(2,1)} %param.11) | copy-start | bytes 3145732
  8.8 176.5 %copy-start.26 = (f32[2048]{0:T(1024)S(1)}, f32[2048]{0:T(1024)}, u32[]{:S(2)}) copy-start(f32[2048]{0:T(1024)} %param.13) | copy-start | bytes 24580
  185.3 2.4 copy-start.28
  189.7 295.1 %reduce-scatter.2.cloned.1.call-start = ((), (), s32[]{:S(2)}) async-start(), calls=%async_computation.2 | async-start | bytes 1310720 | tf_op jit(solution)/shard_map/reduce_scatter | solution.py:1057
  198.5 33.4 %copy-start = (f32[1024,256]{1,0:T(8,128)}, f32[1024,256]{1,0:T(8,128)S(1)}, u32[]{:S(2)}) copy-start(f32[1024,256]{1,0:T(8,128)S(1)} %fusion.18.bias_ref) | copy-start | bytes 3145732
  231.9 22.8 %copy-start.1 = (bf16[4,1024,128]{2,1,0:T(8,128)(2,1)}, bf16[4,1024,128]{2,1,0:T(8,128)(2,1)S(1)}, u32[]{:S(2)}) copy-start(bf16[4,1024,128]{2,1,0:T(8,128)(2,1)S(1)} %get-tuple-element.86.front_ref.kf_ref) | copy-start | bytes 3145732
  231.9 22.8 %copy-start.3 = (bf16[4,1024,128]{2,1,0:T(8,128)(2,1)}, bf16[4,1024,128]{2,1,0:T(8,128)(2,1)S(1)}, u32[]{:S(2)}) copy-start(bf16[4,1024,128]{2,1,0:T(8,128)(2,1)S(1)} %get-tuple-element.87.back_ref.kb_ref) | copy-start | bytes 3145732
  231.9 22.9 %copy-start.14 = (bf16[256,2048]{1,0:T(8,128)(2,1)S(1)}, bf16[256,2048]{1,0:T(8,128)(2,1)}, u32[]{:S(2)}) copy-start(bf16[256,2048]{1,0:T(8,128)(2,1)} %param.11) | copy-start | bytes 3145732
  254.7 6.3 copy-start.7
  254.8 7.6 %copy-start.27 = (f32[2048]{0:T(1024)S(1)}, f32[2048]{0:T(1024)}, u32[]{:S(2)}) copy-start(f32[2048]{0:T(1024)} %param.17) | copy-start | bytes 24580
  261.0 1.4 copy-start.9
  401.1 3.0 copy-start.10
  401.1 3.5 copy-start.17
  406.4 6.6 copy-start.11
  406.5 6.6 copy-start.2
  406.5 6.6 copy-start.4
  406.5 6.6 copy-start.5
  406.5 6.6 copy-start.6
  447.2 4.1 copy-start.16
  454.4 2.1 copy-start.15
  456.5 5.8 copy-start.8
  456.5 5.8 copy-start.12
  456.5 11.4 %slice-start = ((s8[8388608]{0:T(1024)(128)(4,1)}), s8[4194304]{0:T(1024)(128)(4,1)S(1)}, s32[]{:S(2)}) async-start(s8[8388608]{0:T(1024)(128)(4,1)} %bitcast.57), calls=%async_computation.3 | async-start | bytes 8388608
  462.3 5.6 slice-start.1
  485.9 2.3 copy-start.18
  485.9 2.9 copy-start.19
  664.6 3.9 copy-start.23
  668.4 1.3 copy-start.25
  668.4 2.1 copy-start.24
  668.4 2.9 copy-start.22
  670.6 1.9 copy-start.21
  672.5 1.9 copy-start.20
Sparse Core Ops, SparseCore 0:
  189.9 28.4 all-gather.1
  454.5 30.2 reduce-scatter.1

commit v4 on v3

--- a/solution.py
+++ b/solution.py
@@ -239,10 +239,34 @@
     pl.semaphore_wait(barrier, 5 - ends)
 
 
-def gather_kernel(
+def turn(tile, cos, sin):
+    lane = lax.broadcasted_iota(jnp.int32, tile.shape, 1)
+    swapped = jnp.where(
+        lane % HD < HD // 2, pltpu.roll(tile, PAIR - HD // 2, 1), pltpu.roll(tile, HD // 2, 1)
+    )
+    return tile * cos + swapped * sin
+
+
+def head_tiles(keyval, group):
+    columns = slice(group // 2 * PAIR, (group // 2 + 1) * PAIR)
+    tile = keyval[:, columns]
+    values = slice(KVH * HD + columns.start, KVH * HD + columns.stop)
+    if group % 2 == 0:
+        front = front_lanes(tile)
+        keys = (front, pltpu.roll(front, HD, 1))
+    else:
+        back = back_lanes(tile)
+        keys = (pltpu.roll(back, HD, 1), back)
+    return keys, keyval[:, values]
+
+
+def attend_kernel(
+    tokens_ref, normed_ref, cos_ref, sin_ref, bias_ref, gain_ref,
     kv_ref, q_ref, o_ref, d_ref, g_ref, u_ref, c_ref,
+    query_out, keyval_out, heads_out, log_out, residual_out, mlp_out,
     fkv, fq, fo, fd, fg, fu, fc,
-    own_sem, z_send, z_recv, p_send, p_recv,
+    kv_weight, weight, wide_weight, keyval, key_f, key_b, value_t,
+    own_sem, z_send, z_recv, p_send, p_recv, k_send, k_recv, w_sem,
 ):
     dp, place = lax.axis_index("dp"), lax.axis_index("tensor")
     rows = kv_ref.shape[0]
@@ -361,17 +385,118 @@
         plane_copy(index, 3).wait_recv()
         plane_copy(index, 7).start()
 
-    def plane_last(index):
+    def plane_ready(index):
         for lane in range(4, 8):
             plane_copy(index, lane).wait_recv()
+
+    def plane_sent(index):
         for lane in range(8):
             plane_copy(index, lane).wait_send()
+
+    def keyval_block(rank):
+        return keyval.at[rows_of(rank), :]
+
+    def keyval_copy(rank, step):
+        side = 0 if step < 0 else 1
+        return remote(
+            keyval_block(rank), keyval_block(rank), k_send.at[side, rank], k_recv.at[rank],
+            (dp, place + step),
+        )
+
+    def keyval_send(rank, act):
+        @pl.when((rank <= place) & (place < 3))
+        def _():
+            act(keyval_copy(rank, 1))
+
+        @pl.when((rank >= place) & (place > 0))
+        def _():
+            act(keyval_copy(rank, -1))
+
+    def keyval_take(step):
+        keyval_copy(order[step], 1).wait_recv()
+        keyval_send(order[step], start)
+
+    low = jnp.bfloat16
+    wide = KVH * HD
+
+    def make_keyval():
+        load = pltpu.make_async_copy(fkv, kv_weight, w_sem.at[0])
+        load.start()
+        load.wait()
+        made = dot_nn(normed_ref[...], kv_weight[...])
+        for tile in range(wide // PAIR):
+            columns = slice(tile * PAIR, (tile + 1) * PAIR)
+            keyval[rows_of(place), columns] = turn(
+                made[:, columns], cos_ref[...], sin_ref[...]
+            ).astype(low)
+        keyval[rows_of(place), wide:] = made[:, wide:].astype(low)
+        keyval_send(place, start)
+
+    def weight_load(source, rank, by_rows):
+        window = pl.ds(pl.multiple_of(rank * width, width), width)
+        src = source.at[window, :] if by_rows else source.at[:, window]
+        dst = wide_weight.at[rank % 2] if by_rows else weight.at[rank % 2]
+        return pltpu.make_async_copy(src, dst, w_sem.at[rank % 2])
+
+    def make_query():
+        weight_load(fq, 0, False).start()
+        for rank in range(4):
+            if rank < 3:
+                weight_load(fq, rank + 1, False).start()
+            weight_load(fq, rank, False).wait()
+            made = dot_nn(normed_ref[...], weight[rank % 2])
+            for tile in range(width // PAIR):
+                columns = slice(tile * PAIR, (tile + 1) * PAIR)
+                query_out[:, rank * width + tile * PAIR : rank * width + (tile + 1) * PAIR] = (
+                    turn(made[:, columns], cos_ref[...], sin_ref[...]) * (HD**-0.5)
+                ).astype(low)
+
+    def attend(group):
+        key_tile, value_tile = head_tiles(keyval, group)
+        key_f[...], key_b[...] = key_tile
+        side = group % 2
+        value_t[...] = value_tile.T[side * HD : (side + 1) * HD, :]
+        pairs = query_out.shape[1] // PAIR // KVH
+
+        @pl.loop(0, pairs)
+        def _(index):
+            pair = group * pairs + index
+            columns = pl.ds(pl.multiple_of(pair * PAIR, PAIR), PAIR)
+            query = query_out[:, columns]
+            outs, logs = [], []
+            for key_ref in (key_f, key_b):
+                scores = dot_nt(key_ref[...], query) + bias_ref[...]
+                top = jnp.max(scores, axis=0, keepdims=True)
+                expo = jnp.exp(scores - top)
+                total = jnp.sum(expo, axis=0, keepdims=True)
+                outs.append(dot_nn(value_t[...], expo.astype(low)) / total)
+                logs.append(top + jnp.log(total))
+            log_out[pair] = jnp.concatenate(logs, axis=0)
+            heads_out[:, columns] = jnp.concatenate(outs, axis=0).T.astype(low)
+
+    def make_residual():
+        weight_load(fo, 0, True).start()
+        square = jnp.zeros((rows, 1), jnp.float32)
+        for rank in range(4):
+            if rank < 3:
+                weight_load(fo, rank + 1, True).start()
+            weight_load(fo, rank, True).wait()
+            columns = slice(rank * width, (rank + 1) * width)
+            made = tokens_ref[:, columns].astype(jnp.float32) + dot_nt(
+                heads_out[...], wide_weight[rank % 2]
+            )
+            residual_out[:, columns] = made
+            square += jnp.sum(made * made, axis=1, keepdims=True)
+        inverse = lax.rsqrt(square * (1.0 / (4 * width)) + epsilon)
+        for rank in range(4):
+            columns = slice(rank * width, (rank + 1) * width)
+            mlp_out[:, columns] = (
+                residual_out[:, columns] * inverse * gain_ref[:, columns]
+            ).astype(low)
 
     line_send(0, place, start)
     plane_first(0)
     plane_first(1)
-    line_send(1, place, start)
-    line_send(2, place, start)
     count = len(blocks)
     line_of = {2: (0, 0), 3: (0, 1), 4: (0, 2), 6: (1, 0), 7: (1, 1), 8: (1, 2)}
     for index in range(count):
@@ -382,33 +507,77 @@
                 line_copy(which, order[step], 1).wait_recv()
                 line_send(which, order[step], start)
             plane_first(ahead)
-        if ahead in (7, 9, 10):
-            step = (7, 9, 10).index(ahead)
-            line_copy(2, order[step], 1).wait_recv()
-            line_send(2, order[step], start)
+        if index == 0:
+            line_send(1, place, start)
+        if index == 6:
+            line_send(2, place, start)
+        if index >= 9:
+            line_copy(2, order[index - 9], 1).wait_recv()
+            line_send(2, order[index - 9], start)
         plane_second(index)
         if index >= 1:
             plane_third(index - 1)
+        if index == 1:
+            plane_ready(0)
+            own_copies[0].wait()
+            make_keyval()
+        if 2 <= index <= 4:
+            keyval_take(index - 2)
+        if index == 5:
+            for block_index in range(1, 5):
+                plane_ready(block_index)
+            own_copies[1].wait()
+            make_query()
+        if 6 <= index <= 9:
+            attend(index - 6)
+        if index == 10:
+            for block_index in range(5, 9):
+                plane_ready(block_index)
+            own_copies[2].wait()
+            make_residual()
     plane_third(count - 1)
+    for index in range(9, count):
+        plane_ready(index)
     for index in range(count):
-        plane_last(index)
+        plane_sent(index)
     for which in range(3):
         line_send(which, place, wait_send)
         for step in range(3):
             line_send(which, order[step], wait_send)
-    for copy in own_copies:
+    keyval_send(place, wait_send)
+    for step in range(3):
+        keyval_send(order[step], wait_send)
+    for copy in own_copies[3:]:
         copy.wait()
-
-
-def gather_all(w_keyval, w_query, w_output, w_down, w_gate, w_up, cotangent):
+    out_copy = pltpu.make_async_copy(keyval, keyval_out, w_sem.at[0])
+    out_copy.start()
+    out_copy.wait()
+
+
+def attend_all(
+    tokens, normed, cos, sin, bias, gain, w_keyval, w_query, w_output, w_down, w_gate, w_up,
+    cotangent,
+):
     n_dp, n_line = lax.axis_size("dp"), lax.axis_size("tensor")
-
-    def over(array, rows, columns):
-        shape = (array.shape[0] * rows, array.shape[1] * columns)
+    low = jnp.bfloat16
+    rows, depth = tokens.shape
+    length = bias.shape[0]
+    wide = 2 * KVH * HD
+    heads = w_query.shape[1] * n_line // HD
+
+    def over(array, by_rows, by_columns):
+        shape = (array.shape[0] * by_rows, array.shape[1] * by_columns)
         return jax.ShapeDtypeStruct(shape, array.dtype)
 
     anywhere = pl.BlockSpec(memory_space=pl.ANY)
+    in_vmem = pl.BlockSpec(memory_space=pltpu.VMEM)
     shapes = [
+        jax.ShapeDtypeStruct((rows, heads * HD), low),
+        jax.ShapeDtypeStruct((length, wide), low),
+        jax.ShapeDtypeStruct((rows, heads * HD), low),
+        jax.ShapeDtypeStruct((heads // 2, 2, rows), jnp.float32),
+        jax.ShapeDtypeStruct((rows, depth), jnp.float32),
+        jax.ShapeDtypeStruct((rows, depth), low),
         over(w_keyval, n_dp, 1),
         over(w_query, n_dp, n_line),
         over(w_output, n_dp, n_line),
@@ -417,21 +586,31 @@
         over(w_up, n_dp, 1),
         over(cotangent, n_line, 1),
     ]
+    dma = pltpu.SemaphoreType.DMA
     return pl.pallas_call(
-        gather_kernel,
+        attend_kernel,
         out_shape=shapes,
-        in_specs=[anywhere] * 7,
-        out_specs=[anywhere] * 7,
+        in_specs=[in_vmem] * 6 + [anywhere] * 7,
+        out_specs=[in_vmem, anywhere] + [in_vmem] * 4 + [anywhere] * 7,
         scratch_shapes=[
-            pltpu.SemaphoreType.DMA((7,)),
-            pltpu.SemaphoreType.DMA((3, 2, 4)),
-            pltpu.SemaphoreType.DMA((3, 4)),
-            pltpu.SemaphoreType.DMA((12, 8)),
-            pltpu.SemaphoreType.DMA((12, 8)),
+            pltpu.VMEM((depth, wide), low),
+            pltpu.VMEM((2, depth, w_query.shape[1]), low),
+            pltpu.VMEM((2, w_query.shape[1], depth), low),
+            pltpu.VMEM((length, wide), low),
+            pltpu.VMEM((length, PAIR), low),
+            pltpu.VMEM((length, PAIR), low),
+            pltpu.VMEM((HD, length), low),
+            dma((7,)), dma((3, 2, 4)), dma((3, 4)), dma((12, 8)), dma((12, 8)),
+            dma((2, 4)), dma((4,)), dma((2,)),
         ],
-        compiler_params=pltpu.CompilerParams(collective_id=0, has_side_effects=True),
-        name="gather_all",
-    )(w_keyval, w_query, w_output, w_down, w_gate, w_up, cotangent)
+        compiler_params=pltpu.CompilerParams(
+            collective_id=0, has_side_effects=True, vmem_limit_bytes=62 * 1024 * 1024
+        ),
+        name="attend_all",
+    )(
+        tokens, normed, cos, sin, bias, gain, w_keyval, w_query, w_output, w_down, w_gate, w_up,
+        cotangent,
+    )
 
 
 def add_rows(target, source, step=32):
@@ -441,36 +620,46 @@
         target[window, :] = target[window, :] + source[window, :]
 
 
-def scatter_kernel(
-    go_ref, gq_ref, kv_ref, gd_ref, gg_ref, gu_ref, branch_ref, residual_ref,
-    go_out, gq_out, kv_out, gd_out, gg_out, gu_out, layer_out,
-    go_core, gq_core, kv_core, gd_core, gg_core, gu_core,
-    go_part, gq_part, kv_part, gd_part, gg_part, gu_part,
-    go_side, gq_side, kv_side, gd_side, gg_side, gu_side,
-    go_near, gq_near, kv_near, gd_near, gg_near, gu_near,
-    go_line, gq_line, kv_line, layer_line,
-    go_in, gq_in, kv_in, layer_in,
-    held, total_ref,
-    load_sem, core_load, core_send, core_recv, p_send, p_recv, l_send, l_recv, layer_load,
+def over_rows(total_rows, act, step=32):
+    @pl.loop(0, total_rows // step)
+    def _(index):
+        act(pl.ds(pl.multiple_of(index * step, step), step))
+
+
+def reach_back_kernel(
+    gd_ref, gg_ref, gu_ref, branch_ref, fkv, fq, fo, dn_ref, residual_ref,
+    cot_ref, tokens_ref, normed_ref, query_ref, heads_ref, keyval_ref, log_ref, bias_ref,
+    cos_ref, sin_ref, gain_attn_ref, gain_mlp_ref,
+    gd_out, gg_out, gu_out, go_out, gq_out, nar_out, layer_out, tokens_out,
+    gd_core, gg_core, gu_core, go_core, gq_core, nar_core,
+    gd_side, gg_side, gu_side, go_side, gq_side, nar_side,
+    gd_near, gg_near, gu_near, go_near, gq_near, nar_near,
+    go_in, gq_in, nar_in, dkv_in, layer_in,
+    parts, held, stage, go_line, gq_line, nar_line, dkv_line, layer_line,
+    d_residual, total, wide, d_branch, d_heads, dq_low, dkv_low, gains, weight, kv_weight,
+    key_f, key_b, key_t, value_f, value_b, dk, dv,
+    load_sem, fetch_sem, core_send, core_recv, p_send, p_recv, l_send, l_recv, in_sem, w_sem,
 ):
     dp, place = lax.axis_index("dp"), lax.axis_index("tensor")
-    rows = go_part.shape[1]
+    low = jnp.bfloat16
+    rows, depth = d_branch.shape
     half = rows // 2
     enter(dp, place)
     x, y, core = flip(dp, 2), flip(dp, 4), flip(dp, 1)
     far = flip(x, 4)
     mine = (dp, x, y, far)
     theirs = tuple(flip(owner, 1) for owner in mine)
-    grads = (go_ref, gq_ref, kv_ref, gd_ref, gg_ref, gu_ref)
-    outs = (go_out, gq_out, kv_out, gd_out, gg_out, gu_out)
-    cores = (go_core, gq_core, kv_core, gd_core, gg_core, gu_core)
-    parts = (go_part, gq_part, kv_part, gd_part, gg_part, gu_part)
-    sides = (go_side, gq_side, kv_side, gd_side, gg_side, gu_side)
-    nears = (go_near, gq_near, kv_near, gd_near, gg_near, gu_near)
-    lines = (go_line, gq_line, kv_line, layer_line)
-    arrivals = (go_in, gq_in, kv_in, layer_in)
-    count = len(grads)
+    grads = (gd_ref, gg_ref, gu_ref)
+    outs = (gd_out, gg_out, gu_out, go_out, gq_out, nar_out)
+    cores = (gd_core, gg_core, gu_core, go_core, gq_core, nar_core)
+    sides = (gd_side, gg_side, gu_side, go_side, gq_side, nar_side)
+    nears = (gd_near, gg_near, gu_near, go_near, gq_near, nar_near)
+    lines = {3: go_line, 4: gq_line, 5: nar_line, 6: dkv_line, 7: layer_line}
+    arrivals = {3: go_in, 4: gq_in, 5: nar_in, 6: dkv_in, 7: layer_in}
     front, back = pl.ds(0, half), pl.ds(half, half)
+    ranks = dkv_line.shape[0]
+    last = ranks - 1
+    turns = (3, 1, 2, 0)
 
     def rows_of(owner):
         return pl.ds(pl.multiple_of(owner * rows, rows), rows)
@@ -481,249 +670,540 @@
             device_id=device, device_id_type=MESH,
         )
 
+    def width_of(i):
+        return cores[i].shape[2]
+
+    def part(i, k):
+        return parts.at[i % 2, k, :, pl.ds(0, width_of(i))]
+
+    def half_part(i, k, window):
+        return parts.at[i % 2, k, window, pl.ds(0, width_of(i))]
+
+    def held_part(slot, count, width):
+        return held.at[slot, pl.ds(0, count), pl.ds(0, width)]
+
+    def fetch(src, slot):
+        return pltpu.make_async_copy(
+            src, held_part(slot, src.shape[0], src.shape[1]), fetch_sem.at[slot]
+        )
+
     def core_copy(i, k):
+        if i < 3:
+            src = grads[i].at[rows_of(theirs[k]), :]
+        else:
+            src = stage.at[turns.index(k) % 2, :, pl.ds(0, width_of(i))]
         return remote(
-            grads[i].at[rows_of(theirs[k]), :], cores[i].at[k],
-            core_send.at[i, k], core_recv.at[i, k], (core, place),
+            src, cores[i].at[k], core_send.at[i, k], core_recv.at[i, k], (core, place)
         )
 
     def own_load(i, k):
         return pltpu.make_async_copy(
-            grads[i].at[rows_of(mine[k]), :], parts[i].at[k], load_sem.at[i, k]
-        )
-
-    def core_fetch(i, k):
-        width = grads[i].shape[1]
-        return pltpu.make_async_copy(
-            cores[i].at[k], held.at[k, :, pl.ds(0, width)], core_load.at[k]
+            grads[i].at[rows_of(mine[k]), :], part(i, k), load_sem.at[i, k]
         )
 
     def plane_copy(i, lane):
-        part = parts[i]
         src, dst, device = (
-            (part.at[3, front, :], sides[i].at[0], y),
-            (part.at[3, back, :], sides[i].at[1], x),
-            (part.at[1, back, :], nears[i].at[0, back, :], x),
-            (part.at[2, front, :], nears[i].at[1, front, :], y),
-            (part.at[1, front, :], nears[i].at[0, front, :], x),
-            (part.at[2, back, :], nears[i].at[1, back, :], y),
+            (half_part(i, 3, front), sides[i].at[0], y),
+            (half_part(i, 3, back), sides[i].at[1], x),
+            (half_part(i, 1, back), nears[i].at[0, back, :], x),
+            (half_part(i, 2, front), nears[i].at[1, front, :], y),
+            (half_part(i, 1, front), nears[i].at[0, front, :], x),
+            (half_part(i, 2, back), nears[i].at[1, back, :], y),
         )[lane]
         return remote(src, dst, p_send.at[i, lane], p_recv.at[i, lane], (device, place))
 
+    def plane_sent(i):
+        for lane in range(6):
+            plane_copy(i, lane).wait_send()
+
+    def load_own(i):
+        for k in turns:
+            own_load(i, k).start()
+
     def stage_core(i):
-        width = grads[i].shape[1]
-        for k in (3, 1, 2, 0):
-            core_copy(i, k).wait_recv()
-            core_fetch(i, k).start()
-        for k in (3, 1, 2, 0):
-            core_fetch(i, k).wait()
-            own_load(i, k).wait()
-            add_rows(parts[i].at[k], held.at[k, :, pl.ds(0, width)])
+        def begin(n):
+            core_copy(i, turns[n]).wait_recv()
+            fetch(cores[i].at[turns[n]], n % 2).start()
+
+        begin(0)
+        begin(1)
+        for n, k in enumerate(turns):
+            fetch(cores[i].at[k], n % 2).wait()
+            if i < 3:
+                own_load(i, k).wait()
+            add_rows(part(i, k), held_part(n % 2, rows, width_of(i)))
             for lane in ((), (2,), (3,), (0, 1))[k]:
                 plane_copy(i, lane).start()
+            if n + 2 < 4:
+                begin(n + 2)
 
     def stage_side(i):
-        plane_copy(i, 0).wait_recv()
-        add_rows(parts[i].at[1, front, :], sides[i].at[0])
-        plane_copy(i, 4).start()
-        plane_copy(i, 1).wait_recv()
-        add_rows(parts[i].at[2, back, :], sides[i].at[1])
-        plane_copy(i, 5).start()
+        for side in range(2):
+            plane_copy(i, side).wait_recv()
+            fetch(sides[i].at[side], side).start()
+        for side, (k, window, lane) in enumerate(((1, front, 4), (2, back, 5))):
+            fetch(sides[i].at[side], side).wait()
+            add_rows(half_part(i, k, window), held_part(side, half, width_of(i)))
+            plane_copy(i, lane).start()
 
     def stage_near(i):
-        for lane in (2, 3, 4, 5):
-            plane_copy(i, lane).wait_recv()
-        part, near, out = parts[i], nears[i], outs[i]
+        for side, lanes in enumerate(((2, 4), (3, 5))):
+            for lane in lanes:
+                plane_copy(i, lane).wait_recv()
+            fetch(nears[i].at[side], side).start()
+        for side in range(2):
+            fetch(nears[i].at[side], side).wait()
+        own, width, out = part(i, 0), width_of(i), outs[i]
 
         @pl.loop(0, rows // 32)
         def _(index):
             window = pl.ds(pl.multiple_of(index * 32, 32), 32)
-            total = (
-                part[0, window, :].astype(jnp.float32)
-                + near[0, window, :].astype(jnp.float32)
-                + near[1, window, :].astype(jnp.float32)
+            sums = (
+                own[window, :].astype(jnp.float32)
+                + held[0, window, pl.ds(0, width)].astype(jnp.float32)
+                + held[1, window, pl.ds(0, width)].astype(jnp.float32)
             )
-            if i >= 3:
-                out[window, :] = total
-            elif i < 2:
-                width = lines[i].shape[2]
-                for rank in range(4):
-                    lines[i][rank, window, :] = total[:, rank * width : (rank + 1) * width].astype(
-                        jnp.bfloat16
+            if i < 3:
+                out[window, :] = sums
+            elif i < 5:
+                piece = width // ranks
+                for rank in range(ranks):
+                    lines[i][rank, window, :] = sums[:, rank * piece : (rank + 1) * piece].astype(
+                        low
                     )
             else:
-                per = rows // 4
+                per = rows // ranks
                 lines[i][index * 32 // per, pl.ds(pl.multiple_of(index * 32 % per, 32), 32), :] = (
-                    total.astype(jnp.bfloat16)
+                    sums.astype(low)
                 )
 
     def line_copy(i, rank, slot, step):
+        src = lines[i].at[(step + 1) // 2] if i == 7 else lines[i].at[rank]
         return remote(
-            lines[i].at[rank], arrivals[i].at[slot], l_send.at[i, rank], l_recv.at[i, slot],
+            src, arrivals[i].at[slot], l_send.at[i - 3, rank], l_recv.at[i - 3, slot],
             (dp, place + step),
         )
 
-    def line_step(i, step):
-        down, up = place - 3 + step, place + 3 - step
+    def line_add(i, ref, slot, step):
+        line_copy(i, slot, slot, step).wait_recv()
+        copy = fetch(arrivals[i].at[slot], 0)
+        copy.start()
+        copy.wait()
+        add_rows(ref, held_part(0, ref.shape[0], ref.shape[1]))
+
+    def line_own(i, rank, step):
+        if i != 7:
+            return lines[i].at[rank]
+        ref = lines[i].at[(step + 1) // 2]
+        copy = pltpu.make_async_copy(branch_ref.at[rank], ref, in_sem.at[0])
+        copy.start()
+        copy.wait()
+        return ref
+
+    def line_step(i, turn):
+        down, up = place - last + turn, place + last - turn
 
         @pl.when(down >= 0)
         def _():
-            @pl.when(place < 3)
+            if i == 7 and turn > 0:
+
+                @pl.when(down > 0)
+                def _():
+                    line_copy(i, down - 1, down - 1, -1).wait_send()
+
+            ref = line_own(i, down, -1)
+
+            @pl.when(place < last)
             def _():
-                line_copy(i, down, down, -1).wait_recv()
-                add_rows(lines[i].at[down], arrivals[i].at[down])
+                line_add(i, ref, down, -1)
 
             line_copy(i, down, down, -1).start()
 
-        @pl.when(up <= 3)
-        def _():
+        @pl.when(up <= last)
+        def _():
+            if i == 7 and turn > 0:
+
+                @pl.when(up < last)
+                def _():
+                    line_copy(i, up + 1, up + 1, 1).wait_send()
+
+            ref = line_own(i, up, 1)
+
             @pl.when(place > 0)
             def _():
-                line_copy(i, up, up, 1).wait_recv()
-                add_rows(lines[i].at[up], arrivals[i].at[up])
-
-            line_copy(i, up, 4 if step == 2 else up, 1).start()
-
-    def line_last(i, begin, add, finish):
-        begin(lines[i].at[place])
-
-        @pl.when(place < 3)
+                line_add(i, ref, up, 1)
+
+            line_copy(i, up, ranks if turn == last - 1 else up, 1).start()
+
+    def line_last(i, add):
+        @pl.when(place < last)
         def _():
             line_copy(i, place, place, 1).wait_recv()
-            add(arrivals[i].at[place])
+            copy = fetch(arrivals[i].at[place], 0)
+            copy.start()
+            copy.wait()
+            add()
 
         @pl.when(place > 0)
         def _():
-            line_copy(i, place, 4, 1).wait_recv()
-            add(arrivals[i].at[4])
-
-        finish()
+            line_copy(i, place, ranks, 1).wait_recv()
+            copy = fetch(arrivals[i].at[ranks], 0)
+            copy.start()
+            copy.wait()
+            add()
 
     def line_sent(i):
-        for rank in range(4):
-
-            @pl.when(rank != place)
-            def _():
-                line_copy(i, rank, rank, 1).wait_send()
-
-    def by_rows(total_rows, act):
-        @pl.loop(0, total_rows // 32)
-        def _(index):
-            act(pl.ds(pl.multiple_of(index * 32, 32), 32))
+        for rank in range(ranks):
+            if i == 7:
+
+                @pl.when((rank == place - 1) | (rank == place + 1))
+                def _():
+                    line_copy(i, rank, rank, 1).wait_send()
+
+            else:
+
+                @pl.when(rank != place)
+                def _():
+                    line_copy(i, rank, rank, 1).wait_send()
 
     def line_out(i):
         out = outs[i]
-        size = out.shape[0]
-
-        def begin(ref):
+        count, width = out.shape
+
+        def begin(window):
+            out[window, :] = lines[i][place, window, :].astype(jnp.float32)
+
+        def add():
             def act(window):
-                out[window, :] = ref[window, :].astype(jnp.float32)
-
-            by_rows(size, act)
-
-        def add(ref):
+                out[window, :] += held[0, window, pl.ds(0, width)].astype(jnp.float32)
+
+            over_rows(count, act)
+
+        over_rows(count, begin)
+        line_last(i, add)
+
+    def norm_back(grad_ref, rows_ref, gain_ref, gain_row, act):
+        gains[gain_row : gain_row + 1, :] = jnp.zeros((1, depth), jnp.float32)
+
+        def block(window):
+            values = rows_ref[window, :].astype(jnp.float32)
+            inverse = lax.rsqrt(jnp.mean(values * values, axis=1, keepdims=True) + epsilon)
+            unit = values * inverse
+            grad = grad_ref[window, :]
+            gains[gain_row : gain_row + 1, :] += jnp.sum(grad * unit, axis=0, keepdims=True)
+            d_unit = grad * gain_ref[...]
+            act(
+                window,
+                inverse * (d_unit - unit * jnp.mean(d_unit * unit, axis=1, keepdims=True)),
+            )
+
+        over_rows(rows, block, 64)
+
+    def after_mlp(window, d_values):
+        made = cot_ref[window, :].astype(jnp.float32) + d_values
+        d_residual[window, :] = made
+        d_branch[window, :] = made.astype(low)
+
+    def after_attn(window, d_values):
+        tokens_out[window, :] = (d_residual[window, :] + d_values).astype(low)
+
+    def square_tile(left, right, owner):
+        columns = pl.ds(pl.multiple_of(owner * rows, rows), rows)
+        return dot_tn(left[:, columns], right[...]).astype(low)
+
+    def narrow_tile(owner):
+        columns = pl.ds(pl.multiple_of(owner * rows, rows), rows)
+        keys = dot_tn(normed_ref[:, columns], dkv_low[...]).astype(low)
+        line = lax.broadcasted_iota(jnp.int32, (PAIR, rows), 0)
+        both = jnp.where(
+            line == 0, gains[0:1, columns], jnp.where(line == 1, gains[1:2, columns], 0.0)
+        )
+        return jnp.concatenate([keys, both.T.astype(low)], axis=1)
+
+    def send_theirs(i, tile):
+        for n, k in enumerate(turns):
+            if n >= 2:
+                core_copy(i, turns[n - 2]).wait_send()
+            stage[n % 2, :, pl.ds(0, width_of(i))] = tile(theirs[k])
+            core_copy(i, k).start()
+
+    def theirs_sent(i):
+        for k in turns[2:]:
+            core_copy(i, k).wait_send()
+
+    def keep_mine(i, tile):
+        for k in turns:
+            parts[i % 2, k, :, pl.ds(0, width_of(i))] = tile(mine[k])
+
+    def go_tile(owner):
+        return square_tile(d_branch, heads_ref, owner)
+
+    def gq_tile(owner):
+        return square_tile(normed_ref, dq_low, owner)
+
+    size = weight.shape[1]
+    steps = depth // size
+
+    def weight_load(source, index):
+        return pltpu.make_async_copy(
+            source.at[pl.ds(index * size, size), :], weight.at[index % 2], w_sem.at[index % 2]
+        )
+
+    def make_d_heads():
+        weight_load(fo, 0).start()
+        for index in range(steps):
+            if index + 1 < steps:
+                weight_load(fo, index + 1).start()
+            weight_load(fo, index).wait()
+            made = dot_nn(d_branch[:, index * size : (index + 1) * size], weight[index % 2])
+            if index == 0:
+                wide[...] = made
+            elif index + 1 < steps:
+                wide[...] += made
+            else:
+                d_heads[...] = (wide[...] + made).astype(low)
+
+    def make_d_normed():
+        weight_load(fq, 0).start()
+        for index in range(steps):
+            if index + 1 < steps:
+                weight_load(fq, index + 1).start()
+            weight_load(fq, index).wait()
+            wide[:, index * size : (index + 1) * size] = dot_nt(
+                dq_low[...], weight[index % 2]
+            ) + dot_nt(dkv_low[...], kv_weight[index * size : (index + 1) * size, :])
+
+    def attend_back(group):
+        (key_f[...], key_b[...]), value_tile = head_tiles(keyval_ref, group)
+        side = group % 2
+        lane_side = slice(side * HD, (side + 1) * HD)
+        tile_columns = slice(group // 2 * PAIR, (group // 2 + 1) * PAIR)
+        key_t[...] = keyval_ref[:, tile_columns].T[lane_side, :]
+        if side == 0:
+            kept = front_lanes(value_tile)
+            value_f[...], value_b[...] = kept, pltpu.roll(kept, HD, 1)
+        else:
+            kept = back_lanes(value_tile)
+            value_f[...], value_b[...] = pltpu.roll(kept, HD, 1), kept
+        dk[...] = jnp.zeros(dk.shape, jnp.float32)
+        dv[...] = jnp.zeros(dv.shape, jnp.float32)
+        pairs = query_ref.shape[1] // PAIR // KVH
+
+        @pl.loop(0, pairs)
+        def _(index):
+            pair = group * pairs + index
+            columns = pl.ds(pl.multiple_of(pair * PAIR, PAIR), PAIR)
+            query, grad = query_ref[:, columns], d_heads[:, columns]
+            logs = log_ref[pair]
+            made = []
+            for number, (key_ref, value_ref, keep) in enumerate(
+                ((key_f, value_f, front_lanes), (key_b, value_b, back_lanes))
+            ):
+                probs = jnp.exp(
+                    dot_nt(key_ref[...], query) + bias_ref[...] - logs[number : number + 1, :]
+                )
+                d_probs = dot_nt(value_ref[...], grad)
+                row_dot = jnp.sum(probs * d_probs, axis=0, keepdims=True)
+                d_scores = (probs * (d_probs - row_dot)).astype(low)
+                dk[...] += dot_nn(d_scores, keep(query))
+                dv[...] += dot_nn(probs.astype(low), keep(grad))
+                made.append(dot_nn(key_t[...], d_scores))
+            dq = jnp.concatenate(made, axis=0).T * (HD**-0.5)
+            dq_low[:, columns] = turn(dq, cos_ref[...], -sin_ref[...]).astype(low)
+
+        for sums, first in ((dk, 0), (dv, KVH * HD)):
+            joined = (sums[...] + pltpu.roll(sums[...], HD, 1)).astype(low)
+            columns = slice(first + tile_columns.start, first + tile_columns.stop)
+            for rank in range(ranks):
+                block = joined[rank * rows : (rank + 1) * rows, :]
+                if side == 1:
+                    block = front_lanes(dkv_line[rank, :, columns]) + back_lanes(block)
+                dkv_line[rank, :, columns] = block
+
+    def make_dkv():
+        wide_columns = dkv_line.shape[2]
+
+        def begin(window):
+            wide[window, pl.ds(0, wide_columns)] = dkv_line[place, window, :].astype(jnp.float32)
+
+        def add():
             def act(window):
-                out[window, :] += ref[window, :].astype(jnp.float32)
-
-            by_rows(size, act)
-
-        line_last(i, begin, add, lambda: None)
-
-    branch_load = pltpu.make_async_copy(branch_ref, layer_line, layer_load)
-    branch_load.start()
-    for i in range(count):
-        for k in (3, 1, 2, 0):
+                wide[window, pl.ds(0, wide_columns)] += held[
+                    0, window, pl.ds(0, wide_columns)
+                ].astype(jnp.float32)
+
+            over_rows(rows, act)
+
+        over_rows(rows, begin)
+        line_last(6, add)
+        for tile in range(wide_columns // PAIR):
+            columns = slice(tile * PAIR, (tile + 1) * PAIR)
+            made = wide[:, columns]
+            if tile < KVH * HD // PAIR:
+                made = turn(made, cos_ref[...], -sin_ref[...])
+            dkv_low[:, columns] = made.astype(low)
+
+    def finish_layer():
+        line_sent(7)
+        own = line_own(7, place, -1)
+
+        def begin(window):
+            total[window, :] += own[window, :].astype(jnp.float32)
+
+        def add():
+            def act(window):
+                total[window, :] += held[0, window, :].astype(jnp.float32)
+
+            over_rows(rows, act)
+
+        def end(window):
+            layer_out[window, :] = total[window, :].astype(low)
+
+        over_rows(rows, begin)
+        line_last(7, add)
+        over_rows(rows, end)
+
+    dn_load = pltpu.make_async_copy(dn_ref, wide, in_sem.at[1])
+    total_load = pltpu.make_async_copy(residual_ref, total, in_sem.at[2])
+    kv_load = pltpu.make_async_copy(fkv, kv_weight, in_sem.at[3])
+    for i in range(3):
+        for k in turns:
             core_copy(i, k).start()
-            own_load(i, k).start()
-    branch_load.wait()
+    for load in (dn_load, total_load, kv_load):
+        load.start()
+    load_own(0)
+    load_own(1)
+    line_step(7, 0)
+    dn_load.wait()
+    total_load.wait()
+    norm_back(wide, total, gain_mlp_ref, 1, after_mlp)
+    stage_core(0)
+    send_theirs(3, go_tile)
+    stage_core(1)
+    make_d_heads()
+    stage_side(0)
+    line_step(7, 1)
+    attend_back(0)
+    stage_near(0)
+    plane_sent(0)
+    load_own(2)
+    stage_side(1)
+    attend_back(1)
+    stage_core(2)
+    stage_near(1)
+    plane_sent(1)
+    keep_mine(3, go_tile)
+    stage_core(3)
+    line_step(7, 2)
+    attend_back(2)
+    stage_side(2)
+    attend_back(3)
+    theirs_sent(3)
+    send_theirs(4, gq_tile)
+    line_step(6, 0)
+    stage_near(2)
+    plane_sent(2)
+    keep_mine(4, gq_tile)
+    stage_side(3)
+    stage_core(4)
+    line_step(6, 1)
+    stage_near(3)
+    plane_sent(3)
+    line_step(6, 2)
     line_step(3, 0)
-    for i in range(count + 2):
-        if i < count:
-            stage_core(i)
-        if 1 <= i <= count:
-            stage_side(i - 1)
-        if i >= 2:
-            stage_near(i - 2)
-        for j in range(3):
-            if 0 <= i - 2 - j < 3:
-                line_step(j, i - 2 - j)
-        if i in (2, 4):
-            line_step(3, i // 2)
-    for j in range(3):
-        line_out(j)
-
-    def layer_begin(ref):
-        def act(window):
-            total_ref[window, :] = residual_ref[window, :] + ref[window, :].astype(jnp.float32)
-
-        by_rows(rows, act)
-
-    def layer_add(ref):
-        def act(window):
-            total_ref[window, :] += ref[window, :].astype(jnp.float32)
-
-        by_rows(rows, act)
-
-    def layer_finish():
-        def act(window):
-            layer_out[window, :] = total_ref[window, :].astype(jnp.bfloat16)
-
-        by_rows(rows, act)
-
-    line_last(3, layer_begin, layer_add, layer_finish)
-    for i in range(count):
-        for k in range(4):
+    kv_load.wait()
+    make_dkv()
+    make_d_normed()
+    norm_back(wide, tokens_ref, gain_attn_ref, 0, after_attn)
+    theirs_sent(4)
+    send_theirs(5, narrow_tile)
+    keep_mine(5, narrow_tile)
+    stage_side(4)
+    line_step(3, 1)
+    stage_core(5)
+    line_step(3, 2)
+    stage_near(4)
+    line_step(4, 0)
+    stage_side(5)
+    finish_layer()
+    line_step(4, 1)
+    stage_near(5)
+    line_step(5, 0)
+    line_step(4, 2)
+    line_step(5, 1)
+    line_out(3)
+    line_step(5, 2)
+    line_out(4)
+    line_out(5)
+    plane_sent(4)
+    plane_sent(5)
+    theirs_sent(5)
+    for i in range(3):
+        for k in turns:
             core_copy(i, k).wait_send()
-        for lane in range(6):
-            plane_copy(i, lane).wait_send()
-    for i in range(4):
+    for i in range(3, 7):
         line_sent(i)
 
 
-def scatter_all(grads, branch, residual):
-    low = jnp.bfloat16
-    n_line = lax.axis_size("tensor")
-    rows = grads[0].shape[0] // lax.axis_size("dp")
+def reach_back(grads, branch, full, d_normed, residual, others):
+    low, wide = jnp.bfloat16, jnp.float32
+    n_dp, ranks = lax.axis_size("dp"), lax.axis_size("tensor")
+    units = grads[0].shape[1]
+    rows, depth = residual.shape
     half = rows // 2
-    widths = [grad.shape[1] for grad in grads]
-    square = widths[0] // n_line
-    few = rows // n_line
-    tokens, width = residual.shape
+    square = depth // ranks
+    few = depth // n_dp // ranks
+    length, keyval = others[5].shape
+    narrow = keyval + PAIR
+    widths = [units] * 3 + [depth, depth, narrow]
     anywhere = pl.BlockSpec(memory_space=pl.ANY)
     in_vmem = pl.BlockSpec(memory_space=pltpu.VMEM)
-    out_shape = [
-        jax.ShapeDtypeStruct((rows, square), jnp.float32),
-        jax.ShapeDtypeStruct((rows, square), jnp.float32),
-        jax.ShapeDtypeStruct((few, widths[2]), jnp.float32),
+    lined = [(rows, square), (rows, square), (few, narrow), (rows, keyval), (rows, depth)]
+    out_shape = [jax.ShapeDtypeStruct((rows, units), wide)] * 3
+    out_shape += [jax.ShapeDtypeStruct((rows, square), wide)] * 2
+    out_shape += [jax.ShapeDtypeStruct((few, narrow), wide)]
+    out_shape += [jax.ShapeDtypeStruct((rows, depth), low)] * 2
+    out_shape += [jax.ShapeDtypeStruct((4, rows, w), low) for w in widths]
+    out_shape += [jax.ShapeDtypeStruct((2, half, w), low) for w in widths]
+    out_shape += [jax.ShapeDtypeStruct((2, rows, w), low) for w in widths]
+    out_shape += [jax.ShapeDtypeStruct((ranks + 1,) + shape, low) for shape in lined]
+    dma = pltpu.SemaphoreType.DMA
+    scratch = [
+        pltpu.VMEM((2, 4, rows, depth), low),
+        pltpu.VMEM((2, rows, depth), low),
+        pltpu.VMEM((2, rows, depth), low),
     ]
-    out_shape += [jax.ShapeDtypeStruct((rows, w), jnp.float32) for w in widths[3:]]
-    out_shape += [jax.ShapeDtypeStruct((tokens, width), low)]
-    out_shape += [jax.ShapeDtypeStruct((4, rows, w), low) for w in widths]
-    scratch = [pltpu.VMEM((4, rows, w), low) for w in widths]
-    scratch += [pltpu.VMEM((2, half, w), low) for w in widths]
-    scratch += [pltpu.VMEM((2, rows, w), low) for w in widths]
-    line_shapes = [(rows, square), (rows, square), (few, widths[2]), (tokens, width)]
-    scratch += [pltpu.VMEM((4,) + shape, low) for shape in line_shapes]
-    scratch += [pltpu.VMEM((5,) + shape, low) for shape in line_shapes]
-    scratch += [pltpu.VMEM((4, rows, max(widths)), low)]
-    scratch += [pltpu.VMEM((tokens, width), jnp.float32)]
-    dma = pltpu.SemaphoreType.DMA
+    scratch += [pltpu.VMEM((ranks,) + shape, low) for shape in lined[:4]]
+    scratch += [pltpu.VMEM((2, rows, depth), low)]
+    scratch += [pltpu.VMEM((rows, depth), wide)] * 3
+    scratch += [pltpu.VMEM((rows, depth), low)] * 3
     scratch += [
-        dma((6, 4)), dma((4,)), dma((6, 4)), dma((6, 4)), dma((6, 6)), dma((6, 6)),
-        dma((4, 4)), dma((4, 5)), dma,
+        pltpu.VMEM((rows, keyval), low),
+        pltpu.VMEM((8, depth), wide),
+        pltpu.VMEM((2, square, depth), low),
+        pltpu.VMEM((depth, keyval), low),
+        pltpu.VMEM((length, PAIR), low),
+        pltpu.VMEM((length, PAIR), low),
+        pltpu.VMEM((HD, length), low),
+        pltpu.VMEM((length, PAIR), low),
+        pltpu.VMEM((length, PAIR), low),
+        pltpu.VMEM((length, PAIR), wide),
+        pltpu.VMEM((length, PAIR), wide),
+        dma((3, 4)), dma((2,)), dma((6, 4)), dma((6, 4)), dma((6, 6)), dma((6, 6)),
+        dma((5, ranks)), dma((5, ranks + 1)), dma((4,)), dma((2,)),
     ]
     results = pl.pallas_call(
-        scatter_kernel,
+        reach_back_kernel,
         out_shape=out_shape,
-        in_specs=[anywhere] * 7 + [in_vmem],
-        out_specs=[in_vmem] * 7 + [anywhere] * 6,
+        in_specs=[anywhere] * 9 + [in_vmem] * 12,
+        out_specs=[in_vmem] * 8 + [anywhere] * 23,
         scratch_shapes=scratch,
         compiler_params=pltpu.CompilerParams(
-            collective_id=1, has_side_effects=True, vmem_limit_bytes=62 * 1024 * 1024
+            collective_id=1, has_side_effects=True, vmem_limit_bytes=63 * 1024 * 1024
         ),
-        name="scatter_all",
-    )(*grads, branch, residual)
-    return results[:7]
+        name="reach_back",
+    )(*grads, branch, *full, d_normed, residual, *others)
+    return results[:8]
 
 
 def by_tiles(total, size, act):
@@ -1057,17 +1537,6 @@
         return lax.psum_scatter(array, axes, scatter_dimension=axis, tiled=True)
 
     by_kernels = (lax.axis_size("dp"), lax.axis_size("tensor")) == (8, 4)
-    if by_kernels:
-        full_keyval, full_query, full_output, full_down, full_gate, full_up, piece = gather_all(
-            w_keyval, w_query, w_output, w_down, w_gate, w_up, cotangent
-        )
-    else:
-        full_keyval = gather(w_keyval, "dp")
-        full_query = gather(gather(w_query, "tensor", 1), "dp")
-        full_output = gather(gather(w_output, "tensor", 1), "dp")
-        full_gate, full_up = gather(w_gate, "dp"), gather(w_up, "dp")
-        full_down = gather(w_down, "dp")
-        piece = gather(cotangent, "tensor")
     places = doc_positions(segments)
     my_places = lax.dynamic_slice_in_dim(places, tensor_rank * rows, rows, 0)
     my_segments = lax.dynamic_slice_in_dim(segments, tensor_rank * rows, rows, 0)
@@ -1081,10 +1550,57 @@
     token_rows = tokens.astype(jnp.float32)
     normed_attn, unit_attn, inverse_attn = norm_forward(token_rows, gain_attn)
     normed_attn = normed_attn.astype(low)
-    keyval_pre = dot_nn(normed_attn, full_keyval)
     wide = KVH * HD
-    key_low = rotate(keyval_pre[:, :wide], cosine, sine_table).astype(low)
-    keyval = gather(jnp.concatenate([key_low, keyval_pre[:, wide:].astype(low)], axis=1), "tensor")
+    if by_kernels:
+        cos_tile = jnp.tile(cosine, (1, 4))
+        sin_tile = jnp.tile(jnp.concatenate([-sine_table, sine_table], axis=1), (1, 2))
+        (
+            query, keyval, heads_low, log_sum, residual, normed_mlp,
+            full_keyval, full_query, full_output, full_down, full_gate, full_up, piece,
+        ) = attend_all(
+            tokens, normed_attn, cos_tile, sin_tile, bias, gain_mlp[None, :],
+            w_keyval, w_query, w_output, w_down, w_gate, w_up, cotangent,
+        )
+    else:
+        full_keyval = gather(w_keyval, "dp")
+        keyval_pre = dot_nn(normed_attn, full_keyval)
+        key_low = rotate(keyval_pre[:, :wide], cosine, sine_table).astype(low)
+        keyval = jnp.concatenate([key_low, keyval_pre[:, wide:].astype(low)], axis=1)
+        keyval = gather(keyval, "tensor")
+        full_query = gather(gather(w_query, "tensor", 1), "dp")
+        query = rotate(dot_nn(normed_attn, full_query), cosine, sine_table) * (HD**-0.5)
+        query = query.astype(low)
+    if by_kernels:
+        grad_gate, grad_up, grad_down, branch, d_normed_mlp = feed_forward(
+            normed_mlp, full_gate, full_up, full_down, piece
+        )
+        to_down, to_gate, to_up, to_output, to_query, to_narrow, layer_out, grad_tokens = (
+            reach_back(
+                (grad_down, grad_gate, grad_up),
+                branch,
+                (full_keyval, full_query, full_output),
+                d_normed_mlp,
+                residual,
+                (
+                    cotangent, tokens, normed_attn, query, heads_low, keyval, log_sum, bias,
+                    cos_tile, sin_tile, gain_attn[None, :], gain_mlp[None, :],
+                ),
+            )
+        )
+        wide = 2 * KVH * HD
+        return (
+            layer_out,
+            grad_tokens,
+            to_narrow[:, wide],
+            to_query,
+            to_narrow[:, :wide],
+            to_output,
+            to_narrow[:, wide + 1],
+            to_gate,
+            to_up,
+            to_down,
+        )
+
     key_heads, value_heads = by_head(keyval[:, :wide]), by_head(keyval[:, wide:])
     blank = jnp.zeros_like(key_heads)
     key_f = jnp.concatenate([key_heads, blank], axis=2)
@@ -1093,33 +1609,30 @@
     value_b = jnp.concatenate([blank, value_heads], axis=2)
     key_t = key_heads.transpose(0, 2, 1)
     value_t = value_heads.transpose(0, 2, 1)
-
-    query = (rotate(dot_nn(normed_attn, full_query), cosine, sine_table) * (HD**-0.5)).astype(low)
     heads_low, log_sum = attend_forward(query, key_f, key_b, value_t, bias)
+    full_output = gather(gather(w_output, "tensor", 1), "dp")
     residual = token_rows + dot_nt(heads_low, full_output)
-
-    normed_mlp, unit_mlp, inverse_mlp = norm_forward(residual, gain_mlp)
-    if by_kernels:
-        grad_gate, grad_up, grad_down, branch, d_normed_mlp = feed_forward(
-            normed_mlp.astype(low), full_gate, full_up, full_down, piece
-        )
-    else:
-        gathered_mlp = gather(normed_mlp.astype(low), "tensor")
-        gate_act = dot_nn(gathered_mlp, full_gate)
-        up_act = dot_nn(gathered_mlp, full_up)
-        sigmoid_gate = jax.nn.sigmoid(gate_act)
-        silu_gate = gate_act * sigmoid_gate
-        hidden_low = (silu_gate * up_act).astype(low)
-        d_hidden = dot_nn(piece, full_down)
-        d_gate = (d_hidden * up_act * sigmoid_gate * (1.0 + gate_act * (1.0 - sigmoid_gate))).astype(low)
-        d_up = (d_hidden * silu_gate).astype(low)
-        d_normed_mlp = scatter(
-            (dot_nt(d_gate, full_gate) + dot_nt(d_up, full_up)).astype(low), "tensor"
-        ).astype(jnp.float32)
-        branch = dot_nt(hidden_low, full_down).astype(low)
-        grad_down = dot_tn(piece, hidden_low)
-        grad_gate = dot_tn(gathered_mlp, d_gate)
-        grad_up = dot_tn(gathered_mlp, d_up)
+    full_gate, full_up = gather(w_gate, "dp"), gather(w_up, "dp")
+    full_down = gather(w_down, "dp")
+    piece = gather(cotangent, "tensor")
+    normed_mlp_rows, unit_mlp, inverse_mlp = norm_forward(residual, gain_mlp)
+    normed_mlp = normed_mlp_rows.astype(low)
+    gathered_mlp = gather(normed_mlp, "tensor")
+    gate_act = dot_nn(gathered_mlp, full_gate)
+    up_act = dot_nn(gathered_mlp, full_up)
+    sigmoid_gate = jax.nn.sigmoid(gate_act)
+    silu_gate = gate_act * sigmoid_gate
+    hidden_low = (silu_gate * up_act).astype(low)
+    d_hidden = dot_nn(piece, full_down)
+    d_gate = (d_hidden * up_act * sigmoid_gate * (1.0 + gate_act * (1.0 - sigmoid_gate))).astype(low)
+    d_up = (d_hidden * silu_gate).astype(low)
+    d_normed_mlp = scatter(
+        (dot_nt(d_gate, full_gate) + dot_nt(d_up, full_up)).astype(low), "tensor"
+    ).astype(jnp.float32)
+    branch = dot_nt(hidden_low, full_down).astype(low)
+    grad_down = dot_tn(piece, hidden_low)
+    grad_gate = dot_tn(gathered_mlp, d_gate)
+    grad_up = dot_tn(gathered_mlp, d_up)
     d_norm_mlp, gain_mlp_part = norm_backward(d_normed_mlp, unit_mlp, inverse_mlp, gain_mlp)
     d_residual = cotangent.astype(jnp.float32) + d_norm_mlp
 
@@ -1146,28 +1659,6 @@
     d_normed_attn = dot_nt(dq_low, full_query) + dot_nt(dkv_low, full_keyval)
     d_norm_attn, gain_attn_part = norm_backward(d_normed_attn, unit_attn, inverse_attn, gain_attn)
     grad_tokens = (d_residual + d_norm_attn).astype(low)
-
-    if by_kernels:
-        gain_columns = jnp.stack([gain_attn_part, gain_mlp_part], axis=1)
-        gain_columns = jnp.pad(gain_columns, ((0, 0), (0, 126)))
-        grad_narrow = jnp.concatenate([grad_keyval, gain_columns], axis=1)
-        grads = (grad_output, grad_query, grad_narrow, grad_down, grad_gate, grad_up)
-        to_output, to_query, to_narrow, to_down, to_gate, to_up, layer_out = scatter_all(
-            [grad.astype(low) for grad in grads], branch, residual
-        )
-        wide = grad_keyval.shape[1]
-        return (
-            layer_out,
-            grad_tokens,
-            to_narrow[:, wide],
-            to_query,
-            to_narrow[:, :wide],
-            to_output,
-            to_narrow[:, wide + 1],
-            to_gate,
-            to_up,
-            to_down,
-        )
 
     layer_rows = residual + scatter(branch, "tensor").astype(jnp.float32)
 

time: 690 us -> 557 us (0.81)
  matrix products: 41.7 us -> 0 us
  waiting for transfers between devices: 33.1 us -> 0 us
  other arithmetic: 25.2 us -> 5.59 us
  local copies, waits for them, and re-layouts: 33.5 us -> 14.7 us
  between operations: 14.9 us -> 0.95 us
    dot_general x9 -> x0, matrix products: 41.7 us -> none  [the longest x3 15.7 us: dot_nn(): return jnp.dot(left, right, preferred_element_type=jnp.float32)]
    all_gather x1 -> x0, waiting for transfers between devices: 19.9 us -> none  [gather(): return lax.all_gather(array, axes, axis=axis, tiled=True)]
    reduce_scatter x1 -> x0, waiting for transfers between devices: 13.2 us -> none  [scatter(): return lax.psum_scatter(array, axes, scatter_dimension=axis, tiled=True)]
    pallas_call x4 -> x2, Pallas kernels: 397 us -> 391 us  [the longest x1 201 us: reach_back(): pl.pallas_call(reach_back_kernel, out_shape=out_shape, in_specs=[anywhere...]
  transfers between devices with their start and end apart: 2 -> 0, of which waited for: 2 -> 0; matrix products, arithmetic and copies ran while one was open for 4% -> 0% of each run, Pallas kernels for 0% -> 0%
where the time goes in v4:
time: 557 us; the launch traced here: 551 us
  Pallas kernels  530 us (95%)
  local copies, waits for them, and re-layouts  14.7 us (3%)
  other arithmetic  5.59 us (1%)
    pallas_call x1, Pallas kernels, reach_back(): pl.pallas_call(reach_back_kernel, out_shape=out_shape, in_specs=[anywhere...  201 us
    pallas_call x1, Pallas kernels, attend_all(): pl.pallas_call(attend_kernel, out_shape=shapes, in_specs=[in_vmem] * 6 +...  189 us
    pallas_call x1, Pallas kernels, feed_forward(): pl.pallas_call(feed_forward_kernel, out_shape=[jax.ShapeDtypeStruct((dept...  139 us

profile of v4, /device:TPU:0, one launch (start us, length us, event | category | flops | bytes accessed | tf_op | source)
XLA Modules:
  0.0 550.8 jit_solution(13997120449714543741)
XLA Ops:
  0.6 0.0 copy-start
  0.7 0.0 copy-start.7
  0.7 0.0 copy-start.8
  0.7 0.9 slice_compare_fusion
  1.6 0.8 dynamic_slice.7
  2.3 1.5 fusion
  3.8 0.1 add_select_fusion
  3.9 0.3 reduce-window.9
  4.2 0.1 slice.27
  4.3 0.1 slice_reduce_fusion.2
  4.4 0.1 bitcast_subtract_fusion
  4.5 0.1 dynamic-slice_convert_fusion
  4.6 0.2 fusion.5
  4.8 0.8 copy.22.sin_ref
  5.6 0.8 copy.21.cos_ref
  6.3 0.0 copy-done.7
  6.3 1.2 fusion.4.bias_ref
  7.5 0.0 copy-done
  7.5 0.0 copy-done.8
  7.5 1.3 fusion.2.normed_ref
  8.8 189.3 %attend_all.1 = (bf16[256,2048]{1,0:T(8,128)(2,1)}, bf16[1024,512]{1,0:T(8,128)(2,1)}, bf16[256,2048]{1,0:T(8,128)(2,1)}, f32[16,2,256]{2,1,0:T(2,128)}, f32[256...) custom-call(bf16[256,2048]{1,0:T(8,128)(2,1)} %tokens_ref.3, ...), custom_call_target="tpu_custom_call" | custom-call | tf_op jit(solution)/shard_map/attend_all/pallas_call | solution.py:590
  198.1 139.0 %feed_forward.1 = (bf16[2048,1408]{1,0:T(8,128)(2,1)}, bf16[2048,1408]{1,0:T(8,128)(2,1)}, bf16[2048,1408]{1,0:T(8,128)(2,1)}, bf16[4,256,2048]{2,1,0:T(8,128)(2,1)}, f32[256,2048]{1,0:T(8,128)}) custom-call(bf16[256,2048]{1,0:T(8,128)(2,1)} %get-tuple-element.36.normed_ref, bf16[2048,1408]{1,0:T(8,128)(2,1)} %get-tuple-element.37.gate_w_ref, ...), custom_call_target="tpu_custom_call" | custom-call | flops 53150220288 | bytes 62914560 | tf_op jit(solution)/shard_map/feed_forward/pallas_call | solution.py:1485
  337.2 201.3 %reach_back.1 = (f32[256,1408]{1,0:T(8,128)}, f32[256,1408]{1,0:T(8,128)}, f32[256,1408]{1,0:T(8,128)}, f32[256,512]{1,0:T(8,128)}, f32[256,512]{1,0:T(8,128)}, ...) custom-call(bf16[2048,1408]{1,0:T(8,128)(2,1)} %get-tuple-element.41, ...), custom_call_target="tpu_custom_call" | custom-call | tf_op jit(solution)/shard_map/reach_back/pallas_call | solution.py:1195
  538.5 0.0 copy-start.4
  538.5 1.6 slice_reduce_fusion
  540.1 1.6 slice.31
  541.6 0.0 copy-start.6
  541.6 2.4 copy.32
  544.0 0.0 copy-done.4
  544.0 0.0 copy-start.5
  544.0 0.0 copy-start.3
  544.0 1.0 copy.33
  545.0 0.0 copy-done.6
  545.0 0.8 copy.34
  545.8 0.0 copy-done.5
  545.8 0.0 copy-start.2
  545.8 0.8 copy.35
  546.6 0.0 copy-done.3
  546.6 1.1 copy.36
  547.7 0.0 copy-done.2
  547.7 0.0 copy-start.1
  547.7 1.1 copy.37
  548.8 0.8 copy-done.1
  549.5 1.1 copy.38
  (8 shorter events, 0.1 us)
Async XLA Ops:
  0.6 6.9 %copy-start = (bf16[256,2048]{1,0:T(8,128)(2,1)S(1)}, bf16[256,2048]{1,0:T(8,128)(2,1)}, u32[]{:S(2)}) copy-start(bf16[256,2048]{1,0:T(8,128)(2,1)} %tokens_ref.3) | copy-start | bytes 3145732
  0.7 5.7 %copy-start.7 = (s32[1024]{0:T(1024)S(1)}, s32[1024]{0:T(1024)}, u32[]{:S(2)}) copy-start(s32[1024]{0:T(1024)} %param.12) | copy-start | bytes 12292
  0.7 6.9 %copy-start.8 = (f32[2048]{0:T(1024)S(1)}, f32[2048]{0:T(1024)}, u32[]{:S(2)}) copy-start(f32[2048]{0:T(1024)} %param.13) | copy-start | bytes 24580
  538.5 5.5 %copy-start.4 = (bf16[256,2048]{1,0:T(8,128)(2,1)S(1)}, bf16[256,2048]{1,0:T(8,128)(2,1)}, u32[]{:S(2)}) copy-start(bf16[256,2048]{1,0:T(8,128)(2,1)} %get-tuple-element.78) | copy-start | bytes 3145732
  541.6 3.3 copy-start.6
  544.0 1.8 copy-start.5
  544.0 2.6 copy-start.3
  545.8 1.9 copy-start.2
  547.7 1.9 copy-start.1

commit v5 on v4

--- a/solution.py
+++ b/solution.py
@@ -262,9 +262,9 @@
 
 def attend_kernel(
     tokens_ref, normed_ref, cos_ref, sin_ref, bias_ref, gain_ref,
-    kv_ref, q_ref, o_ref, d_ref, g_ref, u_ref, c_ref,
+    kv_ref, q_ref, o_ref, g_ref, u_ref, c_ref,
     query_out, keyval_out, heads_out, log_out, residual_out, mlp_out,
-    fkv, fq, fo, fd, fg, fu, fc,
+    fkv, fq, fo, fg, fu, fc,
     kv_weight, weight, wide_weight, keyval, key_f, key_b, value_t,
     own_sem, z_send, z_recv, p_send, p_recv, k_send, k_recv, w_sem,
 ):
@@ -291,7 +291,6 @@
         (kv_ref, fkv.at[rows_of(dp), :]),
         (q_ref, fq.at[rows_of(dp), columns_of_rank(place)]),
         (o_ref, fo.at[rows_of(dp), columns_of_rank(place)]),
-        (d_ref, fd.at[rows_of(dp), :]),
         (g_ref, fg.at[rows_of(dp), :]),
         (u_ref, fu.at[rows_of(dp), :]),
         (c_ref, fc.at[rows_of(place), :]),
@@ -333,13 +332,12 @@
     x, y, core = flip(dp, 2), flip(dp, 4), flip(dp, 1)
     far = flip(x, 4)
 
-    blocks = [("kv", None), ("q", place), ("q", order[0]), ("q", order[1]), ("q", order[2])]
-    blocks += [("o", place), ("o", order[0]), ("o", order[1]), ("o", order[2])]
-    blocks += [("d", None), ("g", None), ("u", None)]
+    blocks = [("kv", None), ("q", place), ("g", None)] + [("q", rank) for rank in order]
+    blocks += [("o", place)] + [("o", rank) for rank in order] + [("u", None)]
 
     def block(index, owner, part=None):
         name, rank = blocks[index]
-        ref = {"kv": fkv, "q": fq, "o": fo, "d": fd, "g": fg, "u": fu}[name]
+        ref = {"kv": fkv, "q": fq, "o": fo, "g": fg, "u": fu}[name]
         first = owner * rows if part is None else owner * rows + part * half
         size = rows if part is None else half
         window = pl.ds(pl.multiple_of(first, half), size)
@@ -350,7 +348,7 @@
     def own_block(index):
         name, rank = blocks[index]
         if rank is None or rank is place:
-            return {"kv": kv_ref, "q": q_ref, "o": o_ref, "d": d_ref, "g": g_ref, "u": u_ref}[name]
+            return {"kv": kv_ref, "q": q_ref, "o": o_ref, "g": g_ref, "u": u_ref}[name]
         return block(index, dp)
 
     def plane_copy(index, lane):
@@ -494,50 +492,93 @@
                 residual_out[:, columns] * inverse * gain_ref[:, columns]
             ).astype(low)
 
+    inside = (place == 1) | (place == 2)
+
+    def cot_take(rank):
+        line_copy(2, rank, 1).wait_recv()
+        line_send(2, rank, start)
+
+    def line_take(which, step):
+        line_copy(which, order[step], 1).wait_recv()
+        line_send(which, order[step], start)
+
+    count = len(blocks)
+    kv, q_own, gate, o_own, up = 0, 1, 2, 6, 10
+    q_far, o_far = (3, 4, 5), (7, 8, 9)
+    plane_first(kv)
     line_send(0, place, start)
-    plane_first(0)
-    plane_first(1)
-    count = len(blocks)
-    line_of = {2: (0, 0), 3: (0, 1), 4: (0, 2), 6: (1, 0), 7: (1, 1), 8: (1, 2)}
-    for index in range(count):
-        ahead = index + 2
-        if ahead < count:
-            if ahead in line_of:
-                which, step = line_of[ahead]
-                line_copy(which, order[step], 1).wait_recv()
-                line_send(which, order[step], start)
-            plane_first(ahead)
-        if index == 0:
-            line_send(1, place, start)
-        if index == 6:
-            line_send(2, place, start)
-        if index >= 9:
-            line_copy(2, order[index - 9], 1).wait_recv()
-            line_send(2, order[index - 9], start)
-        plane_second(index)
-        if index >= 1:
-            plane_third(index - 1)
-        if index == 1:
-            plane_ready(0)
-            own_copies[0].wait()
-            make_keyval()
-        if 2 <= index <= 4:
-            keyval_take(index - 2)
-        if index == 5:
-            for block_index in range(1, 5):
-                plane_ready(block_index)
-            own_copies[1].wait()
-            make_query()
-        if 6 <= index <= 9:
-            attend(index - 6)
-        if index == 10:
-            for block_index in range(5, 9):
-                plane_ready(block_index)
-            own_copies[2].wait()
-            make_residual()
-    plane_third(count - 1)
-    for index in range(9, count):
+    plane_first(q_own)
+    line_take(0, 0)
+    line_send(1, place, start)
+    plane_second(kv)
+    plane_first(gate)
+    plane_second(q_own)
+    plane_third(kv)
+    plane_ready(kv)
+    own_copies[0].wait()
+    line_take(0, 1)
+    make_keyval()
+    plane_first(q_far[0])
+    plane_third(q_own)
+    line_take(1, 0)
+    line_take(0, 2)
+    plane_second(gate)
+    plane_first(q_far[1])
+    keyval_take(0)
+    line_take(1, 1)
+    plane_second(q_far[0])
+    plane_first(q_far[2])
+    plane_third(gate)
+    keyval_take(1)
+    line_take(1, 2)
+    plane_second(q_far[1])
+    plane_first(o_own)
+    plane_third(q_far[0])
+    keyval_take(2)
+    line_send(2, place, start)
+    plane_second(q_far[2])
+    plane_first(o_far[0])
+    plane_third(q_far[1])
+    plane_second(o_own)
+    plane_first(o_far[1])
+    plane_third(q_far[2])
+    for index in (q_own,) + q_far:
         plane_ready(index)
+    own_copies[1].wait()
+    make_query()
+    cot_take(order[0])
+
+    @pl.when(inside)
+    def _():
+        cot_take(order[1])
+
+    plane_second(o_far[0])
+    plane_first(o_far[2])
+    plane_third(o_own)
+    attend(0)
+    plane_second(o_far[1])
+    plane_first(up)
+    plane_third(o_far[0])
+    attend(1)
+    plane_second(o_far[2])
+    plane_third(o_far[1])
+    attend(2)
+    plane_third(o_far[2])
+    cot_take(jnp.where(inside, order[2], order[1]))
+    attend(3)
+    plane_second(up)
+    for index in (o_own,) + o_far:
+        plane_ready(index)
+    own_copies[2].wait()
+    make_residual()
+    plane_third(up)
+
+    @pl.when(jnp.logical_not(inside))
+    def _():
+        cot_take(order[2])
+
+    plane_ready(gate)
+    plane_ready(up)
     for index in range(count):
         plane_sent(index)
     for which in range(3):
@@ -555,8 +596,7 @@
 
 
 def attend_all(
-    tokens, normed, cos, sin, bias, gain, w_keyval, w_query, w_output, w_down, w_gate, w_up,
-    cotangent,
+    tokens, normed, cos, sin, bias, gain, w_keyval, w_query, w_output, w_gate, w_up, cotangent
 ):
     n_dp, n_line = lax.axis_size("dp"), lax.axis_size("tensor")
     low = jnp.bfloat16
@@ -581,7 +621,6 @@
         over(w_keyval, n_dp, 1),
         over(w_query, n_dp, n_line),
         over(w_output, n_dp, n_line),
-        over(w_down, n_dp, 1),
         over(w_gate, n_dp, 1),
         over(w_up, n_dp, 1),
         over(cotangent, n_line, 1),
@@ -590,8 +629,8 @@
     return pl.pallas_call(
         attend_kernel,
         out_shape=shapes,
-        in_specs=[in_vmem] * 6 + [anywhere] * 7,
-        out_specs=[in_vmem, anywhere] + [in_vmem] * 4 + [anywhere] * 7,
+        in_specs=[in_vmem] * 6 + [anywhere] * 6,
+        out_specs=[in_vmem, anywhere] + [in_vmem] * 4 + [anywhere] * 6,
         scratch_shapes=[
             pltpu.VMEM((depth, wide), low),
             pltpu.VMEM((2, depth, w_query.shape[1]), low),
@@ -600,7 +639,7 @@
             pltpu.VMEM((length, PAIR), low),
             pltpu.VMEM((length, PAIR), low),
             pltpu.VMEM((HD, length), low),
-            dma((7,)), dma((3, 2, 4)), dma((3, 4)), dma((12, 8)), dma((12, 8)),
+            dma((6,)), dma((3, 2, 4)), dma((3, 4)), dma((11, 8)), dma((11, 8)),
             dma((2, 4)), dma((4,)), dma((2,)),
         ],
         compiler_params=pltpu.CompilerParams(
@@ -608,8 +647,7 @@
         ),
         name="attend_all",
     )(
-        tokens, normed, cos, sin, bias, gain, w_keyval, w_query, w_output, w_down, w_gate, w_up,
-        cotangent,
+        tokens, normed, cos, sin, bias, gain, w_keyval, w_query, w_output, w_gate, w_up, cotangent
     )
 
 
@@ -624,6 +662,17 @@
     @pl.loop(0, total_rows // step)
     def _(index):
         act(pl.ds(pl.multiple_of(index * step, step), step))
+
+
+def enter_wide(dp, place):
+    barrier = pltpu.get_barrier_semaphore()
+    for bit in (1, 2, 4):
+        pl.semaphore_signal(barrier, inc=1, device_id=(flip(dp, bit), place), device_id_type=MESH)
+    for step in range(1, 4):
+        pl.semaphore_signal(
+            barrier, inc=1, device_id=(dp, (place + step) % 4), device_id_type=MESH
+        )
+    pl.semaphore_wait(barrier, 6)
 
 
 def reach_back_kernel(
@@ -635,7 +684,7 @@
     gd_side, gg_side, gu_side, go_side, gq_side, nar_side,
     gd_near, gg_near, gu_near, go_near, gq_near, nar_near,
     go_in, gq_in, nar_in, dkv_in, layer_in,
-    parts, held, stage, go_line, gq_line, nar_line, dkv_line, layer_line,
+    parts, held, stage, go_line, gq_line, nar_line, dkv_line, sums,
     d_residual, total, wide, d_branch, d_heads, dq_low, dkv_low, gains, weight, kv_weight,
     key_f, key_b, key_t, value_f, value_b, dk, dv,
     load_sem, fetch_sem, core_send, core_recv, p_send, p_recv, l_send, l_recv, in_sem, w_sem,
@@ -644,7 +693,7 @@
     low = jnp.bfloat16
     rows, depth = d_branch.shape
     half = rows // 2
-    enter(dp, place)
+    enter_wide(dp, place)
     x, y, core = flip(dp, 2), flip(dp, 4), flip(dp, 1)
     far = flip(x, 4)
     mine = (dp, x, y, far)
@@ -654,11 +703,10 @@
     cores = (gd_core, gg_core, gu_core, go_core, gq_core, nar_core)
     sides = (gd_side, gg_side, gu_side, go_side, gq_side, nar_side)
     nears = (gd_near, gg_near, gu_near, go_near, gq_near, nar_near)
-    lines = {3: go_line, 4: gq_line, 5: nar_line, 6: dkv_line, 7: layer_line}
+    lines = {3: go_line, 4: gq_line, 5: nar_line, 6: dkv_line}
     arrivals = {3: go_in, 4: gq_in, 5: nar_in, 6: dkv_in, 7: layer_in}
     front, back = pl.ds(0, half), pl.ds(half, half)
     ranks = dkv_line.shape[0]
-    last = ranks - 1
     turns = (3, 1, 2, 0)
 
     def rows_of(owner):
@@ -673,11 +721,13 @@
     def width_of(i):
         return cores[i].shape[2]
 
+    sets = (0, 1, 0, 0, 1, 1)
+
     def part(i, k):
-        return parts.at[i % 2, k, :, pl.ds(0, width_of(i))]
+        return parts.at[sets[i], k, :, pl.ds(0, width_of(i))]
 
     def half_part(i, k, window):
-        return parts.at[i % 2, k, window, pl.ds(0, width_of(i))]
+        return parts.at[sets[i], k, window, pl.ds(0, width_of(i))]
 
     def held_part(slot, count, width):
         return held.at[slot, pl.ds(0, count), pl.ds(0, width)]
@@ -777,94 +827,33 @@
                     sums.astype(low)
                 )
 
-    def line_copy(i, rank, slot, step):
-        src = lines[i].at[(step + 1) // 2] if i == 7 else lines[i].at[rank]
+    def line_copy(i, step):
+        target = (place + step) % ranks
+        src = branch_ref.at[target] if i == 7 else lines[i].at[target]
         return remote(
-            src, arrivals[i].at[slot], l_send.at[i - 3, rank], l_recv.at[i - 3, slot],
-            (dp, place + step),
-        )
-
-    def line_add(i, ref, slot, step):
-        line_copy(i, slot, slot, step).wait_recv()
-        copy = fetch(arrivals[i].at[slot], 0)
-        copy.start()
-        copy.wait()
-        add_rows(ref, held_part(0, ref.shape[0], ref.shape[1]))
-
-    def line_own(i, rank, step):
-        if i != 7:
-            return lines[i].at[rank]
-        ref = lines[i].at[(step + 1) // 2]
-        copy = pltpu.make_async_copy(branch_ref.at[rank], ref, in_sem.at[0])
-        copy.start()
-        copy.wait()
-        return ref
-
-    def line_step(i, turn):
-        down, up = place - last + turn, place + last - turn
-
-        @pl.when(down >= 0)
-        def _():
-            if i == 7 and turn > 0:
-
-                @pl.when(down > 0)
-                def _():
-                    line_copy(i, down - 1, down - 1, -1).wait_send()
-
-            ref = line_own(i, down, -1)
-
-            @pl.when(place < last)
-            def _():
-                line_add(i, ref, down, -1)
-
-            line_copy(i, down, down, -1).start()
-
-        @pl.when(up <= last)
-        def _():
-            if i == 7 and turn > 0:
-
-                @pl.when(up < last)
-                def _():
-                    line_copy(i, up + 1, up + 1, 1).wait_send()
-
-            ref = line_own(i, up, 1)
-
-            @pl.when(place > 0)
-            def _():
-                line_add(i, ref, up, 1)
-
-            line_copy(i, up, ranks if turn == last - 1 else up, 1).start()
+            src, arrivals[i].at[place], l_send.at[i - 3, step], l_recv.at[i - 3, step],
+            (dp, target),
+        )
+
+    def line_start(i):
+        for step in range(1, ranks):
+            line_copy(i, step).start()
 
     def line_last(i, add):
-        @pl.when(place < last)
-        def _():
-            line_copy(i, place, place, 1).wait_recv()
-            copy = fetch(arrivals[i].at[place], 0)
-            copy.start()
-            copy.wait()
-            add()
-
-        @pl.when(place > 0)
-        def _():
-            line_copy(i, place, ranks, 1).wait_recv()
-            copy = fetch(arrivals[i].at[ranks], 0)
-            copy.start()
-            copy.wait()
-            add()
+        def begin(step):
+            line_copy(i, step).wait_recv()
+            fetch(arrivals[i].at[(place + ranks - step) % ranks], step % 2).start()
+
+        begin(1)
+        for step in range(1, ranks):
+            if step + 1 < ranks:
+                begin(step + 1)
+            fetch(arrivals[i].at[place], step % 2).wait()
+            add(step % 2)
 
     def line_sent(i):
-        for rank in range(ranks):
-            if i == 7:
-
-                @pl.when((rank == place - 1) | (rank == place + 1))
-                def _():
-                    line_copy(i, rank, rank, 1).wait_send()
-
-            else:
-
-                @pl.when(rank != place)
-                def _():
-                    line_copy(i, rank, rank, 1).wait_send()
+        for step in range(1, ranks):
+            line_copy(i, step).wait_send()
 
     def line_out(i):
         out = outs[i]
@@ -873,9 +862,9 @@
         def begin(window):
             out[window, :] = lines[i][place, window, :].astype(jnp.float32)
 
-        def add():
+        def add(slot):
             def act(window):
-                out[window, :] += held[0, window, pl.ds(0, width)].astype(jnp.float32)
+                out[window, :] += held[slot, window, pl.ds(0, width)].astype(jnp.float32)
 
             over_rows(count, act)
 
@@ -933,7 +922,7 @@
 
     def keep_mine(i, tile):
         for k in turns:
-            parts[i % 2, k, :, pl.ds(0, width_of(i))] = tile(mine[k])
+            parts[sets[i], k, :, pl.ds(0, width_of(i))] = tile(mine[k])
 
     def go_tile(owner):
         return square_tile(d_branch, heads_ref, owner)
@@ -969,9 +958,13 @@
             if index + 1 < steps:
                 weight_load(fq, index + 1).start()
             weight_load(fq, index).wait()
-            wide[:, index * size : (index + 1) * size] = dot_nt(
-                dq_low[...], weight[index % 2]
-            ) + dot_nt(dkv_low[...], kv_weight[index * size : (index + 1) * size, :])
+            wide[:, index * size : (index + 1) * size] = dot_nt(dq_low[...], weight[index % 2])
+
+    def add_d_normed():
+        for index in range(steps):
+            wide[:, index * size : (index + 1) * size] += dot_nt(
+                dkv_low[...], kv_weight[index * size : (index + 1) * size, :]
+            )
 
     def attend_back(group):
         (key_f[...], key_b[...]), value_tile = head_tiles(keyval_ref, group)
@@ -1024,13 +1017,11 @@
         wide_columns = dkv_line.shape[2]
 
         def begin(window):
-            wide[window, pl.ds(0, wide_columns)] = dkv_line[place, window, :].astype(jnp.float32)
-
-        def add():
+            sums[window, :] = dkv_line[place, window, :].astype(jnp.float32)
+
+        def add(slot):
             def act(window):
-                wide[window, pl.ds(0, wide_columns)] += held[
-                    0, window, pl.ds(0, wide_columns)
-                ].astype(jnp.float32)
+                sums[window, :] += held[slot, window, pl.ds(0, wide_columns)].astype(jnp.float32)
 
             over_rows(rows, act)
 
@@ -1038,21 +1029,23 @@
         line_last(6, add)
         for tile in range(wide_columns // PAIR):
             columns = slice(tile * PAIR, (tile + 1) * PAIR)
-            made = wide[:, columns]
+            made = sums[:, columns]
             if tile < KVH * HD // PAIR:
                 made = turn(made, cos_ref[...], -sin_ref[...])
             dkv_low[:, columns] = made.astype(low)
 
     def finish_layer():
-        line_sent(7)
-        own = line_own(7, place, -1)
+        own = parts.at[0, 0]
+        copy = pltpu.make_async_copy(branch_ref.at[place], own, in_sem.at[0])
+        copy.start()
+        copy.wait()
 
         def begin(window):
             total[window, :] += own[window, :].astype(jnp.float32)
 
-        def add():
+        def add(slot):
             def act(window):
-                total[window, :] += held[0, window, :].astype(jnp.float32)
+                total[window, :] += held[slot, window, :].astype(jnp.float32)
 
             over_rows(rows, act)
 
@@ -1066,82 +1059,78 @@
     dn_load = pltpu.make_async_copy(dn_ref, wide, in_sem.at[1])
     total_load = pltpu.make_async_copy(residual_ref, total, in_sem.at[2])
     kv_load = pltpu.make_async_copy(fkv, kv_weight, in_sem.at[3])
-    for i in range(3):
+
+    def send_core(i):
         for k in turns:
             core_copy(i, k).start()
+
+    send_core(0)
     for load in (dn_load, total_load, kv_load):
         load.start()
     load_own(0)
     load_own(1)
-    line_step(7, 0)
+    line_start(7)
     dn_load.wait()
     total_load.wait()
+    send_core(1)
     norm_back(wide, total, gain_mlp_ref, 1, after_mlp)
     stage_core(0)
     send_theirs(3, go_tile)
     stage_core(1)
+    send_core(2)
     make_d_heads()
     stage_side(0)
-    line_step(7, 1)
     attend_back(0)
+    stage_side(1)
     stage_near(0)
     plane_sent(0)
-    load_own(2)
-    stage_side(1)
+    keep_mine(3, go_tile)
+    stage_core(3)
     attend_back(1)
-    stage_core(2)
     stage_near(1)
     plane_sent(1)
-    keep_mine(3, go_tile)
-    stage_core(3)
-    line_step(7, 2)
     attend_back(2)
-    stage_side(2)
+    stage_side(3)
     attend_back(3)
+    line_start(6)
     theirs_sent(3)
     send_theirs(4, gq_tile)
-    line_step(6, 0)
-    stage_near(2)
-    plane_sent(2)
     keep_mine(4, gq_tile)
-    stage_side(3)
     stage_core(4)
-    line_step(6, 1)
     stage_near(3)
+    line_start(3)
     plane_sent(3)
-    line_step(6, 2)
-    line_step(3, 0)
+    load_own(2)
+    stage_core(2)
+    make_d_normed()
     kv_load.wait()
     make_dkv()
-    make_d_normed()
+    add_d_normed()
+    stage_side(4)
     norm_back(wide, tokens_ref, gain_attn_ref, 0, after_attn)
     theirs_sent(4)
     send_theirs(5, narrow_tile)
+    stage_near(4)
+    line_start(4)
+    plane_sent(4)
     keep_mine(5, narrow_tile)
-    stage_side(4)
-    line_step(3, 1)
     stage_core(5)
-    line_step(3, 2)
-    stage_near(4)
-    line_step(4, 0)
+    stage_side(2)
+    line_out(3)
     stage_side(5)
+    stage_near(5)
+    line_start(5)
+    stage_near(2)
+    plane_sent(2)
     finish_layer()
-    line_step(4, 1)
-    stage_near(5)
-    line_step(5, 0)
-    line_step(4, 2)
-    line_step(5, 1)
-    line_out(3)
-    line_step(5, 2)
     line_out(4)
     line_out(5)
-    plane_sent(4)
     plane_sent(5)
     theirs_sent(5)
     for i in range(3):
         for k in turns:
             core_copy(i, k).wait_send()
-    for i in range(3, 7):
+    for i in range(3, 8):
         line_sent(i)
 
 
@@ -1166,7 +1155,7 @@
     out_shape += [jax.ShapeDtypeStruct((4, rows, w), low) for w in widths]
     out_shape += [jax.ShapeDtypeStruct((2, half, w), low) for w in widths]
     out_shape += [jax.ShapeDtypeStruct((2, rows, w), low) for w in widths]
-    out_shape += [jax.ShapeDtypeStruct((ranks + 1,) + shape, low) for shape in lined]
+    out_shape += [jax.ShapeDtypeStruct((ranks,) + shape, low) for shape in lined]
     dma = pltpu.SemaphoreType.DMA
     scratch = [
         pltpu.VMEM((2, 4, rows, depth), low),
@@ -1174,7 +1163,7 @@
         pltpu.VMEM((2, rows, depth), low),
     ]
     scratch += [pltpu.VMEM((ranks,) + shape, low) for shape in lined[:4]]
-    scratch += [pltpu.VMEM((2, rows, depth), low)]
+    scratch += [pltpu.VMEM((rows, keyval), wide)]
     scratch += [pltpu.VMEM((rows, depth), wide)] * 3
     scratch += [pltpu.VMEM((rows, depth), low)] * 3
     scratch += [
@@ -1190,7 +1179,7 @@
         pltpu.VMEM((length, PAIR), wide),
         pltpu.VMEM((length, PAIR), wide),
         dma((3, 4)), dma((2,)), dma((6, 4)), dma((6, 4)), dma((6, 6)), dma((6, 6)),
-        dma((5, ranks)), dma((5, ranks + 1)), dma((4,)), dma((2,)),
+        dma((5, ranks)), dma((5, ranks)), dma((4,)), dma((2,)),
     ]
     results = pl.pallas_call(
         reach_back_kernel,
@@ -1221,7 +1210,7 @@
     normed_ref, gate_w_ref, up_w_ref, down_w_ref, cot_ref,
     gg_out, gu_out, gd_out, branch_out, dn_out,
     wg, wu, wd, cot, normed, hid, dg, du, part, arrival, branch_stage, gate_stage, up_stage,
-    load_sem, n_send, n_recv, l_send, l_recv, stage_sem,
+    load_sem, n_send, n_recv, l_send, l_recv, stage_sem, p_send, p_recv,
 ):
     dp, place = lax.axis_index("dp"), lax.axis_index("tensor")
     rows, depth = normed_ref.shape
@@ -1250,15 +1239,42 @@
         ref = normed.at[chunk(rank), :]
         return remote(ref, ref, n_send.at[(step + 1) // 2, rank], n_recv.at[rank], step)
 
+    x, y, core = flip(dp, 2), flip(dp, 4), flip(dp, 1)
+    far = flip(x, 4)
+    shards = (down_w_ref,)
+    weights = (wd,)
+    depth_rows = down_w_ref.shape[0]
+    half = depth_rows // 2
+
+    def weight_rows(i, owner, part=None):
+        first = owner * depth_rows if part is None else owner * depth_rows + part * half
+        count = depth_rows if part is None else half
+        return weights[i].at[pl.ds(pl.multiple_of(first, half), count), :]
+
+    def plane_copy(i, lane):
+        if lane < 2:
+            src, dst, device = shards[i], weight_rows(i, dp), (x, y)[lane]
+        elif lane < 4:
+            src = dst = weight_rows(i, (x, y)[lane - 2], lane - 2)
+            device = (y, x)[lane - 2]
+        else:
+            owner = (dp, x, y, far)[lane - 4]
+            dst, device = weight_rows(i, owner), core
+            src = shards[i] if lane == 4 else dst
+        return pltpu.make_async_remote_copy(
+            src_ref=src, dst_ref=dst, send_sem=p_send.at[i, lane], recv_sem=p_recv.at[i, lane],
+            device_id=(device, place), device_id_type=MESH,
+        )
+
     loads = [
         pltpu.make_async_copy(src, dst, load_sem.at[i])
         for i, (src, dst) in enumerate(
             (
                 (normed_ref, normed.at[chunk(place), :]),
                 (gate_w_ref, wg),
+                (cot_ref, cot),
                 (up_w_ref, wu),
-                (cot_ref, cot),
-                (down_w_ref, wd),
+                (down_w_ref, weight_rows(0, dp)),
             )
         )
     ]
@@ -1271,13 +1287,28 @@
     def _():
         own_copy(-1).start()
 
+    for lane in (0, 1, 4):
+        plane_copy(0, lane).start()
     for load in loads:
         load.start()
-    for load in loads:
-        load.wait()
+
+    def plane_second(i):
+        for lane in range(2):
+            plane_copy(i, lane).wait_recv()
+            plane_copy(i, lane + 2).start()
+            plane_copy(i, lane + 5).start()
+
+    def plane_third(i):
+        plane_copy(i, 2).wait_recv()
+        plane_copy(i, 3).wait_recv()
+        plane_copy(i, 7).start()
+
+    def plane_ready(i):
+        for lane in range(4, 8):
+            plane_copy(i, lane).wait_recv()
 
     def sums_copy(rank, cut, slot, step):
-        window = pl.ds(cut * few, few)
+        window = pl.ds(pl.multiple_of(cut * few, few), few)
         return remote(
             part.at[rank, window, :], arrival.at[slot, window, :], l_send.at[rank, cut],
             l_recv.at[slot, cut], step,
@@ -1326,53 +1357,52 @@
         def _():
             pass_copy(rank, -1).start()
 
+    inside = (place == 1) | (place == 2)
+    plane_second(0)
+    take(order[0])
+
+    @pl.when(inside)
+    def _():
+        take(order[1])
+
+    plane_third(0)
+    for load in loads:
+        load.wait()
+    plane_ready(0)
+
     @pl.loop(0, 4)
     def _(turn):
         rank = jnp.where(
             turn == 0,
-            place,
-            jnp.where(turn == 1, order[0], jnp.where(turn == 2, order[1], order[2])),
-        )
-
-        inside = (place == 1) | (place == 2)
-
-        @pl.when(turn == 1)
-        def _():
-            take(order[0])
-
-            @pl.when(inside)
-            def _():
-                take(order[1])
-
-        @pl.when((turn == 2) & (place != 1) & (place != 2))
+            order[0],
+            jnp.where(turn == 1, place, jnp.where(turn == 2, order[1], order[2])),
+        )
+
+        @pl.when((turn == 1) & inside)
+        def _():
+            take(order[2])
+
+        @pl.when((turn == 2) & jnp.logical_not(inside))
         def _():
             take(order[1])
 
-        @pl.when(turn == 3)
+        @pl.when((turn == 3) & jnp.logical_not(inside))
         def _():
             take(order[2])
 
         compute(rank)
 
-        @pl.when((turn > 0) & (place == 3))
+        @pl.when((turn != 1) & (place == 3))
         def _():
             for cut in range(cuts):
                 sums_copy(rank, cut, rank, -1).start()
 
-        @pl.when((turn > 0) & (place == 0))
+        @pl.when((turn != 1) & (place == 0))
         def _():
             slot = jnp.where(rank == 1, 4, rank)
             for cut in range(cuts):
                 sums_copy(rank, cut, slot, 1).start()
 
-        @pl.when(turn > 0)
-        def _():
-            branch_copy(rank).wait()
-
-        branch(rank)
-
-    branch_copy(0).wait()
-
     def gate_copy(tile):
         return pltpu.make_async_copy(gate_stage, gg_out.at[tile, :], stage_sem.at[1])
 
@@ -1383,9 +1413,9 @@
         return pltpu.make_async_copy(gate_stage, gd_out.at[tile, :], stage_sem.at[1])
 
     size = gate_stage.shape[0]
-
-    @pl.loop(0, depth // size)
-    def _(index):
+    tiles = depth // size
+
+    def gate_up_tile(index):
         tile = pl.ds(pl.multiple_of(index * size, size), size)
         left = normed[:, tile]
         gate_grad = dot_tn(left, dg[...]).astype(low)
@@ -1400,38 +1430,62 @@
         up_stage[...] = dot_tn(left, du[...]).astype(low)
         up_copy(tile).start()
 
+    def down_tile(index):
+        tile = pl.ds(pl.multiple_of(index * size, size), size)
+        down_grad = dot_tn(cot[:, tile], hid[...]).astype(low)
+
+        @pl.when(index > 0)
+        def _():
+            down_copy(tile).wait()
+
+        gate_stage[...] = down_grad
+        down_copy(tile).start()
+
     last = pl.ds(depth - size, size)
+
+    def relay(rank, slot, step, cut):
+        sums_copy(rank, cut, rank, step).wait_recv()
+        window = pl.ds(pl.multiple_of(cut * few, few), few)
+        part[rank, window, :] = part[rank, window, :] + arrival[rank, window, :]
+        sums_copy(rank, cut, slot, step).start()
+
+    outward = 3 - 2 * place
+
+    @pl.loop(0, cuts)
+    def _(cut):
+        @pl.when(inside)
+        def _():
+            relay(3 - place, 4 - 3 * (place - 1), outward, cut)
+
+        @pl.loop(0, tiles // cuts)
+        def _(index):
+            gate_up_tile(cut * (tiles // cuts) + index)
+
     gate_copy(last).wait()
     up_copy(last).wait()
 
-    def relay(rank, slot, step, cut):
-        sums_copy(rank, cut, rank, step).wait_recv()
-        window = pl.ds(cut * few, few)
-        part[rank, window, :] = part[rank, window, :] + arrival[rank, window, :]
-        sums_copy(rank, cut, slot, step).start()
-
-    @pl.when((place == 1) | (place == 2))
-    def _():
-        outward = 3 - 2 * place
-        for cut in range(cuts):
-            relay(3 - place, 4 - 3 * (place - 1), outward, cut)
-        for cut in range(cuts):
+    @pl.loop(0, cuts)
+    def _(cut):
+        @pl.when(inside)
+        def _():
             relay(6 - 3 * place, 6 - 3 * place, outward, cut)
             relay(3 * (place - 1), 4 * (place - 1), -outward, cut)
 
-    @pl.loop(0, depth // size)
-    def _(index):
-        tile = pl.ds(pl.multiple_of(index * size, size), size)
-        down_grad = dot_tn(cot[:, tile], hid[...]).astype(low)
-
-        @pl.when(index > 0)
-        def _():
-            down_copy(tile).wait()
-
-        gate_stage[...] = down_grad
-        down_copy(tile).start()
+        @pl.loop(0, tiles // cuts)
+        def _(index):
+            down_tile(cut * (tiles // cuts) + index)
 
     down_copy(last).wait()
+
+    @pl.loop(0, 4)
+    def _(rank):
+        @pl.when(rank > 0)
+        def _():
+            branch_copy(rank).wait()
+
+        branch(rank)
+
+    branch_copy(0).wait()
 
     for cut in range(cuts):
         window = pl.ds(cut * few, few)
@@ -1469,6 +1523,9 @@
         def _():
             for cut in range(cuts):
                 sums_copy(rank, cut, rank, 1).wait_send()
+
+    for lane in range(8):
+        plane_copy(0, lane).wait_send()
 
 
 def feed_forward(normed, w_gate, w_up, w_down, cotangent):
@@ -1501,7 +1558,7 @@
             pltpu.VMEM((256, units), low),
             pltpu.VMEM((256, units), low),
             dma((5,)), dma((2, ranks)), dma((ranks,)), dma((ranks, cuts)), dma((ranks + 1, cuts)),
-            dma((3,)),
+            dma((3,)), dma((1, 8)), dma((1, 8)),
         ],
         compiler_params=pltpu.CompilerParams(
             collective_id=2, has_side_effects=True, vmem_limit_bytes=62 * 1024 * 1024
@@ -1556,10 +1613,10 @@
         sin_tile = jnp.tile(jnp.concatenate([-sine_table, sine_table], axis=1), (1, 2))
         (
             query, keyval, heads_low, log_sum, residual, normed_mlp,
-            full_keyval, full_query, full_output, full_down, full_gate, full_up, piece,
+            full_keyval, full_query, full_output, full_gate, full_up, piece,
         ) = attend_all(
             tokens, normed_attn, cos_tile, sin_tile, bias, gain_mlp[None, :],
-            w_keyval, w_query, w_output, w_down, w_gate, w_up, cotangent,
+            w_keyval, w_query, w_output, w_gate, w_up, cotangent,
         )
     else:
         full_keyval = gather(w_keyval, "dp")
@@ -1572,7 +1629,7 @@
         query = query.astype(low)
     if by_kernels:
         grad_gate, grad_up, grad_down, branch, d_normed_mlp = feed_forward(
-            normed_mlp, full_gate, full_up, full_down, piece
+            normed_mlp, full_gate, full_up, w_down, piece
         )
         to_down, to_gate, to_up, to_output, to_query, to_narrow, layer_out, grad_tokens = (
             reach_back(

time: 557 us -> 513 us (0.921)
  Pallas kernels: 530 us -> 485 us
    pallas_call x1, Pallas kernels: 189 us -> 149 us  [attend_all(): pl.pallas_call(attend_kernel, out_shape=shapes, in_specs=[in_vmem] * 6 +...]
    pallas_call x1, Pallas kernels: 201 us -> 191 us  [reach_back(): pl.pallas_call(reach_back_kernel, out_shape=out_shape, in_specs=[anywhere...]
    pallas_call x1, Pallas kernels: 139 us -> 145 us  [feed_forward(): pl.pallas_call(feed_forward_kernel, out_shape=[jax.ShapeDtypeStruct((dept...]
where the time goes in v5:
time: 513 us; the launch traced here: 506 us
  Pallas kernels  485 us (95%)
  local copies, waits for them, and re-layouts  14.7 us (3%)
  other arithmetic  5.59 us (1%)
    pallas_call x1, Pallas kernels, reach_back(): pl.pallas_call(reach_back_kernel, out_shape=out_shape, in_specs=[anywhere...  191 us
    pallas_call x1, Pallas kernels, attend_all(): pl.pallas_call(attend_kernel, out_shape=shapes, in_specs=[in_vmem] * 6 +...  149 us
    pallas_call x1, Pallas kernels, feed_forward(): pl.pallas_call(feed_forward_kernel, out_shape=[jax.ShapeDtypeStruct((dept...  145 us

profile of v5, /device:TPU:0, one launch (start us, length us, event | category | flops | bytes accessed | tf_op | source)
XLA Modules:
  0.0 506.4 jit_solution(15767142103021828207)
XLA Ops:
  0.6 0.0 copy-start
  0.7 0.0 copy-start.7
  0.7 0.0 copy-start.8
  0.7 0.9 slice_compare_fusion
  1.6 0.8 dynamic_slice.7
  2.3 1.5 fusion
  3.8 0.1 add_select_fusion
  3.9 0.3 reduce-window.9
  4.2 0.1 slice.27
  4.3 0.1 slice_reduce_fusion.2
  4.4 0.1 bitcast_subtract_fusion
  4.5 0.1 dynamic-slice_convert_fusion
  4.6 0.2 fusion.5
  4.8 0.8 copy.22.sin_ref
  5.6 0.8 copy.21.cos_ref
  6.3 0.0 copy-done.7
  6.3 1.2 fusion.4.bias_ref
  7.5 0.0 copy-done
  7.5 0.0 copy-done.8
  7.5 1.3 fusion.2.normed_ref
  8.8 148.8 %attend_all.1 = (bf16[256,2048]{1,0:T(8,128)(2,1)}, bf16[1024,512]{1,0:T(8,128)(2,1)}, bf16[256,2048]{1,0:T(8,128)(2,1)}, f32[16,2,256]{2,1,0:T(2,128)}, f32[256...) custom-call(bf16[256,2048]{1,0:T(8,128)(2,1)} %tokens_ref.3, ...), custom_call_target="tpu_custom_call" | custom-call | tf_op jit(solution)/shard_map/attend_all/pallas_call | solution.py:629
  157.6 145.2 %feed_forward.1 = (bf16[2048,1408]{1,0:T(8,128)(2,1)}, bf16[2048,1408]{1,0:T(8,128)(2,1)}, bf16[2048,1408]{1,0:T(8,128)(2,1)}, bf16[4,256,2048]{2,1,0:T(8,128)(2,1)}, f32[256,2048]{1,0:T(8,128)}) custom-call(bf16[256,2048]{1,0:T(8,128)(2,1)} %get-tuple-element.35.normed_ref, bf16[2048,1408]{1,0:T(8,128)(2,1)} %get-tuple-element.36.gate_w_ref, ...), custom_call_target="tpu_custom_call" | custom-call | flops 53150220288 | bytes 62914560 | tf_op jit(solution)/shard_map/feed_forward/pallas_call | solution.py:1542
  302.8 191.3 %reach_back.1 = (f32[256,1408]{1,0:T(8,128)}, f32[256,1408]{1,0:T(8,128)}, f32[256,1408]{1,0:T(8,128)}, f32[256,512]{1,0:T(8,128)}, f32[256,512]{1,0:T(8,128)}, ...) custom-call(bf16[2048,1408]{1,0:T(8,128)(2,1)} %get-tuple-element.39, ...), custom_call_target="tpu_custom_call" | custom-call | tf_op jit(solution)/shard_map/reach_back/pallas_call | solution.py:1184
  494.1 0.0 copy-start.4
  494.1 1.6 slice_reduce_fusion
  495.7 1.6 slice.31
  497.2 0.0 copy-start.6
  497.2 2.4 copy.32
  499.6 0.0 copy-done.4
  499.6 0.0 copy-start.5
  499.6 0.0 copy-start.3
  499.6 1.0 copy.33
  500.6 0.0 copy-done.6
  500.6 0.8 copy.34
  501.4 0.0 copy-done.5
  501.4 0.0 copy-start.2
  501.4 0.8 copy.35
  502.2 0.0 copy-done.3
  502.2 1.1 copy.36
  503.3 0.0 copy-done.2
  503.3 0.0 copy-start.1
  503.3 1.1 copy.37
  504.4 0.8 copy-done.1
  505.2 1.1 copy.38
  (8 shorter events, 0.1 us)
Async XLA Ops:
  0.6 6.9 %copy-start = (bf16[256,2048]{1,0:T(8,128)(2,1)S(1)}, bf16[256,2048]{1,0:T(8,128)(2,1)}, u32[]{:S(2)}) copy-start(bf16[256,2048]{1,0:T(8,128)(2,1)} %tokens_ref.3) | copy-start | bytes 3145732
  0.7 5.7 %copy-start.7 = (s32[1024]{0:T(1024)S(1)}, s32[1024]{0:T(1024)}, u32[]{:S(2)}) copy-start(s32[1024]{0:T(1024)} %param.12) | copy-start | bytes 12292
  0.7 6.9 %copy-start.8 = (f32[2048]{0:T(1024)S(1)}, f32[2048]{0:T(1024)}, u32[]{:S(2)}) copy-start(f32[2048]{0:T(1024)} %param.13) | copy-start | bytes 24580
  494.1 5.5 %copy-start.4 = (bf16[256,2048]{1,0:T(8,128)(2,1)S(1)}, bf16[256,2048]{1,0:T(8,128)(2,1)}, u32[]{:S(2)}) copy-start(bf16[256,2048]{1,0:T(8,128)(2,1)} %get-tuple-element.76) | copy-start | bytes 3145732
  497.2 3.3 copy-start.6
  499.6 1.8 copy-start.5
  499.6 2.6 copy-start.3
  501.4 1.9 copy-start.2
  503.3 1.9 copy-start.1

commit v6 on v5

--- a/solution.py
+++ b/solution.py
@@ -677,22 +677,53 @@
 
 def reach_back_kernel(
     gd_ref, gg_ref, gu_ref, branch_ref, fkv, fq, fo, dn_ref, residual_ref,
+    cot_in, tokens_in, normed_in, query_in, heads_in, keyval_in, log_in, bias_in,
+    cos_in, sin_in, gain_attn_in, gain_mlp_in,
+    gd_out, gg_out, gu_out, go_out, gq_out, nar_out, layer_out, tokens_out,
+    gd_core, gg_core, gu_core, go_core, gq_core, nar_core,
+    gd_near, gg_near, gu_near, go_near, gq_near, nar_near,
+    go_in, gq_in, nar_in, dkv_in, layer_in,
+    gd_side, gg_side, gu_side, go_side, gq_side, nar_side,
+    parts, held, early, stage, go_line, gq_line, nar_line, dkv_line, sums,
+    d_residual, total, wide, d_branch, d_heads, dq_low, dkv_low, gains, weight, kv_weight,
+    key_f, key_b, key_t, value_f, value_b, dk, dv,
+    chain, units_made, go_made, gq_made, nar_made, tokens_made,
     cot_ref, tokens_ref, normed_ref, query_ref, heads_ref, keyval_ref, log_ref, bias_ref,
     cos_ref, sin_ref, gain_attn_ref, gain_mlp_ref,
-    gd_out, gg_out, gu_out, go_out, gq_out, nar_out, layer_out, tokens_out,
-    gd_core, gg_core, gu_core, go_core, gq_core, nar_core,
-    gd_side, gg_side, gu_side, go_side, gq_side, nar_side,
-    gd_near, gg_near, gu_near, go_near, gq_near, nar_near,
-    go_in, gq_in, nar_in, dkv_in, layer_in,
-    parts, held, stage, go_line, gq_line, nar_line, dkv_line, sums,
-    d_residual, total, wide, d_branch, d_heads, dq_low, dkv_low, gains, weight, kv_weight,
-    key_f, key_b, key_t, value_f, value_b, dk, dv,
     load_sem, fetch_sem, core_send, core_recv, p_send, p_recv, l_send, l_recv, in_sem, w_sem,
+    c_send, c_recv, early_sem, leave_sem, enter_sem,
 ):
     dp, place = lax.axis_index("dp"), lax.axis_index("tensor")
     low = jnp.bfloat16
     rows, depth = d_branch.shape
     half = rows // 2
+    arriving = [
+        pltpu.make_async_copy(src, dst, enter_sem.at[number])
+        for number, (src, dst) in enumerate(
+            (
+                (cot_in, cot_ref),
+                (gain_mlp_in, gain_mlp_ref),
+                (keyval_in, keyval_ref),
+                (query_in, query_ref),
+                (bias_in, bias_ref),
+                (log_in, log_ref),
+                (cos_in, cos_ref),
+                (sin_in, sin_ref),
+                (heads_in, heads_ref),
+                (normed_in, normed_ref),
+                (tokens_in, tokens_ref),
+                (gain_attn_in, gain_attn_ref),
+            )
+        )
+    ]
+    dn_load = pltpu.make_async_copy(dn_ref, wide, in_sem.at[1])
+    total_load = pltpu.make_async_copy(residual_ref, total, in_sem.at[2])
+    kv_load = pltpu.make_async_copy(fkv, kv_weight, in_sem.at[3])
+    for load in (dn_load, total_load):
+        load.start()
+    for load in arriving:
+        load.start()
+    kv_load.start()
     enter_wide(dp, place)
     x, y, core = flip(dp, 2), flip(dp, 4), flip(dp, 1)
     far = flip(x, 4)
@@ -704,7 +735,7 @@
     sides = (gd_side, gg_side, gu_side, go_side, gq_side, nar_side)
     nears = (gd_near, gg_near, gu_near, go_near, gq_near, nar_near)
     lines = {3: go_line, 4: gq_line, 5: nar_line, 6: dkv_line}
-    arrivals = {3: go_in, 4: gq_in, 5: nar_in, 6: dkv_in, 7: layer_in}
+    arrivals = {3: go_in, 4: gq_in, 5: nar_in, 6: dkv_in}
     front, back = pl.ds(0, half), pl.ds(half, half)
     ranks = dkv_line.shape[0]
     turns = (3, 1, 2, 0)
@@ -741,10 +772,13 @@
         if i < 3:
             src = grads[i].at[rows_of(theirs[k]), :]
         else:
-            src = stage.at[turns.index(k) % 2, :, pl.ds(0, width_of(i))]
+            src = stage.at[turns.index(k), :, pl.ds(0, width_of(i))]
         return remote(
             src, cores[i].at[k], core_send.at[i, k], core_recv.at[i, k], (core, place)
         )
+
+    def leave(src, dst, number):
+        return pltpu.make_async_copy(src, dst, leave_sem.at[number])
 
     def own_load(i, k):
         return pltpu.make_async_copy(
@@ -770,30 +804,35 @@
         for k in turns:
             own_load(i, k).start()
 
+    def core_fetch(i, n):
+        src = cores[i].at[turns[n]]
+        return pltpu.make_async_copy(
+            src, early.at[n % 2, :, pl.ds(0, width_of(i))], early_sem.at[n % 2]
+        )
+
+    def core_begin(i, n):
+        core_copy(i, turns[n]).wait_recv()
+        core_fetch(i, n).start()
+
+    def ready_core(i):
+        core_begin(i, 0)
+        core_begin(i, 1)
+
     def stage_core(i):
-        def begin(n):
-            core_copy(i, turns[n]).wait_recv()
-            fetch(cores[i].at[turns[n]], n % 2).start()
-
-        begin(0)
-        begin(1)
         for n, k in enumerate(turns):
-            fetch(cores[i].at[k], n % 2).wait()
+            core_fetch(i, n).wait()
             if i < 3:
                 own_load(i, k).wait()
-            add_rows(part(i, k), held_part(n % 2, rows, width_of(i)))
+            add_rows(part(i, k), early.at[n % 2, :, pl.ds(0, width_of(i))])
             for lane in ((), (2,), (3,), (0, 1))[k]:
                 plane_copy(i, lane).start()
             if n + 2 < 4:
-                begin(n + 2)
+                core_begin(i, n + 2)
 
     def stage_side(i):
-        for side in range(2):
+        for side, (k, window, lane) in enumerate(((1, front, 4), (2, back, 5))):
             plane_copy(i, side).wait_recv()
-            fetch(sides[i].at[side], side).start()
-        for side, (k, window, lane) in enumerate(((1, front, 4), (2, back, 5))):
-            fetch(sides[i].at[side], side).wait()
-            add_rows(half_part(i, k, window), held_part(side, half, width_of(i)))
+            add_rows(half_part(i, k, window), sides[i].at[side])
             plane_copy(i, lane).start()
 
     def stage_near(i):
@@ -804,6 +843,8 @@
         for side in range(2):
             fetch(nears[i].at[side], side).wait()
         own, width, out = part(i, 0), width_of(i), outs[i]
+        if 0 < i < 3:
+            leave(units_made, out, i - 1).wait()
 
         @pl.loop(0, rows // 32)
         def _(index):
@@ -814,7 +855,7 @@
                 + held[1, window, pl.ds(0, width)].astype(jnp.float32)
             )
             if i < 3:
-                out[window, :] = sums
+                units_made[window, :] = sums
             elif i < 5:
                 piece = width // ranks
                 for rank in range(ranks):
@@ -827,11 +868,13 @@
                     sums.astype(low)
                 )
 
+        if i < 3:
+            leave(units_made, out, i).start()
+
     def line_copy(i, step):
         target = (place + step) % ranks
-        src = branch_ref.at[target] if i == 7 else lines[i].at[target]
         return remote(
-            src, arrivals[i].at[place], l_send.at[i - 3, step], l_recv.at[i - 3, step],
+            lines[i].at[target], arrivals[i].at[place], l_send.at[i - 3, step], l_recv.at[i - 3, step],
             (dp, target),
         )
 
@@ -855,8 +898,60 @@
         for step in range(1, ranks):
             line_copy(i, step).wait_send()
 
+    def chain_copy(rank, slot, step):
+        return remote(
+            chain.at[(step + 1) // 2], layer_in.at[slot], c_send.at[rank], c_recv.at[slot],
+            (dp, place + step),
+        )
+
+    def chain_load(rank, step):
+        copy = pltpu.make_async_copy(
+            branch_ref.at[rank], chain.at[(step + 1) // 2], in_sem.at[0]
+        )
+        copy.start()
+        copy.wait()
+
+    def chain_fetch(slot):
+        chain_copy(slot, slot, 1).wait_recv()
+        copy = fetch(layer_in.at[slot], 0)
+        copy.start()
+        copy.wait()
+
+    def chain_step(turn):
+        down, up = place - ranks + 1 + turn, place + ranks - 1 - turn
+
+        @pl.when(down >= 0)
+        def _():
+            @pl.when((down > 0) & (turn > 0))
+            def _():
+                chain_copy(down - 1, down - 1, -1).wait_send()
+
+            chain_load(down, -1)
+
+            @pl.when(place < ranks - 1)
+            def _():
+                chain_fetch(down)
+                add_rows(chain.at[0], held.at[0])
+
+            chain_copy(down, down, -1).start()
+
+        @pl.when(up < ranks)
+        def _():
+            @pl.when((up < ranks - 1) & (turn > 0))
+            def _():
+                chain_copy(up + 1, up + 1, 1).wait_send()
+
+            chain_load(up, 1)
+
+            @pl.when(place > 0)
+            def _():
+                chain_fetch(up)
+                add_rows(chain.at[1], held.at[0])
+
+            chain_copy(up, ranks if turn == ranks - 2 else up, 1).start()
+
     def line_out(i):
-        out = outs[i]
+        out = (go_made, gq_made, nar_made)[i - 3]
         count, width = out.shape
 
         def begin(window):
@@ -870,6 +965,7 @@
 
         over_rows(count, begin)
         line_last(i, add)
+        leave(out, outs[i], i).start()
 
     def norm_back(grad_ref, rows_ref, gain_ref, gain_row, act):
         gains[gain_row : gain_row + 1, :] = jnp.zeros((1, depth), jnp.float32)
@@ -894,7 +990,7 @@
         d_branch[window, :] = made.astype(low)
 
     def after_attn(window, d_values):
-        tokens_out[window, :] = (d_residual[window, :] + d_values).astype(low)
+        tokens_made[window, :] = (d_residual[window, :] + d_values).astype(low)
 
     def square_tile(left, right, owner):
         columns = pl.ds(pl.multiple_of(owner * rows, rows), rows)
@@ -911,13 +1007,11 @@
 
     def send_theirs(i, tile):
         for n, k in enumerate(turns):
-            if n >= 2:
-                core_copy(i, turns[n - 2]).wait_send()
-            stage[n % 2, :, pl.ds(0, width_of(i))] = tile(theirs[k])
+            stage[n, :, pl.ds(0, width_of(i))] = tile(theirs[k])
             core_copy(i, k).start()
 
     def theirs_sent(i):
-        for k in turns[2:]:
+        for k in turns:
             core_copy(i, k).wait_send()
 
     def keep_mine(i, tile):
@@ -939,7 +1033,6 @@
         )
 
     def make_d_heads():
-        weight_load(fo, 0).start()
         for index in range(steps):
             if index + 1 < steps:
                 weight_load(fo, index + 1).start()
@@ -953,7 +1046,6 @@
                 d_heads[...] = (wide[...] + made).astype(low)
 
     def make_d_normed():
-        weight_load(fq, 0).start()
         for index in range(steps):
             if index + 1 < steps:
                 weight_load(fq, index + 1).start()
@@ -1035,84 +1127,102 @@
             dkv_low[:, columns] = made.astype(low)
 
     def finish_layer():
-        own = parts.at[0, 0]
-        copy = pltpu.make_async_copy(branch_ref.at[place], own, in_sem.at[0])
-        copy.start()
-        copy.wait()
+        for step in (-1, 1):
+
+            @pl.when((place + step >= 0) & (place + step < ranks))
+            def _():
+                chain_copy(place + step, place, step).wait_send()
+
+        chain_load(place, -1)
 
         def begin(window):
-            total[window, :] += own[window, :].astype(jnp.float32)
-
-        def add(slot):
-            def act(window):
-                total[window, :] += held[slot, window, :].astype(jnp.float32)
-
-            over_rows(rows, act)
+            total[window, :] += chain[0, window, :].astype(jnp.float32)
+
+        def add(window):
+            total[window, :] += held[0, window, :].astype(jnp.float32)
 
         def end(window):
-            layer_out[window, :] = total[window, :].astype(low)
+            chain[1, window, :] = total[window, :].astype(low)
 
         over_rows(rows, begin)
-        line_last(7, add)
+
+        @pl.when(place < ranks - 1)
+        def _():
+            chain_fetch(place)
+            over_rows(rows, add)
+
+        @pl.when(place > 0)
+        def _():
+            chain_fetch(ranks)
+            over_rows(rows, add)
+
         over_rows(rows, end)
-
-    dn_load = pltpu.make_async_copy(dn_ref, wide, in_sem.at[1])
-    total_load = pltpu.make_async_copy(residual_ref, total, in_sem.at[2])
-    kv_load = pltpu.make_async_copy(fkv, kv_weight, in_sem.at[3])
+        leave(chain.at[1], layer_out, 6).start()
 
     def send_core(i):
         for k in turns:
             core_copy(i, k).start()
 
     send_core(0)
-    for load in (dn_load, total_load, kv_load):
-        load.start()
     load_own(0)
     load_own(1)
-    line_start(7)
+    chain_step(0)
     dn_load.wait()
     total_load.wait()
+    for load in arriving:
+        load.wait()
     send_core(1)
     norm_back(wide, total, gain_mlp_ref, 1, after_mlp)
+    ready_core(0)
+    weight_load(fo, 0).start()
     stage_core(0)
     send_theirs(3, go_tile)
+    ready_core(1)
+    make_d_heads()
     stage_core(1)
     send_core(2)
-    make_d_heads()
     stage_side(0)
+    chain_step(1)
     attend_back(0)
     stage_side(1)
     stage_near(0)
     plane_sent(0)
+    ready_core(3)
     keep_mine(3, go_tile)
     stage_core(3)
     attend_back(1)
     stage_near(1)
     plane_sent(1)
+    chain_step(2)
     attend_back(2)
     stage_side(3)
     attend_back(3)
     line_start(6)
     theirs_sent(3)
     send_theirs(4, gq_tile)
+    ready_core(4)
     keep_mine(4, gq_tile)
     stage_core(4)
     stage_near(3)
     line_start(3)
     plane_sent(3)
     load_own(2)
-    stage_core(2)
+    ready_core(2)
+    weight_load(fq, 0).start()
     make_d_normed()
     kv_load.wait()
     make_dkv()
     add_d_normed()
+    stage_core(2)
     stage_side(4)
     norm_back(wide, tokens_ref, gain_attn_ref, 0, after_attn)
+    leave(tokens_made, tokens_out, 7).start()
     theirs_sent(4)
     send_theirs(5, narrow_tile)
     stage_near(4)
     line_start(4)
     plane_sent(4)
+    ready_core(5)
     keep_mine(5, narrow_tile)
     stage_core(5)
     stage_side(2)
@@ -1120,17 +1230,26 @@
     stage_side(5)
     stage_near(5)
     line_start(5)
+    finish_layer()
     stage_near(2)
     plane_sent(2)
-    finish_layer()
     line_out(4)
     line_out(5)
+    for src, dst, number in (
+        (units_made, gu_out, 2),
+        (go_made, go_out, 3),
+        (gq_made, gq_out, 4),
+        (nar_made, nar_out, 5),
+        (chain.at[1], layer_out, 6),
+        (tokens_made, tokens_out, 7),
+    ):
+        leave(src, dst, number).wait()
     plane_sent(5)
     theirs_sent(5)
     for i in range(3):
         for k in turns:
             core_copy(i, k).wait_send()
-    for i in range(3, 8):
+    for i in range(3, 7):
         line_sent(i)
 
 
@@ -1153,14 +1272,16 @@
     out_shape += [jax.ShapeDtypeStruct((few, narrow), wide)]
     out_shape += [jax.ShapeDtypeStruct((rows, depth), low)] * 2
     out_shape += [jax.ShapeDtypeStruct((4, rows, w), low) for w in widths]
-    out_shape += [jax.ShapeDtypeStruct((2, half, w), low) for w in widths]
     out_shape += [jax.ShapeDtypeStruct((2, rows, w), low) for w in widths]
-    out_shape += [jax.ShapeDtypeStruct((ranks,) + shape, low) for shape in lined]
+    out_shape += [jax.ShapeDtypeStruct((ranks,) + shape, low) for shape in lined[:4]]
+    out_shape += [jax.ShapeDtypeStruct((ranks + 1, rows, depth), low)]
     dma = pltpu.SemaphoreType.DMA
-    scratch = [
+    scratch = [pltpu.VMEM((2, half, w), low) for w in widths]
+    scratch += [
         pltpu.VMEM((2, 4, rows, depth), low),
         pltpu.VMEM((2, rows, depth), low),
         pltpu.VMEM((2, rows, depth), low),
+        pltpu.VMEM((4, rows, depth), low),
     ]
     scratch += [pltpu.VMEM((ranks,) + shape, low) for shape in lined[:4]]
     scratch += [pltpu.VMEM((rows, keyval), wide)]
@@ -1178,14 +1299,24 @@
         pltpu.VMEM((length, PAIR), low),
         pltpu.VMEM((length, PAIR), wide),
         pltpu.VMEM((length, PAIR), wide),
+        pltpu.VMEM((2, rows, depth), low),
+        pltpu.VMEM((rows, units), wide),
+        pltpu.VMEM((rows, square), wide),
+        pltpu.VMEM((rows, square), wide),
+        pltpu.VMEM((few, narrow), wide),
+        pltpu.VMEM((rows, depth), low),
+    ]
+    scratch += [pltpu.VMEM(array.shape, array.dtype) for array in others]
+    scratch += [
         dma((3, 4)), dma((2,)), dma((6, 4)), dma((6, 4)), dma((6, 6)), dma((6, 6)),
-        dma((5, ranks)), dma((5, ranks)), dma((4,)), dma((2,)),
+        dma((5, ranks)), dma((5, ranks)), dma((4,)), dma((2,)), dma((ranks,)), dma((ranks + 1,)),
+        dma((2,)), dma((8,)), dma((12,)),
     ]
     results = pl.pallas_call(
         reach_back_kernel,
         out_shape=out_shape,
-        in_specs=[anywhere] * 9 + [in_vmem] * 12,
-        out_specs=[in_vmem] * 8 + [anywhere] * 23,
+        in_specs=[anywhere] * 21,
+        out_specs=[anywhere] * len(out_shape),
         scratch_shapes=scratch,
         compiler_params=pltpu.CompilerParams(
             collective_id=1, has_side_effects=True, vmem_limit_bytes=63 * 1024 * 1024
@@ -1317,20 +1448,29 @@
     def branch_copy(rank):
         return pltpu.make_async_copy(branch_stage, branch_out.at[rank], stage_sem.at[0])
 
-    def compute(rank):
+    def forward(rank):
         here = chunk(rank)
 
         def activate(columns):
             gate = dot_nn(normed[here, :], wg[:, columns])
             up = dot_nn(normed[here, :], wu[:, columns])
-            d_hidden = dot_nn(cot[here, :], wd[:, columns])
             sig = 1.0 / (1.0 + jnp.exp(-gate))
             silu = gate * sig
             hid[here, columns] = (silu * up).astype(low)
-            dg[here, columns] = (d_hidden * up * sig * (1.0 + gate * (1.0 - sig))).astype(low)
-            du[here, columns] = (d_hidden * silu).astype(low)
+            dg[here, columns] = (up * sig * (1.0 + gate * (1.0 - sig))).astype(low)
+            du[here, columns] = silu.astype(low)
 
         by_tiles(wg.shape[1], 256, activate)
+
+    def backward(rank):
+        here = chunk(rank)
+
+        def meet(columns):
+            d_hidden = dot_nn(cot[here, :], wd[:, columns])
+            dg[here, columns] = (d_hidden * dg[here, columns].astype(jnp.float32)).astype(low)
+            du[here, columns] = (d_hidden * du[here, columns].astype(jnp.float32)).astype(low)
+
+        by_tiles(wg.shape[1], 256, meet)
 
         def pull(columns):
             part[rank, :, columns] = (
@@ -1358,6 +1498,9 @@
             pass_copy(rank, -1).start()
 
     inside = (place == 1) | (place == 2)
+    for load in loads:
+        load.wait()
+    forward(place)
     plane_second(0)
     take(order[0])
 
@@ -1366,8 +1509,11 @@
         take(order[1])
 
     plane_third(0)
-    for load in loads:
-        load.wait()
+
+    @pl.loop(0, jnp.where(inside, 2, 1))
+    def _(index):
+        forward(jnp.where(index == 0, order[0], order[1]))
+
     plane_ready(0)
 
     @pl.loop(0, 4)
@@ -1375,22 +1521,23 @@
         rank = jnp.where(
             turn == 0,
             order[0],
-            jnp.where(turn == 1, place, jnp.where(turn == 2, order[1], order[2])),
-        )
-
-        @pl.when((turn == 1) & inside)
-        def _():
-            take(order[2])
-
-        @pl.when((turn == 2) & jnp.logical_not(inside))
-        def _():
-            take(order[1])
-
-        @pl.when((turn == 3) & jnp.logical_not(inside))
-        def _():
-            take(order[2])
-
-        compute(rank)
+            jnp.where(
+                turn == 1,
+                jnp.where(inside, order[1], place),
+                jnp.where(
+                    turn == 2,
+                    jnp.where(inside, order[2], order[1]),
+                    jnp.where(inside, place, order[2]),
+                ),
+            ),
+        )
+
+        @pl.when((turn == 2) | ((turn == 3) & jnp.logical_not(inside)))
+        def _():
+            take(rank)
+            forward(rank)
+
+        backward(rank)
 
         @pl.when((turn != 1) & (place == 3))
         def _():
@@ -1475,16 +1622,13 @@
         def _(index):
             down_tile(cut * (tiles // cuts) + index)
 
+        @pl.when(cut > 0)
+        def _():
+            branch_copy(cut).wait()
+
+        branch(cut)
+
     down_copy(last).wait()
-
-    @pl.loop(0, 4)
-    def _(rank):
-        @pl.when(rank > 0)
-        def _():
-            branch_copy(rank).wait()
-
-        branch(rank)
-
     branch_copy(0).wait()
 
     for cut in range(cuts):

time: 513 us -> 496 us (0.967)
  Pallas kernels: 485 us -> 468 us
    pallas_call x1, Pallas kernels: 191 us -> 179 us  [reach_back(): pl.pallas_call(reach_back_kernel, out_shape=out_shape, in_specs=[anywhere...]
where the time goes in v6:
time: 496 us; the launch traced here: 489 us
  Pallas kernels  468 us (94%)
  local copies, waits for them, and re-layouts  14.7 us (3%)
  other arithmetic  5.59 us (1%)
    pallas_call x1, Pallas kernels, reach_back(): pl.pallas_call(reach_back_kernel, out_shape=out_shape, in_specs=[anywhere...  179 us
    pallas_call x1, Pallas kernels, attend_all(): pl.pallas_call(attend_kernel, out_shape=shapes, in_specs=[in_vmem] * 6 +...  149 us
    pallas_call x1, Pallas kernels, feed_forward(): pl.pallas_call(feed_forward_kernel, out_shape=[jax.ShapeDtypeStruct((dept...  140 us

profile of v6, /device:TPU:0, one launch (start us, length us, event | category | flops | bytes accessed | tf_op | source)
XLA Modules:
  0.0 489.3 jit_solution(509922148583499517)
XLA Ops:
  0.6 0.0 copy-start
  0.7 0.0 copy-start.7
  0.7 0.0 copy-start.8
  0.7 0.9 slice_compare_fusion
  1.6 0.8 dynamic_slice.7
  2.3 1.5 fusion
  3.8 0.1 add_select_fusion
  3.9 0.3 reduce-window.9
  4.2 0.1 slice.27
  4.3 0.1 slice_reduce_fusion.2
  4.4 0.1 bitcast_subtract_fusion
  4.5 0.1 dynamic-slice_convert_fusion
  4.6 0.2 fusion.5
  4.8 0.8 copy.22.sin_ref.sin_in
  5.6 0.8 copy.21.cos_ref.cos_in
  6.3 0.0 copy-done.7
  6.3 1.2 fusion.4.bias_ref.bias_in
  7.5 0.0 copy-done
  7.5 0.0 copy-done.8
  7.5 1.3 fusion.2.normed_ref.normed_in
  8.8 148.7 %attend_all.1 = (bf16[256,2048]{1,0:T(8,128)(2,1)}, bf16[1024,512]{1,0:T(8,128)(2,1)}, bf16[256,2048]{1,0:T(8,128)(2,1)}, f32[16,2,256]{2,1,0:T(2,128)}, f32[256...) custom-call(bf16[256,2048]{1,0:T(8,128)(2,1)} %tokens_in.1, ...), custom_call_target="tpu_custom_call" | custom-call | tf_op jit(solution)/shard_map/attend_all/pallas_call | solution.py:629
  157.6 140.1 %feed_forward.1 = (bf16[2048,1408]{1,0:T(8,128)(2,1)}, bf16[2048,1408]{1,0:T(8,128)(2,1)}, bf16[2048,1408]{1,0:T(8,128)(2,1)}, bf16[4,256,2048]{2,1,0:T(8,128)(2,1)}, f32[256,2048]{1,0:T(8,128)}) custom-call(bf16[256,2048]{1,0:T(8,128)(2,1)} %get-tuple-element.35.normed_ref, bf16[2048,1408]{1,0:T(8,128)(2,1)} %get-tuple-element.36.gate_w_ref, ...), custom_call_target="tpu_custom_call" | custom-call | flops 53150220288 | bytes 62914560 | tf_op jit(solution)/shard_map/feed_forward/pallas_call | solution.py:1686
  297.7 179.3 %reach_back.1 = (f32[256,1408]{1,0:T(8,128)}, f32[256,1408]{1,0:T(8,128)}, f32[256,1408]{1,0:T(8,128)}, f32[256,512]{1,0:T(8,128)}, f32[256,512]{1,0:T(8,128)}, ...) custom-call(bf16[2048,1408]{1,0:T(8,128)(2,1)} %get-tuple-element.39, ...), custom_call_target="tpu_custom_call" | custom-call | tf_op jit(solution)/shard_map/reach_back/pallas_call | solution.py:1315
  477.0 0.0 copy-start.4
  477.0 1.6 slice_reduce_fusion
  478.5 1.6 slice.31
  480.1 0.0 copy-start.6
  480.1 2.4 copy.32
  482.5 0.0 copy-done.4
  482.5 0.0 copy-start.5
  482.5 0.0 copy-start.3
  482.5 1.0 copy.33
  483.4 0.0 copy-done.6
  483.4 0.8 copy.34
  484.2 0.0 copy-done.5
  484.2 0.0 copy-start.2
  484.2 0.8 copy.35
  485.0 0.0 copy-done.3
  485.0 1.1 copy.36
  486.1 0.0 copy-done.2
  486.1 0.0 copy-start.1
  486.1 1.1 copy.37
  487.2 0.8 copy-done.1
  488.0 1.1 copy.38
  (8 shorter events, 0.1 us)
Async XLA Ops:
  0.6 6.9 %copy-start = (bf16[256,2048]{1,0:T(8,128)(2,1)S(1)}, bf16[256,2048]{1,0:T(8,128)(2,1)}, u32[]{:S(2)}) copy-start(bf16[256,2048]{1,0:T(8,128)(2,1)} %tokens_in.1) | copy-start | bytes 3145732
  0.7 5.7 %copy-start.7 = (s32[1024]{0:T(1024)S(1)}, s32[1024]{0:T(1024)}, u32[]{:S(2)}) copy-start(s32[1024]{0:T(1024)} %param.12) | copy-start | bytes 12292
  0.7 6.9 %copy-start.8 = (f32[2048]{0:T(1024)S(1)}, f32[2048]{0:T(1024)}, u32[]{:S(2)}) copy-start(f32[2048]{0:T(1024)} %param.13) | copy-start | bytes 24580
  477.0 5.5 %copy-start.4 = (bf16[256,2048]{1,0:T(8,128)(2,1)S(1)}, bf16[256,2048]{1,0:T(8,128)(2,1)}, u32[]{:S(2)}) copy-start(bf16[256,2048]{1,0:T(8,128)(2,1)} %get-tuple-element.76) | copy-start | bytes 3145732
  480.1 3.3 copy-start.6
  482.5 1.8 copy-start.5
  482.5 2.6 copy-start.3
  484.2 1.9 copy-start.2
  486.1 1.9 copy-start.1

commit v7 on v6

--- a/solution.py
+++ b/solution.py
@@ -261,18 +261,48 @@
 
 
 def attend_kernel(
-    tokens_ref, normed_ref, cos_ref, sin_ref, bias_ref, gain_ref,
+    tokens_in, gain_attn_in, cos_in, sin_in, bias_in, gain_in,
     kv_ref, q_ref, o_ref, g_ref, u_ref, c_ref,
-    query_out, keyval_out, heads_out, log_out, residual_out, mlp_out,
+    normed_to, query_to, keyval_out, heads_to, log_to, residual_to, mlp_to,
     fkv, fq, fo, fg, fu, fc,
+    tokens_ref, gain_attn_ref, cos_ref, sin_ref, bias_ref, gain_ref,
+    normed_ref, query_out, heads_out, log_out, residual_out, mlp_out,
     kv_weight, weight, wide_weight, keyval, key_f, key_b, value_t,
-    own_sem, z_send, z_recv, p_send, p_recv, k_send, k_recv, w_sem,
+    own_sem, z_send, z_recv, p_send, p_recv, k_send, k_recv, w_sem, enter_sem, leave_sem,
 ):
     dp, place = lax.axis_index("dp"), lax.axis_index("tensor")
     rows = kv_ref.shape[0]
     half = rows // 2
     width = q_ref.shape[1]
     order = line_order(place)
+    arriving = [
+        pltpu.make_async_copy(src, dst, enter_sem.at[number])
+        for number, (src, dst) in enumerate(
+            (
+                (tokens_in, tokens_ref),
+                (gain_attn_in, gain_attn_ref),
+                (cos_in, cos_ref),
+                (sin_in, sin_ref),
+                (bias_in, bias_ref),
+                (gain_in, gain_ref),
+            )
+        )
+    ]
+    leaving = [
+        pltpu.make_async_copy(src, dst, leave_sem.at[number])
+        for number, (src, dst) in enumerate(
+            (
+                (normed_ref, normed_to),
+                (query_out, query_to),
+                (heads_out, heads_to),
+                (log_out, log_to),
+                (residual_out, residual_to),
+                (mlp_out, mlp_to),
+            )
+        )
+    ]
+    for copy in arriving:
+        copy.start()
     enter(dp, place)
 
     def rows_of(owner):
@@ -416,6 +446,19 @@
 
     low = jnp.bfloat16
     wide = KVH * HD
+
+    def make_normed():
+        for copy in arriving:
+            copy.wait()
+
+        @pl.loop(0, rows // 64)
+        def _(index):
+            window = pl.ds(pl.multiple_of(index * 64, 64), 64)
+            values = tokens_ref[window, :].astype(jnp.float32)
+            inverse = lax.rsqrt(jnp.mean(values * values, axis=1, keepdims=True) + epsilon)
+            normed_ref[window, :] = (values * inverse * gain_attn_ref[...]).astype(low)
+
+        leaving[0].start()
 
     def make_keyval():
         load = pltpu.make_async_copy(fkv, kv_weight, w_sem.at[0])
@@ -508,6 +551,7 @@
     plane_first(kv)
     line_send(0, place, start)
     plane_first(q_own)
+    make_normed()
     line_take(0, 0)
     line_send(1, place, start)
     plane_second(kv)
@@ -546,6 +590,7 @@
         plane_ready(index)
     own_copies[1].wait()
     make_query()
+    leaving[1].start()
     cot_take(order[0])
 
     @pl.when(inside)
@@ -566,11 +611,15 @@
     plane_third(o_far[2])
     cot_take(jnp.where(inside, order[2], order[1]))
     attend(3)
+    leaving[2].start()
+    leaving[3].start()
     plane_second(up)
     for index in (o_own,) + o_far:
         plane_ready(index)
     own_copies[2].wait()
     make_residual()
+    leaving[4].start()
+    leaving[5].start()
     plane_third(up)
 
     @pl.when(jnp.logical_not(inside))
@@ -592,11 +641,13 @@
         copy.wait()
     out_copy = pltpu.make_async_copy(keyval, keyval_out, w_sem.at[0])
     out_copy.start()
+    for copy in leaving:
+        copy.wait()
     out_copy.wait()
 
 
 def attend_all(
-    tokens, normed, cos, sin, bias, gain, w_keyval, w_query, w_output, w_gate, w_up, cotangent
+    tokens, gain_attn, cos, sin, bias, gain, w_keyval, w_query, w_output, w_gate, w_up, cotangent
 ):
     n_dp, n_line = lax.axis_size("dp"), lax.axis_size("tensor")
     low = jnp.bfloat16
@@ -610,8 +661,8 @@
         return jax.ShapeDtypeStruct(shape, array.dtype)
 
     anywhere = pl.BlockSpec(memory_space=pl.ANY)
-    in_vmem = pl.BlockSpec(memory_space=pltpu.VMEM)
     shapes = [
+        jax.ShapeDtypeStruct((rows, depth), low),
         jax.ShapeDtypeStruct((rows, heads * HD), low),
         jax.ShapeDtypeStruct((length, wide), low),
         jax.ShapeDtypeStruct((rows, heads * HD), low),
@@ -629,9 +680,16 @@
     return pl.pallas_call(
         attend_kernel,
         out_shape=shapes,
-        in_specs=[in_vmem] * 6 + [anywhere] * 6,
-        out_specs=[in_vmem, anywhere] + [in_vmem] * 4 + [anywhere] * 6,
+        in_specs=[anywhere] * 12,
+        out_specs=[anywhere] * len(shapes),
         scratch_shapes=[
+            pltpu.VMEM(array.shape, array.dtype) for array in (tokens, gain_attn, cos, sin, bias, gain)
+        ]
+        + [
+            pltpu.VMEM(shapes[number].shape, shapes[number].dtype)
+            for number in (0, 1, 3, 4, 5, 6)
+        ]
+        + [
             pltpu.VMEM((depth, wide), low),
             pltpu.VMEM((2, depth, w_query.shape[1]), low),
             pltpu.VMEM((2, w_query.shape[1], depth), low),
@@ -640,14 +698,14 @@
             pltpu.VMEM((length, PAIR), low),
             pltpu.VMEM((HD, length), low),
             dma((6,)), dma((3, 2, 4)), dma((3, 4)), dma((11, 8)), dma((11, 8)),
-            dma((2, 4)), dma((4,)), dma((2,)),
+            dma((2, 4)), dma((4,)), dma((2,)), dma((6,)), dma((6,)),
         ],
         compiler_params=pltpu.CompilerParams(
             collective_id=0, has_side_effects=True, vmem_limit_bytes=62 * 1024 * 1024
         ),
         name="attend_all",
     )(
-        tokens, normed, cos, sin, bias, gain, w_keyval, w_query, w_output, w_gate, w_up, cotangent
+        tokens, gain_attn, cos, sin, bias, gain, w_keyval, w_query, w_output, w_gate, w_up, cotangent
     )
 
 
@@ -679,15 +737,15 @@
     gd_ref, gg_ref, gu_ref, branch_ref, fkv, fq, fo, dn_ref, residual_ref,
     cot_in, tokens_in, normed_in, query_in, heads_in, keyval_in, log_in, bias_in,
     cos_in, sin_in, gain_attn_in, gain_mlp_in,
-    gd_out, gg_out, gu_out, go_out, gq_out, nar_out, layer_out, tokens_out,
+    gd_out, gg_out, gu_out, go_out, gq_out, nar_out, layer_out, tokens_out, gains_out,
     gd_core, gg_core, gu_core, go_core, gq_core, nar_core,
     gd_near, gg_near, gu_near, go_near, gq_near, nar_near,
     go_in, gq_in, nar_in, dkv_in, layer_in,
     gd_side, gg_side, gu_side, go_side, gq_side, nar_side,
-    parts, held, early, stage, go_line, gq_line, nar_line, dkv_line, sums,
+    parts, nar_part, held, early, stage, go_line, gq_line, nar_line, dkv_line, sums,
     d_residual, total, wide, d_branch, d_heads, dq_low, dkv_low, gains, weight, kv_weight,
     key_f, key_b, key_t, value_f, value_b, dk, dv,
-    chain, units_made, go_made, gq_made, nar_made, tokens_made,
+    chain, units_made, go_made, gq_made, nar_made, gains_made,
     cot_ref, tokens_ref, normed_ref, query_ref, heads_ref, keyval_ref, log_ref, bias_ref,
     cos_ref, sin_ref, gain_attn_ref, gain_mlp_ref,
     load_sem, fetch_sem, core_send, core_recv, p_send, p_recv, l_send, l_recv, in_sem, w_sem,
@@ -738,6 +796,7 @@
     arrivals = {3: go_in, 4: gq_in, 5: nar_in, 6: dkv_in}
     front, back = pl.ds(0, half), pl.ds(half, half)
     ranks = dkv_line.shape[0]
+    narrow_width = nar_out.shape[1]
     turns = (3, 1, 2, 0)
 
     def rows_of(owner):
@@ -755,9 +814,13 @@
     sets = (0, 1, 0, 0, 1, 1)
 
     def part(i, k):
+        if i == 5:
+            return nar_part.at[k]
         return parts.at[sets[i], k, :, pl.ds(0, width_of(i))]
 
     def half_part(i, k, window):
+        if i == 5:
+            return nar_part.at[k, window, :]
         return parts.at[sets[i], k, window, pl.ds(0, width_of(i))]
 
     def held_part(slot, count, width):
@@ -965,7 +1028,12 @@
 
         over_rows(count, begin)
         line_last(i, add)
-        leave(out, outs[i], i).start()
+        if i == 5:
+            gains_made[...] = out[:, narrow_width:].T
+            leave(gains_made, gains_out, 8).start()
+            leave(out.at[:, pl.ds(0, narrow_width)], nar_out, 5).start()
+        else:
+            leave(out, outs[i], i).start()
 
     def norm_back(grad_ref, rows_ref, gain_ref, gain_row, act):
         gains[gain_row : gain_row + 1, :] = jnp.zeros((1, depth), jnp.float32)
@@ -990,7 +1058,7 @@
         d_branch[window, :] = made.astype(low)
 
     def after_attn(window, d_values):
-        tokens_made[window, :] = (d_residual[window, :] + d_values).astype(low)
+        d_residual[window, :] += d_values
 
     def square_tile(left, right, owner):
         columns = pl.ds(pl.multiple_of(owner * rows, rows), rows)
@@ -1016,7 +1084,7 @@
 
     def keep_mine(i, tile):
         for k in turns:
-            parts[sets[i], k, :, pl.ds(0, width_of(i))] = tile(mine[k])
+            part(i, k)[...] = tile(mine[k])
 
     def go_tile(owner):
         return square_tile(d_branch, heads_ref, owner)
@@ -1141,9 +1209,6 @@
         def add(window):
             total[window, :] += held[0, window, :].astype(jnp.float32)
 
-        def end(window):
-            chain[1, window, :] = total[window, :].astype(low)
-
         over_rows(rows, begin)
 
         @pl.when(place < ranks - 1)
@@ -1156,8 +1221,7 @@
             chain_fetch(ranks)
             over_rows(rows, add)
 
-        over_rows(rows, end)
-        leave(chain.at[1], layer_out, 6).start()
+        leave(total, layer_out, 6).start()
 
     def send_core(i):
         for k in turns:
@@ -1216,32 +1280,33 @@
     stage_core(2)
     stage_side(4)
     norm_back(wide, tokens_ref, gain_attn_ref, 0, after_attn)
-    leave(tokens_made, tokens_out, 7).start()
+    leave(d_residual, tokens_out, 7).start()
     theirs_sent(4)
     send_theirs(5, narrow_tile)
-    stage_near(4)
-    line_start(4)
-    plane_sent(4)
     ready_core(5)
     keep_mine(5, narrow_tile)
     stage_core(5)
+    stage_near(4)
+    line_start(4)
+    stage_side(5)
     stage_side(2)
     line_out(3)
-    stage_side(5)
     stage_near(5)
     line_start(5)
     finish_layer()
     stage_near(2)
-    plane_sent(2)
     line_out(4)
     line_out(5)
+    plane_sent(2)
+    plane_sent(4)
     for src, dst, number in (
         (units_made, gu_out, 2),
         (go_made, go_out, 3),
         (gq_made, gq_out, 4),
-        (nar_made, nar_out, 5),
-        (chain.at[1], layer_out, 6),
-        (tokens_made, tokens_out, 7),
+        (nar_made.at[:, pl.ds(0, narrow_width)], nar_out, 5),
+        (gains_made, gains_out, 8),
+        (total, layer_out, 6),
+        (d_residual, tokens_out, 7),
     ):
         leave(src, dst, number).wait()
     plane_sent(5)
@@ -1269,8 +1334,9 @@
     lined = [(rows, square), (rows, square), (few, narrow), (rows, keyval), (rows, depth)]
     out_shape = [jax.ShapeDtypeStruct((rows, units), wide)] * 3
     out_shape += [jax.ShapeDtypeStruct((rows, square), wide)] * 2
-    out_shape += [jax.ShapeDtypeStruct((few, narrow), wide)]
-    out_shape += [jax.ShapeDtypeStruct((rows, depth), low)] * 2
+    out_shape += [jax.ShapeDtypeStruct((few, keyval), wide)]
+    out_shape += [jax.ShapeDtypeStruct((rows, depth), wide)] * 2
+    out_shape += [jax.ShapeDtypeStruct((PAIR, few), wide)]
     out_shape += [jax.ShapeDtypeStruct((4, rows, w), low) for w in widths]
     out_shape += [jax.ShapeDtypeStruct((2, rows, w), low) for w in widths]
     out_shape += [jax.ShapeDtypeStruct((ranks,) + shape, low) for shape in lined[:4]]
@@ -1279,6 +1345,7 @@
     scratch = [pltpu.VMEM((2, half, w), low) for w in widths]
     scratch += [
         pltpu.VMEM((2, 4, rows, depth), low),
+        pltpu.VMEM((4, rows, narrow), low),
         pltpu.VMEM((2, rows, depth), low),
         pltpu.VMEM((2, rows, depth), low),
         pltpu.VMEM((4, rows, depth), low),
@@ -1304,13 +1371,13 @@
         pltpu.VMEM((rows, square), wide),
         pltpu.VMEM((rows, square), wide),
         pltpu.VMEM((few, narrow), wide),
-        pltpu.VMEM((rows, depth), low),
+        pltpu.VMEM((PAIR, few), wide),
     ]
     scratch += [pltpu.VMEM(array.shape, array.dtype) for array in others]
     scratch += [
         dma((3, 4)), dma((2,)), dma((6, 4)), dma((6, 4)), dma((6, 6)), dma((6, 6)),
         dma((5, ranks)), dma((5, ranks)), dma((4,)), dma((2,)), dma((ranks,)), dma((ranks + 1,)),
-        dma((2,)), dma((8,)), dma((12,)),
+        dma((2,)), dma((9,)), dma((12,)),
     ]
     results = pl.pallas_call(
         reach_back_kernel,
@@ -1323,7 +1390,7 @@
         ),
         name="reach_back",
     )(*grads, branch, *full, d_normed, residual, *others)
-    return results[:8]
+    return results[:9]
 
 
 def by_tiles(total, size, act):
@@ -1753,13 +1820,18 @@
     normed_attn = normed_attn.astype(low)
     wide = KVH * HD
     if by_kernels:
-        cos_tile = jnp.tile(cosine, (1, 4))
-        sin_tile = jnp.tile(jnp.concatenate([-sine_table, sine_table], axis=1), (1, 2))
+        before = jnp.sum(segments[None, :] < my_segments[:, None], axis=1, dtype=jnp.int32)
+        my_order = tensor_rank * rows + jnp.arange(rows, dtype=jnp.int32)
+        lane = jnp.arange(PAIR, dtype=jnp.int32)
+        spin = rope_base ** (-(2.0 * (lane % (HD // 2)).astype(jnp.float32)) / HD)
+        angles = (my_order - before).astype(jnp.float32)[:, None] * spin[None, :]
+        cos_tile = jnp.cos(angles)
+        sin_tile = jnp.where((lane % HD < HD // 2)[None, :], -jnp.sin(angles), jnp.sin(angles))
         (
-            query, keyval, heads_low, log_sum, residual, normed_mlp,
+            normed_attn, query, keyval, heads_low, log_sum, residual, normed_mlp,
             full_keyval, full_query, full_output, full_gate, full_up, piece,
         ) = attend_all(
-            tokens, normed_attn, cos_tile, sin_tile, bias, gain_mlp[None, :],
+            tokens, gain_attn[None, :], cos_tile, sin_tile, bias, gain_mlp[None, :],
             w_keyval, w_query, w_output, w_gate, w_up, cotangent,
         )
     else:
@@ -1775,7 +1847,7 @@
         grad_gate, grad_up, grad_down, branch, d_normed_mlp = feed_forward(
             normed_mlp, full_gate, full_up, w_down, piece
         )
-        to_down, to_gate, to_up, to_output, to_query, to_narrow, layer_out, grad_tokens = (
+        to_down, to_gate, to_up, to_output, to_query, to_keyval, layer_out, grad_tokens, to_gains = (
             reach_back(
                 (grad_down, grad_gate, grad_up),
                 branch,
@@ -1788,15 +1860,14 @@
                 ),
             )
         )
-        wide = 2 * KVH * HD
         return (
-            layer_out,
-            grad_tokens,
-            to_narrow[:, wide],
+            layer_out.astype(low),
+            grad_tokens.astype(low),
+            to_gains[0],
             to_query,
-            to_narrow[:, :wide],
+            to_keyval,
             to_output,
-            to_narrow[:, wide + 1],
+            to_gains[1],
             to_gate,
             to_up,
             to_down,

time: 496 us -> 488 us (0.984)
  Pallas kernels: 468 us -> 461 us
  local copies, waits for them, and re-layouts: 14.7 us -> 8.38 us
where the time goes in v7:
time: 488 us; the launch traced here: 479 us
  Pallas kernels  461 us (94%)
  local copies, waits for them, and re-layouts  8.38 us (2%)
  other arithmetic  8.06 us (2%)
    pallas_call x1, Pallas kernels, reach_back(): pl.pallas_call(reach_back_kernel, out_shape=out_shape, in_specs=[anywhere...  176 us
    pallas_call x1, Pallas kernels, attend_all(): pl.pallas_call(attend_kernel, out_shape=shapes, in_specs=[anywhere] * 12,...  145 us
    pallas_call x1, Pallas kernels, feed_forward(): pl.pallas_call(feed_forward_kernel, out_shape=[jax.ShapeDtypeStruct((dept...  141 us

profile of v7, /device:TPU:0, one launch (start us, length us, event | category | flops | bytes accessed | tf_op | source)
XLA Modules:
  0.0 479.0 jit_solution(17525675703905492485)
XLA Ops:
  0.6 0.8 dynamic_slice.3
  1.4 0.9 convert_reduce_fusion
  2.4 1.2 negate_select_fusion
  3.6 1.9 fusion.1.bias_in
  5.5 144.6 %attend_all.1 = (bf16[256,2048]{1,0:T(8,128)(2,1)}, bf16[256,2048]{1,0:T(8,128)(2,1)}, bf16[1024,512]{1,0:T(8,128)(2,1)}, bf16[256,2048]{1,0:T(8,128)(2,1)}, f32...) custom-call(bf16[256,2048]{1,0:T(8,128)(2,1)} %tokens_in.3, ...), custom_call_target="tpu_custom_call" | custom-call | tf_op jit(solution)/shard_map/attend_all/pallas_call | solution.py:680
  150.1 140.5 %feed_forward.1 = (bf16[2048,1408]{1,0:T(8,128)(2,1)}, bf16[2048,1408]{1,0:T(8,128)(2,1)}, bf16[2048,1408]{1,0:T(8,128)(2,1)}, bf16[4,256,2048]{2,1,0:T(8,128)(2,1)}, f32[256,2048]{1,0:T(8,128)}) custom-call(bf16[256,2048]{1,0:T(8,128)(2,1)} %get-tuple-element.37.normed_ref, bf16[2048,1408]{1,0:T(8,128)(2,1)} %get-tuple-element.38.gate_w_ref, ...), custom_call_target="tpu_custom_call" | custom-call | flops 53150220288 | bytes 62914560 | tf_op jit(solution)/shard_map/feed_forward/pallas_call | solution.py:1753
  290.6 176.3 %reach_back.1 = (f32[256,1408]{1,0:T(8,128)}, f32[256,1408]{1,0:T(8,128)}, f32[256,1408]{1,0:T(8,128)}, f32[256,512]{1,0:T(8,128)}, f32[256,512]{1,0:T(8,128)}, ...) custom-call(bf16[2048,1408]{1,0:T(8,128)(2,1)} %get-tuple-element.41, ...), custom_call_target="tpu_custom_call" | custom-call | tf_op jit(solution)/shard_map/reach_back/pallas_call | solution.py:1382
  467.0 0.0 copy-start
  467.0 2.9 convert_element_type.26
  469.8 0.0 copy-start.5
  469.8 1.3 slice_bitcast_fusion
  471.1 0.0 copy-done
  471.1 0.0 copy-start.6
  471.1 0.0 copy-start.4
  471.1 0.0 copy-start.3
  471.1 1.1 convert_element_type.27
  472.2 0.0 copy-done.5
  472.2 0.8 copy.27
  473.0 0.0 copy-done.6
  473.0 0.0 copy-start.2
  473.0 0.7 copy.28
  473.7 0.0 copy-done.4
  473.7 0.8 copy.29
  474.5 0.0 copy-done.3
  474.5 1.1 copy.30
  475.6 0.0 copy-done.2
  475.6 0.0 copy-start.1
  475.6 1.1 copy.31
  476.7 0.8 copy-done.1
  477.5 1.1 copy.32
  (4 shorter events, 0.0 us)
Async XLA Ops:
  467.0 4.1 copy-start
  469.8 2.4 copy-start.5
  471.1 1.9 copy-start.6
  471.1 2.6 copy-start.4
  471.1 3.4 copy-start.3
  473.0 2.6 copy-start.2
  475.6 1.9 copy-start.1

commit v8 on v7

--- a/solution.py
+++ b/solution.py
@@ -363,14 +363,18 @@
     far = flip(x, 4)
 
     blocks = [("kv", None), ("q", place), ("g", None)] + [("q", rank) for rank in order]
-    blocks += [("o", place)] + [("o", rank) for rank in order] + [("u", None)]
+    blocks += [("o", place)] + [("o", rank) for rank in order] + [("u0", None), ("u1", None)]
 
     def block(index, owner, part=None):
         name, rank = blocks[index]
-        ref = {"kv": fkv, "q": fq, "o": fo, "g": fg, "u": fu}[name]
-        first = owner * rows if part is None else owner * rows + part * half
-        size = rows if part is None else half
-        window = pl.ds(pl.multiple_of(first, half), size)
+        ref = {"kv": fkv, "q": fq, "o": fo, "g": fg, "u0": fu, "u1": fu}[name]
+        span = half if name in ("u0", "u1") else rows
+        first = owner * rows + (span if name == "u1" else 0)
+        size = span
+        if part is not None:
+            size = span // 2
+            first = first + part * size
+        window = pl.ds(pl.multiple_of(first, span // 2), size)
         if rank is None:
             return ref.at[window, :]
         return ref.at[window, columns_of_rank(rank)]
@@ -378,7 +382,10 @@
     def own_block(index):
         name, rank = blocks[index]
         if rank is None or rank is place:
-            return {"kv": kv_ref, "q": q_ref, "o": o_ref, "g": g_ref, "u": u_ref}[name]
+            return {
+                "kv": kv_ref, "q": q_ref, "o": o_ref, "g": g_ref,
+                "u0": u_ref.at[pl.ds(0, half), :], "u1": u_ref.at[pl.ds(half, half), :],
+            }[name]
         return block(index, dp)
 
     def plane_copy(index, lane):
@@ -546,7 +553,7 @@
         line_send(which, order[step], start)
 
     count = len(blocks)
-    kv, q_own, gate, o_own, up = 0, 1, 2, 6, 10
+    kv, q_own, gate, o_own, up, up_back = 0, 1, 2, 6, 10, 11
     q_far, o_far = (3, 4, 5), (7, 8, 9)
     plane_first(kv)
     line_send(0, place, start)
@@ -603,6 +610,7 @@
     attend(0)
     plane_second(o_far[1])
     plane_first(up)
+    plane_first(up_back)
     plane_third(o_far[0])
     attend(1)
     plane_second(o_far[2])
@@ -614,6 +622,7 @@
     leaving[2].start()
     leaving[3].start()
     plane_second(up)
+    plane_second(up_back)
     for index in (o_own,) + o_far:
         plane_ready(index)
     own_copies[2].wait()
@@ -621,6 +630,7 @@
     leaving[4].start()
     leaving[5].start()
     plane_third(up)
+    plane_third(up_back)
 
     @pl.when(jnp.logical_not(inside))
     def _():
@@ -628,6 +638,7 @@
 
     plane_ready(gate)
     plane_ready(up)
+    plane_ready(up_back)
     for index in range(count):
         plane_sent(index)
     for which in range(3):
@@ -697,7 +708,7 @@
             pltpu.VMEM((length, PAIR), low),
             pltpu.VMEM((length, PAIR), low),
             pltpu.VMEM((HD, length), low),
-            dma((6,)), dma((3, 2, 4)), dma((3, 4)), dma((11, 8)), dma((11, 8)),
+            dma((6,)), dma((3, 2, 4)), dma((3, 4)), dma((12, 8)), dma((12, 8)),
             dma((2, 4)), dma((4,)), dma((2,)), dma((6,)), dma((6,)),
         ],
         compiler_params=pltpu.CompilerParams(
@@ -1439,15 +1450,15 @@
 
     x, y, core = flip(dp, 2), flip(dp, 4), flip(dp, 1)
     far = flip(x, 4)
-    shards = (down_w_ref,)
-    weights = (wd,)
     depth_rows = down_w_ref.shape[0]
-    half = depth_rows // 2
+    span = depth_rows // 2
+    half = span // 2
+    shards = (down_w_ref.at[pl.ds(0, span), :], down_w_ref.at[pl.ds(span, span), :])
 
     def weight_rows(i, owner, part=None):
-        first = owner * depth_rows if part is None else owner * depth_rows + part * half
-        count = depth_rows if part is None else half
-        return weights[i].at[pl.ds(pl.multiple_of(first, half), count), :]
+        first = owner * depth_rows + i * span + (0 if part is None else part * half)
+        count = span if part is None else half
+        return wd.at[pl.ds(pl.multiple_of(first, half), count), :]
 
     def plane_copy(i, lane):
         if lane < 2:
@@ -1472,7 +1483,7 @@
                 (gate_w_ref, wg),
                 (cot_ref, cot),
                 (up_w_ref, wu),
-                (down_w_ref, weight_rows(0, dp)),
+                (down_w_ref, wd.at[pl.ds(pl.multiple_of(dp * depth_rows, span), depth_rows), :]),
             )
         )
     ]
@@ -1485,8 +1496,9 @@
     def _():
         own_copy(-1).start()
 
-    for lane in (0, 1, 4):
-        plane_copy(0, lane).start()
+    for i in range(2):
+        for lane in (0, 1, 4):
+            plane_copy(i, lane).start()
     for load in loads:
         load.start()
 
@@ -1569,6 +1581,7 @@
         load.wait()
     forward(place)
     plane_second(0)
+    plane_second(1)
     take(order[0])
 
     @pl.when(inside)
@@ -1576,12 +1589,14 @@
         take(order[1])
 
     plane_third(0)
+    plane_third(1)
 
     @pl.loop(0, jnp.where(inside, 2, 1))
     def _(index):
         forward(jnp.where(index == 0, order[0], order[1]))
 
     plane_ready(0)
+    plane_ready(1)
 
     @pl.loop(0, 4)
     def _(turn):
@@ -1735,8 +1750,9 @@
             for cut in range(cuts):
                 sums_copy(rank, cut, rank, 1).wait_send()
 
-    for lane in range(8):
-        plane_copy(0, lane).wait_send()
+    for i in range(2):
+        for lane in range(8):
+            plane_copy(i, lane).wait_send()
 
 
 def feed_forward(normed, w_gate, w_up, w_down, cotangent):
@@ -1769,7 +1785,7 @@
             pltpu.VMEM((256, units), low),
             pltpu.VMEM((256, units), low),
             dma((5,)), dma((2, ranks)), dma((ranks,)), dma((ranks, cuts)), dma((ranks + 1, cuts)),
-            dma((3,)), dma((1, 8)), dma((1, 8)),
+            dma((3,)), dma((2, 8)), dma((2, 8)),
         ],
         compiler_params=pltpu.CompilerParams(
             collective_id=2, has_side_effects=True, vmem_limit_bytes=62 * 1024 * 1024

time: 488 us -> 487 us (level)
  no operation moved by 1% of the time
where the time goes in v8:
time: 487 us; the launch traced here: 478 us
  Pallas kernels  460 us (94%)
  local copies, waits for them, and re-layouts  8.38 us (2%)
  other arithmetic  8.06 us (2%)
    pallas_call x1, Pallas kernels, reach_back(): pl.pallas_call(reach_back_kernel, out_shape=out_shape, in_specs=[anywhere...  175 us
    pallas_call x1, Pallas kernels, attend_all(): pl.pallas_call(attend_kernel, out_shape=shapes, in_specs=[anywhere] * 12,...  145 us
    pallas_call x1, Pallas kernels, feed_forward(): pl.pallas_call(feed_forward_kernel, out_shape=[jax.ShapeDtypeStruct((dept...  140 us

profile of v8, /device:TPU:0, one launch (start us, length us, event | category | flops | bytes accessed | tf_op | source)
XLA Modules:
  0.0 477.6 jit_solution(14634667811123861459)
XLA Ops:
  0.6 0.8 dynamic_slice.3
  1.4 0.9 convert_reduce_fusion
  2.4 1.2 negate_select_fusion
  3.6 1.9 fusion.1.bias_in
  5.5 144.8 %attend_all.1 = (bf16[256,2048]{1,0:T(8,128)(2,1)}, bf16[256,2048]{1,0:T(8,128)(2,1)}, bf16[1024,512]{1,0:T(8,128)(2,1)}, bf16[256,2048]{1,0:T(8,128)(2,1)}, f32...) custom-call(bf16[256,2048]{1,0:T(8,128)(2,1)} %tokens_in.3, ...), custom_call_target="tpu_custom_call" | custom-call | tf_op jit(solution)/shard_map/attend_all/pallas_call | solution.py:691
  150.3 140.4 %feed_forward.1 = (bf16[2048,1408]{1,0:T(8,128)(2,1)}, bf16[2048,1408]{1,0:T(8,128)(2,1)}, bf16[2048,1408]{1,0:T(8,128)(2,1)}, bf16[4,256,2048]{2,1,0:T(8,128)(2,1)}, f32[256,2048]{1,0:T(8,128)}) custom-call(bf16[256,2048]{1,0:T(8,128)(2,1)} %get-tuple-element.37.normed_ref, bf16[2048,1408]{1,0:T(8,128)(2,1)} %get-tuple-element.38.gate_w_ref, ...), custom_call_target="tpu_custom_call" | custom-call | flops 53150220288 | bytes 62914560 | tf_op jit(solution)/shard_map/feed_forward/pallas_call | solution.py:1769
  290.7 175.1 %reach_back.1 = (f32[256,1408]{1,0:T(8,128)}, f32[256,1408]{1,0:T(8,128)}, f32[256,1408]{1,0:T(8,128)}, f32[256,512]{1,0:T(8,128)}, f32[256,512]{1,0:T(8,128)}, ...) custom-call(bf16[2048,1408]{1,0:T(8,128)(2,1)} %get-tuple-element.41, ...), custom_call_target="tpu_custom_call" | custom-call | tf_op jit(solution)/shard_map/reach_back/pallas_call | solution.py:1393
  465.8 0.0 copy-start
  465.8 2.9 convert_element_type.26
  468.7 0.0 copy-start.5
  468.7 1.3 slice_bitcast_fusion
  470.0 0.0 copy-done
  470.0 0.0 copy-start.6
  470.0 0.0 copy-start.4
  470.0 0.0 copy-start.3
  470.0 1.1 convert_element_type.27
  471.1 0.0 copy-done.5
  471.1 0.8 copy.27
  471.9 0.0 copy-done.6
  471.9 0.0 copy-start.2
  471.9 0.7 copy.28
  472.5 0.0 copy-done.4
  472.5 0.8 copy.29
  473.3 0.0 copy-done.3
  473.3 1.1 copy.30
  474.4 0.0 copy-done.2
  474.4 0.0 copy-start.1
  474.4 1.1 copy.31
  475.6 0.8 copy-done.1
  476.3 1.1 copy.32
  (4 shorter events, 0.0 us)
Async XLA Ops:
  465.8 4.1 copy-start
  468.7 2.4 copy-start.5
  470.0 1.9 copy-start.6
  470.0 2.6 copy-start.4
  470.0 3.4 copy-start.3
  471.9 2.6 copy-start.2
  474.4 1.9 copy-start.1
